TPU v7x, 32 devices: a whole 2x2x4 slice. The times are simulated.
32 devices in a mesh: lat: 4 (over z), lon: 8 (over y, x, core).
Axes of the slice: x: 2, y: 2, z: 4, core: 2. Of those that a mesh axis runs over, the one named last changes fastest.
Arguments:
- adjoint_in: float32 [2, 32, 32, 1024], P(None, None, 'lat', 'lon'), may hold values from -6 to 6
- lat_weights: float32 [2, 4, 32, 1024], P(None, None, 'lat', 'lon'), may hold values from -0.07 to 1, as said below
- lon_weights: float32 [2, 4, 32, 1024], P(None, None, 'lat', 'lon'), may hold values from -0.07 to 1, as said below
- depart_rows: int32 [2, 32, 8], P(None, 'lat', 'lon'), may hold values from 0 to 28, as said below
- depart_blocks: int32 [2, 32, 8], P(None, 'lat', 'lon'), may hold values from 0 to 7, as said below
- vertical_inverse: float32 [2, 32, 32, 32], P(None, 'lat'), may hold values from -0.36 to 1, as said below
Outputs:
- adjoint_out: float32 [2, 32, 32, 1024], P(None, None, 'lat', 'lon')
Inputs may be any that keep to these rules, and one draw needn't show every extreme that they name: `lat_weights`: interpolation weights of the nodes -1, 0, 1, 2 for a fraction of 0 to 1. `lon_weights`: interpolation weights of the nodes -1, 0, 1, 2 for a fraction of 0 to 1. depart_rows[s, i, b] lies between max(0, i - 3) and min(i + 1, 28). depart_blocks[s, i, b] equals (b + d) mod 8 for some d with |d| <= 2; d = 2 or -2 occurs in every draw. `vertical_inverse`: diagonal entries are 1; entries off the diagonal are independent, spread about 0.09, within -0.36 to 0.36.
All inputs are finite; a program needn't handle non-finite values.
Results may differ from a plain program's by a relative error of at most 0.0001.
Values sent between devices are 32-bit elements; how exact they have to be, the bound alone decides.
No kernel may reach another device: no remote copies, remote signals or barrier semaphores. Data moves between devices by JAX's collectives and lax.ppermute only.
A program may use at most 64 MiB of HBM per device.

v0:
```python
import jax
import jax.numpy as jnp
from jax import lax
from jax.sharding import PartitionSpec as P

R = 2
H = 2


def shifted(array, axis, by):
    size = lax.axis_size(axis)
    return lax.ppermute(array, axis, [(i, (i + by) % size) for i in range(size)])


def from_behind(value, axis, steps):
    count = lax.axis_size(axis)
    leading, last = (max(0, -steps), min(count, count - steps))
    return lax.ppermute(value, axis, [(source, source + steps) for source in range(leading, last)])


def spread_local(carried, lat_w, lon_w, row_table, block_table, lat_start, own_block, cycle_size):
    fields, levels, lat_rows, points = carried.shape
    low_rim = H + 1
    high_rim = H + 2
    ext_rows = lat_rows + low_rim + high_rim
    block_count = 2 * R + 3
    width = block_count * points
    rel_row = row_table - lat_start + low_rim
    rel_block = (block_table - own_block + R) % cycle_size
    target = lax.broadcasted_iota(jnp.int32, (ext_rows, 4, lat_rows), 0)
    node = lax.broadcasted_iota(jnp.int32, (ext_rows, 4, lat_rows), 1)
    row_onehot = (target == rel_row[None, None, :] + node).astype(jnp.float32)
    placed_all = []
    for m in range(4):
        lon_row = jnp.zeros((fields, levels, lat_rows, points + 3), jnp.float32)
        for o in range(4):
            term = carried * (lat_w[m] * lon_w[o])[None, None]
            lon_row = lon_row + jnp.pad(term, ((0, 0), (0, 0), (0, 0), (o, 3 - o)))
        placed = jnp.zeros((fields, levels, lat_rows, width), jnp.float32)
        for d in range(2 * R + 1):
            left = (d + 1) * points - 1
            right = width - left - (points + 3)
            selected = (rel_block == d).astype(jnp.float32)[None, None, :, None]
            placed = placed + selected * jnp.pad(lon_row, ((0, 0), (0, 0), (0, 0), (left, right)))
        placed_all.append(placed)
    stacked = jnp.stack(placed_all, axis=2)
    return jnp.einsum("emj,fkmjc->fkec", row_onehot, stacked, precision=lax.Precision.HIGHEST)


def cycle_total(buffer, points):
    block_count = 2 * R + 3
    pieces = [buffer[..., q * points : (q + 1) * points] for q in range(block_count)]
    summed = pieces[R + 1]
    for q in range(block_count):
        if q != R + 1:
            summed = summed + shifted(pieces[q], "lon", q - R - 1)
    return summed


def fold_rims(buffer, lat_rows):
    low_rim = H + 1
    high_rim = H + 2
    upper = buffer[:, :, :low_rim]
    lower = buffer[:, :, low_rim + lat_rows :]
    interior = buffer[:, :, low_rim : low_rim + lat_rows]
    from_after = from_behind(upper, "lat", -1)
    from_before = from_behind(lower, "lat", 1)
    interior = interior + jnp.pad(from_after, ((0, 0), (0, 0), (lat_rows - low_rim, 0), (0, 0)))
    interior = interior + jnp.pad(from_before, ((0, 0), (0, 0), (0, lat_rows - high_rim), (0, 0)))
    return interior


def body(adjoint_in, lat_weights, lon_weights, depart_rows, depart_blocks, vertical_inverse):
    fields, levels, lat_rows, points = adjoint_in.shape
    cycle_size = lax.axis_size("lon")
    own_block = lax.axis_index("lon")
    lat_start = lax.axis_index("lat") * lat_rows
    carried = adjoint_in
    for s in (1, 0):
        partial_value = spread_local(
            carried,
            lat_weights[s],
            lon_weights[s],
            depart_rows[s, :, 0],
            depart_blocks[s, :, 0],
            lat_start,
            own_block,
            cycle_size,
        )
        gathered_rows = cycle_total(partial_value, points)
        interior = fold_rims(gathered_rows, lat_rows)
        carried = jnp.einsum(
            "imk,fmip->fkip", vertical_inverse[s], interior, precision=lax.Precision.HIGHEST
        )
    return carried


def solution(mesh):
    return jax.shard_map(
        body,
        mesh=mesh,
        in_specs=(
            P(None, None, "lat", "lon"),
            P(None, None, "lat", "lon"),
            P(None, None, "lat", "lon"),
            P(None, "lat", "lon"),
            P(None, "lat", "lon"),
            P(None, "lat", None, None),
        ),
        out_specs=P(None, None, "lat", "lon"),
        check_vma=False,
    )
```

profile of v0, /device:TPU:8, one launch (start us, length us, event | category | flops | bytes accessed | tf_op | source)
XLA Modules:
  0.0 152.4 jit_solution(13734621438295129513)
XLA Ops:
  0.0 0.8 multiply_bitcast_fusion.28
  0.8 0.8 multiply_bitcast_fusion.30
  1.6 0.8 multiply_bitcast_fusion.31
  2.4 0.7 add_bitcast_fusion.8
  3.1 0.7 compare_convert_fusion.9
  3.8 1.4 broadcast_multiply_fusion.15
  5.2 0.9 pad_add_fusion.4
  6.1 2.9 %add_bitcast_fusion.5 = (f32[2,32,1,8,896]{4,3,2,1,0:T(8,128)S(1)}, f32[2,32,1,8,896]{4,3,2,1,0:T(8,128)S(1)}) fusion(f32[2,32,8,131]{3,2,1,0:T(8,128)S(1)} %get-tuple-element.106, f32[8]{0:T(128)S(1)} %get-tuple-element.109, f32[8]{0:T(128)S(1)} %get-tuple-element.111, f32[8]{0:T(128)S(1)} %get-tuple-element.110, f32[8]{0:T(128)S(1)} %get-tuple-element.112, ...), kind=kLoop, calls=%fused_computation.18 | loop fusion | flops 8257536 | bytes 4206752 | tf_op jit(solution)/shard_map/stack | solution.py:46
  9.0 0.9 pad_add_fusion.6
  9.9 2.9 %add_bitcast_fusion.7 = (f32[2,32,1,8,896]{4,3,2,1,0:T(8,128)S(1)}, f32[2,32,1,8,896]{4,3,2,1,0:T(8,128)S(1)}) fusion(f32[2,32,8,131]{3,2,1,0:T(8,128)S(1)} %get-tuple-element.108, f32[8]{0:T(128)S(1)} %get-tuple-element.109, f32[8]{0:T(128)S(1)} %get-tuple-element.111, f32[8]{0:T(128)S(1)} %get-tuple-element.110, f32[8]{0:T(128)S(1)} %get-tuple-element.112, ...), kind=kLoop, calls=%fused_computation.20 | loop fusion | flops 8257536 | bytes 4206752 | tf_op jit(solution)/shard_map/stack | solution.py:46
  12.8 2.8 %fusion.13 = f32[2,32,15,896]{3,2,1,0:T(8,128)S(1)} fusion(f32[2,32,1,8,896]{4,3,2,1,0:T(8,128)S(1)} %get-tuple-element.92, f32[2,32,1,8,896]{4,3,2,1,0:T(8,128)S(1)} %get-tuple-element.91, f32[2,32,1,8,896]{4,3,2,1,0:T(8,128)S(1)} %get-tuple-element.90, f32[2,32,1,8,896]{4,3,2,1,0:T(8,128)S(1)} %get-tuple-element.89, s32[8]{0:T(128)S(1)} %get-tuple-element.94), kind=kOutput, calls=%fused_computation.12 | convolution fusion | flops 335807424 | bytes 10780704 | tf_op jit(solution)/shard_map/emj,fkmjc->fkec/dot_general | solution.py:47
  15.6 0.3 fusion.45
  15.9 1.0 collective-permute-start
  16.9 0.8 collective-permute-start.5
  17.7 2.4 %collective-permute-start.4 = (f32[2,32,15,128]{3,2,1,0:T(8,128)S(1)}, f32[2,32,15,128]{3,2,1,0:T(8,128)S(1)}, u32[]{:S(2)}, u32[]{:S(2)}) collective-permute-start(f32[2,32,15,128]{3,2,1,0:T(8,128)S(1)} %get-tuple-element.17), channel_id=1, source_target_pairs={{0,2},{1,3},{2,4},{3,5},{4,6},{5,7},{6,0},{7,1},{8,10},{9,11},{10,... | collective-permute-start | bytes 1474568 | tf_op jit(solution)/shard_map/ppermute | solution.py:12
  20.1 0.0 collective-permute-start.3
  20.1 2.6 %collective-permute-start.2 = (f32[2,32,15,128]{3,2,1,0:T(8,128)S(1)}, f32[2,32,15,128]{3,2,1,0:T(8,128)S(1)}, u32[]{:S(2)}, u32[]{:S(2)}) collective-permute-start(f32[2,32,15,128]{3,2,1,0:T(8,128)S(1)} %get-tuple-element.19), channel_id=1, source_target_pairs={{0,7},{1,0},{2,1},{3,2},{4,3},{5,4},{6,5},{7,6},{8,15},{9,8},{10,9... | collective-permute-start | bytes 1474568 | tf_op jit(solution)/shard_map/ppermute | solution.py:12
  22.7 28.0 %collective-permute-done = f32[2,32,15,128]{3,2,1,0:T(8,128)S(1)} collective-permute-done((f32[2,32,15,128]{3,2,1,0:T(8,128)S(1)}, f32[2,32,15,128]{3,2,1,0:T(8,128)S(1)}, u32[]{:S(2)}, u32[]{:S(2)}) %collective-permute-start) | collective-permute-done | bytes 491552 | tf_op jit(solution)/shard_map/ppermute | solution.py:12
  50.8 0.0 copy-start.1
  50.8 0.0 collective-permute-start.1
  50.8 1.9 %collective-permute-done.5 = f32[2,32,15,128]{3,2,1,0:T(8,128)S(1)} collective-permute-done((f32[2,32,15,128]{3,2,1,0:T(8,128)S(1)}, f32[2,32,15,128]{3,2,1,0:T(8,128)S(1)}, u32[]{:S(2)}, u32[]{:S(2)}) %collective-permute-start.5) | collective-permute-done | bytes 491552 | tf_op jit(solution)/shard_map/ppermute | solution.py:12
  52.7 0.0 collective-permute-done.4
  52.7 0.0 collective-permute-done.3
  52.7 0.0 collective-permute-done.2
  52.7 12.6 %collective-permute-done.1 = f32[2,32,15,128]{3,2,1,0:T(8,128)S(1)} collective-permute-done((f32[2,32,15,128]{3,2,1,0:T(8,128)S(1)}, f32[2,32,15,128]{3,2,1,0:T(8,128)S(1)}, u32[]{:S(2)}, u32[]{:S(2)}) %collective-permute-start.1) | collective-permute-done | bytes 491552 | tf_op jit(solution)/shard_map/ppermute | solution.py:12
  65.4 0.3 fusion.25
  65.7 2.4 %collective-permute-start.6 = (f32[2,32,3,128]{3,2,1,0:T(4,128)S(1)}, f32[2,32,3,128]{3,2,1,0:T(4,128)S(1)}, u32[]{:S(2)}, u32[]{:S(2)}) collective-permute-start(f32[2,32,3,128]{3,2,1,0:T(4,128)S(1)} %slice.260), channel_id=1, source_target_pairs={{8,0},{16,8},{24,16},{9,1},{17,9},{25,17},{10,2},{18,10},{26,18},{... | collective-permute-start | bytes 294920 | tf_op jit(solution)/shard_map/ppermute | solution.py:18
  68.1 3.5 %collective-permute-start.7 = (f32[2,32,4,128]{3,2,1,0:T(4,128)S(1)}, f32[2,32,4,128]{3,2,1,0:T(4,128)S(1)}, u32[]{:S(2)}, u32[]{:S(2)}) collective-permute-start(f32[2,32,4,128]{3,2,1,0:T(4,128)S(1)} %slice.261), channel_id=1, source_target_pairs={{0,8},{8,16},{16,24},{1,9},{9,17},{17,25},{2,10},{10,18},{18,26},{... | collective-permute-start | bytes 393224 | tf_op jit(solution)/shard_map/ppermute | solution.py:18
  71.6 0.0 copy-done.1
  71.6 0.7 multiply_bitcast_fusion.29
  72.3 0.8 collective-permute-done.6
  73.1 2.1 %collective-permute-done.7 = f32[2,32,4,128]{3,2,1,0:T(4,128)S(1)} collective-permute-done((f32[2,32,4,128]{3,2,1,0:T(4,128)S(1)}, f32[2,32,4,128]{3,2,1,0:T(4,128)S(1)}, u32[]{:S(2)}, u32[]{:S(2)}) %collective-permute-start.7) | collective-permute-done | bytes 131104 | tf_op jit(solution)/shard_map/ppermute | solution.py:18
  75.2 0.1 fusion.27
  75.3 0.0 copy-done
  75.3 1.0 multiply_bitcast_fusion.15
  76.3 0.5 pad_add_fusion.3
  76.8 0.5 pad_add_fusion
  77.2 0.5 pad_add_fusion.1
  77.7 0.5 pad_add_fusion.2
  78.2 3.1 %add_bitcast_fusion.3 = (f32[2,32,1,8,896]{4,1,0,3,2:T(8,128)S(1)}, f32[2,32,1,8,896]{4,1,0,3,2:T(8,128)S(1)}) fusion(f32[2,32,8,131]{3,1,0,2:T(8,128)S(1)} %pad_add_fusion.3, f32[8]{0:T(128)S(1)} %get-tuple-element.100, f32[8]{0:T(128)S(1)} %get-tuple-element.98, f32[8]{0:T(128)S(1)} %get-tuple-element.99, f32[8]{0:T(128)S(1)} %get-tuple-element.97, ...), kind=kLoop, calls=%fused_computation.16 | loop fusion | flops 8257536 | bytes 4206752 | tf_op jit(solution)/shard_map/stack | solution.py:46
  81.3 3.0 %add_bitcast_fusion.1 = (f32[2,32,1,8,896]{4,1,0,3,2:T(8,128)S(1)}, f32[2,32,1,8,896]{4,1,0,3,2:T(8,128)S(1)}) fusion(f32[2,32,8,131]{3,1,0,2:T(8,128)S(1)} %pad_add_fusion.1, f32[8]{0:T(128)S(1)} %get-tuple-element.100, f32[8]{0:T(128)S(1)} %get-tuple-element.98, f32[8]{0:T(128)S(1)} %get-tuple-element.99, f32[8]{0:T(128)S(1)} %get-tuple-element.97, ...), kind=kLoop, calls=%fused_computation.14 | loop fusion | flops 8257536 | bytes 4206752 | tf_op jit(solution)/shard_map/stack | solution.py:46
  84.3 0.8 pad_maximum_fusion
  85.1 6.9 %fusion.10 = f32[2,32,15,896]{3,2,1,0:T(8,128)S(1)} fusion(f32[2,32,4,8,896]{4,1,0,3,2:T(8,128)S(1)} %pad_maximum_fusion, s32[8]{0:T(128)S(1)} %get-tuple-element.93), kind=kOutput, calls=%fused_computation.11 | convolution fusion | flops 330302400 | bytes 10780704 | tf_op jit(solution)/shard_map/emj,fkmjc->fkec/dot_general | solution.py:47
  92.0 0.3 fusion.44
  92.3 0.1 collective-permute-start.8
  92.4 1.7 %collective-permute-start.13 = (f32[2,32,15,128]{3,2,1,0:T(8,128)S(1)}, f32[2,32,15,128]{3,2,1,0:T(8,128)S(1)}, u32[]{:S(2)}, u32[]{:S(2)}) collective-permute-start(f32[2,32,15,128]{3,2,1,0:T(8,128)S(1)} %get-tuple-element.10), channel_id=1, source_target_pairs={{0,3},{1,4},{2,5},{3,6},{4,7},{5,0},{6,1},{7,2},{8,11},{9,12},{10,... | collective-permute-start | bytes 1474568 | tf_op jit(solution)/shard_map/ppermute | solution.py:12
  94.1 1.5 collective-permute-start.12
  95.6 0.0 collective-permute-start.11
  95.6 2.6 %collective-permute-start.10 = (f32[2,32,15,128]{3,2,1,0:T(8,128)S(1)}, f32[2,32,15,128]{3,2,1,0:T(8,128)S(1)}, u32[]{:S(2)}, u32[]{:S(2)}) collective-permute-start(f32[2,32,15,128]{3,2,1,0:T(8,128)S(1)} %get-tuple-element.13), channel_id=1, source_target_pairs={{0,7},{1,0},{2,1},{3,2},{4,3},{5,4},{6,5},{7,6},{8,15},{9,8},{10,9... | collective-permute-start | bytes 1474568 | tf_op jit(solution)/shard_map/ppermute | solution.py:12
  98.3 27.7 %collective-permute-done.8 = f32[2,32,15,128]{3,2,1,0:T(8,128)S(1)} collective-permute-done((f32[2,32,15,128]{3,2,1,0:T(8,128)S(1)}, f32[2,32,15,128]{3,2,1,0:T(8,128)S(1)}, u32[]{:S(2)}, u32[]{:S(2)}) %collective-permute-start.8) | collective-permute-done | bytes 491552 | tf_op jit(solution)/shard_map/ppermute | solution.py:12
  126.0 0.0 collective-permute-start.9
  126.0 2.3 %collective-permute-done.13 = f32[2,32,15,128]{3,2,1,0:T(8,128)S(1)} collective-permute-done((f32[2,32,15,128]{3,2,1,0:T(8,128)S(1)}, f32[2,32,15,128]{3,2,1,0:T(8,128)S(1)}, u32[]{:S(2)}, u32[]{:S(2)}) %collective-permute-start.13) | collective-permute-done | bytes 491552 | tf_op jit(solution)/shard_map/ppermute | solution.py:12
  128.2 0.0 collective-permute-done.12
  128.2 0.0 collective-permute-done.11
  128.2 0.0 collective-permute-done.10
  128.2 12.1 %collective-permute-done.9 = f32[2,32,15,128]{3,2,1,0:T(8,128)S(1)} collective-permute-done((f32[2,32,15,128]{3,2,1,0:T(8,128)S(1)}, f32[2,32,15,128]{3,2,1,0:T(8,128)S(1)}, u32[]{:S(2)}, u32[]{:S(2)}) %collective-permute-start.9) | collective-permute-done | bytes 491552 | tf_op jit(solution)/shard_map/ppermute | solution.py:12
  140.3 0.3 fusion.20
  140.6 2.7 %collective-permute-start.15 = (f32[2,32,4,128]{3,2,1,0:T(4,128)S(1)}, f32[2,32,4,128]{3,2,1,0:T(4,128)S(1)}, u32[]{:S(2)}, u32[]{:S(2)}) collective-permute-start(f32[2,32,4,128]{3,2,1,0:T(4,128)S(1)} %slice.271), channel_id=1, source_target_pairs={{0,8},{8,16},{16,24},{1,9},{9,17},{17,25},{2,10},{10,18},{18,26},{... | collective-permute-start | bytes 393224 | tf_op jit(solution)/shard_map/ppermute | solution.py:18
  143.3 3.2 %collective-permute-start.14 = (f32[2,32,3,128]{3,2,1,0:T(4,128)S(1)}, f32[2,32,3,128]{3,2,1,0:T(4,128)S(1)}, u32[]{:S(2)}, u32[]{:S(2)}) collective-permute-start(f32[2,32,3,128]{3,2,1,0:T(4,128)S(1)} %slice.270), channel_id=1, source_target_pairs={{8,0},{16,8},{24,16},{9,1},{17,9},{25,17},{10,2},{18,10},{26,18},{... | collective-permute-start | bytes 294920 | tf_op jit(solution)/shard_map/ppermute | solution.py:18
  146.5 4.5 %collective-permute-done.14 = f32[2,32,3,128]{3,2,1,0:T(4,128)S(1)} collective-permute-done((f32[2,32,3,128]{3,2,1,0:T(4,128)S(1)}, f32[2,32,3,128]{3,2,1,0:T(4,128)S(1)}, u32[]{:S(2)}, u32[]{:S(2)}) %collective-permute-start.14) | collective-permute-done | bytes 98336 | tf_op jit(solution)/shard_map/ppermute | solution.py:18
  151.0 0.0 collective-permute-done.15
  151.0 0.1 fusion.26
  151.1 0.4 convolution_bitcast_fusion
  151.5 0.9 copy.15
  (6 shorter events, 0.1 us)
Async XLA Ops:
  15.9 34.9 %collective-permute-start = (f32[2,32,15,128]{3,2,1,0:T(8,128)S(1)}, f32[2,32,15,128]{3,2,1,0:T(8,128)S(1)}, u32[]{:S(2)}, u32[]{:S(2)}) collective-permute-start(f32[2,32,15,128]{3,2,1,0:T(8,128)S(1)} %get-tuple-element.15), channel_id=1, source_target_pairs={{0,5},{1,6},{2,7},{3,0},{4,1},{5,2},{6,3},{7,4},{8,13},{9,14},{10,... | collective-permute-start | bytes 1474568 | tf_op jit(solution)/shard_map/ppermute | solution.py:12
  16.9 35.8 %collective-permute-start.5 = (f32[2,32,15,128]{3,2,1,0:T(8,128)S(1)}, f32[2,32,15,128]{3,2,1,0:T(8,128)S(1)}, u32[]{:S(2)}, u32[]{:S(2)}) collective-permute-start(f32[2,32,15,128]{3,2,1,0:T(8,128)S(1)} %get-tuple-element.16), channel_id=1, source_target_pairs={{0,3},{1,4},{2,5},{3,6},{4,7},{5,0},{6,1},{7,2},{8,11},{9,12},{10,... | collective-permute-start | bytes 1474568 | tf_op jit(solution)/shard_map/ppermute | solution.py:12
  17.7 35.0 %collective-permute-start.4 = (f32[2,32,15,128]{3,2,1,0:T(8,128)S(1)}, f32[2,32,15,128]{3,2,1,0:T(8,128)S(1)}, u32[]{:S(2)}, u32[]{:S(2)}) collective-permute-start(f32[2,32,15,128]{3,2,1,0:T(8,128)S(1)} %get-tuple-element.17), channel_id=1, source_target_pairs={{0,2},{1,3},{2,4},{3,5},{4,6},{5,7},{6,0},{7,1},{8,10},{9,11},{10,... | collective-permute-start | bytes 1474568 | tf_op jit(solution)/shard_map/ppermute | solution.py:12
  20.1 32.6 %collective-permute-start.3 = (f32[2,32,15,128]{3,2,1,0:T(8,128)S(1)}, f32[2,32,15,128]{3,2,1,0:T(8,128)S(1)}, u32[]{:S(2)}, u32[]{:S(2)}) collective-permute-start(f32[2,32,15,128]{3,2,1,0:T(8,128)S(1)} %get-tuple-element.18), channel_id=1, source_target_pairs={{0,1},{1,2},{2,3},{3,4},{4,5},{5,6},{6,7},{7,0},{8,9},{9,10},{10,1... | collective-permute-start | bytes 1474568 | tf_op jit(solution)/shard_map/ppermute | solution.py:12
  20.1 32.6 %collective-permute-start.2 = (f32[2,32,15,128]{3,2,1,0:T(8,128)S(1)}, f32[2,32,15,128]{3,2,1,0:T(8,128)S(1)}, u32[]{:S(2)}, u32[]{:S(2)}) collective-permute-start(f32[2,32,15,128]{3,2,1,0:T(8,128)S(1)} %get-tuple-element.19), channel_id=1, source_target_pairs={{0,7},{1,0},{2,1},{3,2},{4,3},{5,4},{6,5},{7,6},{8,15},{9,8},{10,9... | collective-permute-start | bytes 1474568 | tf_op jit(solution)/shard_map/ppermute | solution.py:12
  50.8 20.8 %copy-start.1 = (f32[2,4,8,128]{3,2,1,0:T(8,128)S(1)}, f32[2,4,8,128]{3,2,1,0:T(8,128)}, u32[]{:S(2)}) copy-start(f32[2,4,8,128]{3,2,1,0:T(8,128)} %param.7) | copy-start | bytes 98308
  50.8 24.5 %copy-start = (f32[2,8,32,32]{3,2,1,0:T(8,128)S(1)}, f32[2,8,32,32]{3,2,1,0:T(8,128)}, u32[]{:S(2)}) copy-start(f32[2,8,32,32]{3,2,1,0:T(8,128)} %param.11) | copy-start | bytes 196612
  50.8 14.6 %collective-permute-start.1 = (f32[2,32,15,128]{3,2,1,0:T(8,128)S(1)}, f32[2,32,15,128]{3,2,1,0:T(8,128)S(1)}, u32[]{:S(2)}, u32[]{:S(2)}) collective-permute-start(f32[2,32,15,128]{3,2,1,0:T(8,128)S(1)} %get-tuple-element.20), channel_id=1, source_target_pairs={{0,6},{1,7},{2,0},{3,1},{4,2},{5,3},{6,4},{7,5},{8,14},{9,15},{10,... | collective-permute-start | bytes 1474568 | tf_op jit(solution)/shard_map/ppermute | solution.py:12
  65.7 7.4 %collective-permute-start.6 = (f32[2,32,3,128]{3,2,1,0:T(4,128)S(1)}, f32[2,32,3,128]{3,2,1,0:T(4,128)S(1)}, u32[]{:S(2)}, u32[]{:S(2)}) collective-permute-start(f32[2,32,3,128]{3,2,1,0:T(4,128)S(1)} %slice.260), channel_id=1, source_target_pairs={{8,0},{16,8},{24,16},{9,1},{17,9},{25,17},{10,2},{18,10},{26,18},{... | collective-permute-start | bytes 294920 | tf_op jit(solution)/shard_map/ppermute | solution.py:18
  68.1 7.1 %collective-permute-start.7 = (f32[2,32,4,128]{3,2,1,0:T(4,128)S(1)}, f32[2,32,4,128]{3,2,1,0:T(4,128)S(1)}, u32[]{:S(2)}, u32[]{:S(2)}) collective-permute-start(f32[2,32,4,128]{3,2,1,0:T(4,128)S(1)} %slice.261), channel_id=1, source_target_pairs={{0,8},{8,16},{16,24},{1,9},{9,17},{17,25},{2,10},{10,18},{18,26},{... | collective-permute-start | bytes 393224 | tf_op jit(solution)/shard_map/ppermute | solution.py:18
  92.3 33.6 %collective-permute-start.8 = (f32[2,32,15,128]{3,2,1,0:T(8,128)S(1)}, f32[2,32,15,128]{3,2,1,0:T(8,128)S(1)}, u32[]{:S(2)}, u32[]{:S(2)}) collective-permute-start(f32[2,32,15,128]{3,2,1,0:T(8,128)S(1)} %get-tuple-element.9), channel_id=1, source_target_pairs={{0,5},{1,6},{2,7},{3,0},{4,1},{5,2},{6,3},{7,4},{8,13},{9,14},{10,... | collective-permute-start | bytes 1474568 | tf_op jit(solution)/shard_map/ppermute | solution.py:12
  92.4 35.8 %collective-permute-start.13 = (f32[2,32,15,128]{3,2,1,0:T(8,128)S(1)}, f32[2,32,15,128]{3,2,1,0:T(8,128)S(1)}, u32[]{:S(2)}, u32[]{:S(2)}) collective-permute-start(f32[2,32,15,128]{3,2,1,0:T(8,128)S(1)} %get-tuple-element.10), channel_id=1, source_target_pairs={{0,3},{1,4},{2,5},{3,6},{4,7},{5,0},{6,1},{7,2},{8,11},{9,12},{10,... | collective-permute-start | bytes 1474568 | tf_op jit(solution)/shard_map/ppermute | solution.py:12
  94.1 34.1 %collective-permute-start.12 = (f32[2,32,15,128]{3,2,1,0:T(8,128)S(1)}, f32[2,32,15,128]{3,2,1,0:T(8,128)S(1)}, u32[]{:S(2)}, u32[]{:S(2)}) collective-permute-start(f32[2,32,15,128]{3,2,1,0:T(8,128)S(1)} %get-tuple-element.11), channel_id=1, source_target_pairs={{0,2},{1,3},{2,4},{3,5},{4,6},{5,7},{6,0},{7,1},{8,10},{9,11},{10,... | collective-permute-start | bytes 1474568 | tf_op jit(solution)/shard_map/ppermute | solution.py:12
  95.6 32.6 %collective-permute-start.11 = (f32[2,32,15,128]{3,2,1,0:T(8,128)S(1)}, f32[2,32,15,128]{3,2,1,0:T(8,128)S(1)}, u32[]{:S(2)}, u32[]{:S(2)}) collective-permute-start(f32[2,32,15,128]{3,2,1,0:T(8,128)S(1)} %get-tuple-element.12), channel_id=1, source_target_pairs={{0,1},{1,2},{2,3},{3,4},{4,5},{5,6},{6,7},{7,0},{8,9},{9,10},{10,1... | collective-permute-start | bytes 1474568 | tf_op jit(solution)/shard_map/ppermute | solution.py:12
  95.6 32.6 %collective-permute-start.10 = (f32[2,32,15,128]{3,2,1,0:T(8,128)S(1)}, f32[2,32,15,128]{3,2,1,0:T(8,128)S(1)}, u32[]{:S(2)}, u32[]{:S(2)}) collective-permute-start(f32[2,32,15,128]{3,2,1,0:T(8,128)S(1)} %get-tuple-element.13), channel_id=1, source_target_pairs={{0,7},{1,0},{2,1},{3,2},{4,3},{5,4},{6,5},{7,6},{8,15},{9,8},{10,9... | collective-permute-start | bytes 1474568 | tf_op jit(solution)/shard_map/ppermute | solution.py:12
  126.0 14.4 %collective-permute-start.9 = (f32[2,32,15,128]{3,2,1,0:T(8,128)S(1)}, f32[2,32,15,128]{3,2,1,0:T(8,128)S(1)}, u32[]{:S(2)}, u32[]{:S(2)}) collective-permute-start(f32[2,32,15,128]{3,2,1,0:T(8,128)S(1)} %get-tuple-element.14), channel_id=1, source_target_pairs={{0,6},{1,7},{2,0},{3,1},{4,2},{5,3},{6,4},{7,5},{8,14},{9,15},{10,... | collective-permute-start | bytes 1474568 | tf_op jit(solution)/shard_map/ppermute | solution.py:12
  140.6 10.4 %collective-permute-start.15 = (f32[2,32,4,128]{3,2,1,0:T(4,128)S(1)}, f32[2,32,4,128]{3,2,1,0:T(4,128)S(1)}, u32[]{:S(2)}, u32[]{:S(2)}) collective-permute-start(f32[2,32,4,128]{3,2,1,0:T(4,128)S(1)} %slice.271), channel_id=1, source_target_pairs={{0,8},{8,16},{16,24},{1,9},{9,17},{17,25},{2,10},{10,18},{18,26},{... | collective-permute-start | bytes 393224 | tf_op jit(solution)/shard_map/ppermute | solution.py:18
  143.3 7.7 %collective-permute-start.14 = (f32[2,32,3,128]{3,2,1,0:T(4,128)S(1)}, f32[2,32,3,128]{3,2,1,0:T(4,128)S(1)}, u32[]{:S(2)}, u32[]{:S(2)}) collective-permute-start(f32[2,32,3,128]{3,2,1,0:T(4,128)S(1)} %slice.270), channel_id=1, source_target_pairs={{8,0},{16,8},{24,16},{9,1},{17,9},{25,17},{10,2},{18,10},{26,18},{... | collective-permute-start | bytes 294920 | tf_op jit(solution)/shard_map/ppermute | solution.py:18
where the time goes:
time: 155 us; the launch traced here: 152 us
  waiting for transfers between devices  92.1 us (59%)
  starting transfers between devices  24.5 us (16%)
  other arithmetic  22.9 us (15%)
  matrix products  11.1 us (7%)
  local copies, waits for them, and re-layouts  1.58 us (1%)
    ppermute x12, waiting for transfers between devices, shifted(): lax.ppermute(array, axis, [(i, (i + by) % size) for i in range(size)])  84.7 us
    ppermute x12, starting transfers between devices, shifted(): lax.ppermute(array, axis, [(i, (i + by) % size) for i in range(size)])  12.8 us
    another operation x5, other arithmetic, spread_local(): stacked = jnp.stack(placed_all, axis=2)  12.7 us
    ppermute x4, starting transfers between devices, from_behind(): lax.ppermute(value, axis, [(source, source + steps) for source in range(l...  11.7 us
    dot_general x2, matrix products, spread_local(): jnp.einsum('emj,fkmjc->fkec', row_onehot, stacked, precision=lax.Precisio...  9.75 us
    ppermute x4, waiting for transfers between devices, from_behind(): lax.ppermute(value, axis, [(source, source + steps) for source in range(l...  7.41 us
    mul x5, other arithmetic, spread_local(): term = carried * (lat_w[m] * lon_w[o])[None, None]  4.53 us
    add x6, other arithmetic, spread_local(): lon_row = lon_row + jnp.pad(term, ((0, 0), (0, 0), (0, 0), (o, 3 - o)))  3.65 us
  transfers between devices with their start and end apart: 16, of which 9 were waited for; matrix products, arithmetic and copies ran while one was open for 0% of the time, Pallas kernels for 0%

commit v1 on v0

--- a/solution.py
+++ b/solution.py
@@ -1,10 +1,19 @@
+import functools
+
 import jax
 import jax.numpy as jnp
 from jax import lax
+from jax.experimental import pallas as pl
+from jax.experimental.pallas import tpu as pltpu
 from jax.sharding import PartitionSpec as P
 
 R = 2
 H = 2
+NODES = 4
+RING = 8
+LOW = H + 1
+HIGH = H + 2
+VMEM_LIMIT = 48 * 1024 * 1024
 
 
 def shifted(array, axis, by):
@@ -20,12 +29,10 @@
 
 def spread_local(carried, lat_w, lon_w, row_table, block_table, lat_start, own_block, cycle_size):
     fields, levels, lat_rows, points = carried.shape
-    low_rim = H + 1
-    high_rim = H + 2
-    ext_rows = lat_rows + low_rim + high_rim
+    ext_rows = lat_rows + LOW + HIGH
     block_count = 2 * R + 3
     width = block_count * points
-    rel_row = row_table - lat_start + low_rim
+    rel_row = row_table - lat_start + LOW
     rel_block = (block_table - own_block + R) % cycle_size
     target = lax.broadcasted_iota(jnp.int32, (ext_rows, 4, lat_rows), 0)
     node = lax.broadcasted_iota(jnp.int32, (ext_rows, 4, lat_rows), 1)
@@ -58,19 +65,17 @@
 
 
 def fold_rims(buffer, lat_rows):
-    low_rim = H + 1
-    high_rim = H + 2
-    upper = buffer[:, :, :low_rim]
-    lower = buffer[:, :, low_rim + lat_rows :]
-    interior = buffer[:, :, low_rim : low_rim + lat_rows]
+    upper = buffer[:, :, :LOW]
+    lower = buffer[:, :, LOW + lat_rows :]
+    interior = buffer[:, :, LOW : LOW + lat_rows]
     from_after = from_behind(upper, "lat", -1)
     from_before = from_behind(lower, "lat", 1)
-    interior = interior + jnp.pad(from_after, ((0, 0), (0, 0), (lat_rows - low_rim, 0), (0, 0)))
-    interior = interior + jnp.pad(from_before, ((0, 0), (0, 0), (0, lat_rows - high_rim), (0, 0)))
+    interior = interior + jnp.pad(from_after, ((0, 0), (0, 0), (lat_rows - LOW, 0), (0, 0)))
+    interior = interior + jnp.pad(from_before, ((0, 0), (0, 0), (0, lat_rows - HIGH), (0, 0)))
     return interior
 
 
-def body(adjoint_in, lat_weights, lon_weights, depart_rows, depart_blocks, vertical_inverse):
+def plain_body(adjoint_in, lat_weights, lon_weights, depart_rows, depart_blocks, vertical_inverse):
     fields, levels, lat_rows, points = adjoint_in.shape
     cycle_size = lax.axis_size("lon")
     own_block = lax.axis_index("lon")
@@ -95,18 +100,413 @@
     return carried
 
 
+def vmem(shape, rank=2):
+    return pl.BlockSpec(shape, lambda i: (0,) * rank, memory_space=pltpu.VMEM)
+
+
+def smem_tile(tile):
+    return pl.BlockSpec((8, 128), lambda i: (tile, 0), memory_space=pltpu.SMEM)
+
+
+def smem_whole(size):
+    return pl.BlockSpec((size,), lambda i: (0,), memory_space=pltpu.SMEM)
+
+
+def call(kernel, out_rows, in_specs, scratch, cost, *args):
+    outs = [jax.ShapeDtypeStruct((n, 128), jnp.float32) for n in out_rows]
+    return pl.pallas_call(
+        kernel,
+        grid=(1,),
+        out_shape=outs,
+        in_specs=in_specs,
+        out_specs=[vmem((n, 128)) for n in out_rows],
+        scratch_shapes=scratch,
+        compiler_params=pltpu.CompilerParams(vmem_limit_bytes=VMEM_LIMIT),
+        cost_estimate=pl.CostEstimate(flops=cost, bytes_accessed=cost, transcendentals=0),
+    )(*args)
+
+
+def rolled(value):
+    return [pltpu.roll(value, 127, 1), value, pltpu.roll(value, 1, 1), pltpu.roll(value, 2, 1)]
+
+
+def products(weights):
+    turned = rolled(weights)
+    return [turned[o][0:4] * turned[o][4 + o : 5 + o] for o in range(NODES)]
+
+
+def lanes_in(low, high):
+    lane = lax.broadcasted_iota(jnp.int32, (4, 128), 1)
+    return ((lane >= low) & (lane < high)).astype(jnp.float32)
+
+
+def main_products(prods):
+    return [
+        (0, prods[0] * lanes_in(0, 127)),
+        (1, prods[1]),
+        (2, prods[2] * lanes_in(1, 128)),
+        (3, prods[3] * lanes_in(2, 128)),
+    ]
+
+
+def left_products(prods):
+    return [(0, prods[0] * lanes_in(127, 128))]
+
+
+def right_products(prods):
+    return [(2, prods[2] * lanes_in(0, 1)), (3, prods[3] * lanes_in(0, 2))]
+
+
+def add_terms(sources, terms, target, first):
+    for m in range(NODES):
+        for kk, turned in enumerate(sources):
+            total = None
+            for o, weight in terms:
+                term = turned[o] * weight[m : m + 1]
+                total = term if total is None else total + term
+            target[first + m, 8 * kk : 8 * kk + 8, :] += total
+
+
+def assemble(levels, me_ref, adj, lat_w, lon_w, rows, blocks, mx, my, md, w0):
+    field = me_ref[0] // 4
+    per_row = levels + 8
+    lane = lax.broadcasted_iota(jnp.int32, (8, 128), 1)
+    table = jnp.zeros((8, 128), jnp.float32)
+    for at, value in enumerate((rows[1], blocks[1], rows[0], blocks[0])):
+        table = jnp.where(lane == at, value.astype(jnp.float32), table)
+    for out in (mx, my, md):
+        out[8 * per_row : 8 * per_row + 8, :] = table
+    for i in range(8):
+        base = i * per_row
+        for kk in range(0, levels, 8):
+            own = adj[pl.ds((field * levels + kk) * 8 + i, 8, stride=8), :]
+            other = adj[pl.ds(((1 - field) * levels + kk) * 8 + i, 8, stride=8), :]
+            mx[base + kk : base + kk + 8, :] = own
+            my[base + kk : base + kk + 8, :] = other
+            md[base + kk : base + kk + 8, :] = other
+        for s in (0, 1):
+            lat = lat_w[pl.ds(s * 32 + i, 4, stride=8), :]
+            lon = lon_w[pl.ds(s * 32 + i, 4, stride=8), :]
+            if s == 1:
+                for out in (mx, my, md):
+                    out[base + levels : base + levels + 4, :] = lat
+                    out[base + levels + 4 : base + levels + 8, :] = lon
+            else:
+                tail = 8 * per_row + 8
+                w0[8 * i : 8 * i + 4, :] = lat
+                w0[8 * i + 4 : 8 * i + 8, :] = lon
+                my[tail + 8 * i : tail + 8 * i + 4, :] = lat
+                my[tail + 8 * i + 4 : tail + 8 * i + 8, :] = lon
+
+
+def first_spread(levels, me_ref, *refs):
+    messages, tables = refs[0:8], refs[8:16]
+    w0, v1, part, m1, m2, acc = refs[16:]
+    per_row = levels + 8
+    me, lat_start, even = me_ref[0], me_ref[1], me_ref[2]
+    slot = me // 4
+    acc[...] = jnp.zeros_like(acc)
+    for message, table in zip(messages, tables):
+
+        def row(i, _, message=message, table=table):
+            first = table[i, 0].astype(jnp.int32) - lat_start + LOW
+            tau = table[i, 1].astype(jnp.int32)
+            delta = (tau - me) & 3
+            base = pl.multiple_of(i * per_row, 8)
+
+            def work(which, block):
+                prods = which(products(message[pl.ds(base + levels, 8), :]))
+                sources = [rolled(message[pl.ds(base + kk, 8), :]) for kk in range(0, levels, 8)]
+                add_terms(sources, prods, acc, (block // 4) * 15 + first)
+
+            @pl.when(delta == 0)
+            def _():
+                work(main_products, tau)
+
+            @pl.when(delta == 1)
+            def _():
+                work(left_products, (tau + 7) & 7)
+
+            @pl.when(delta == 3)
+            def _():
+                work(right_products, (tau + 1) & 7)
+
+            return 0
+
+        lax.fori_loop(0, 8, row, 0)
+    part[...] = acc[...].reshape(part.shape)
+
+    def write(out, part_row, count, row):
+        for h in range(2):
+            out[h * 8 * levels : (h * 8 + count) * levels, :] = acc[
+                h * 15 + part_row : h * 15 + part_row + count
+            ].reshape(count * levels, 128)
+        at = 16 * levels
+        tail = 8 * per_row + 8
+        for_y = messages[2][tail + 8 * row : tail + 8 * row + 32, :]
+        out[pl.ds(pl.multiple_of(at + slot * 32, 8), 32), :] = w0[8 * row : 8 * row + 32, :]
+        out[pl.ds(pl.multiple_of(at + (1 - slot) * 32, 8), 32), :] = for_y
+        at += 64
+        out[at : at + levels, :] = jnp.concatenate([v1[row + j] for j in range(4)], axis=1)
+        at += levels
+        out[pl.ds(pl.multiple_of(at + slot * 8, 8), 8), :] = messages[0][8 * per_row : tail, :]
+        out[pl.ds(pl.multiple_of(at + (1 - slot) * 8, 8), 8), :] = messages[2][8 * per_row : tail, :]
+
+    @pl.when(even == 1)
+    def _():
+        write(m1, 7, 8, 4)
+        write(m2, 0, 6, 0)
+
+    @pl.when(even == 0)
+    def _():
+        write(m2, 7, 8, 4)
+        write(m1, 0, 6, 0)
+
+
+def vertical(matrix, column):
+    m_high = matrix.astype(jnp.bfloat16)
+    m_low = (matrix - m_high.astype(jnp.float32)).astype(jnp.bfloat16)
+    c_high = column.astype(jnp.bfloat16)
+    c_low = (column - c_high.astype(jnp.float32)).astype(jnp.bfloat16)
+    return lax.dot_general(
+        jnp.concatenate([m_high, m_low, m_high], axis=0),
+        jnp.concatenate([c_high, c_high, c_low], axis=0),
+        (((0,), (0,)), ((), ())),
+        preferred_element_type=jnp.float32,
+    )
+
+
+def second_spread(levels, me_ref, part, r1, r2, w0, ry, v1, own_tab, y_tab, *refs):
+    r1_tabs, r2_tabs, outs, (state, weights, acc) = refs[0:2], refs[2:4], refs[4:12], refs[12:]
+    per_row = levels + 8
+    me, lat_start, even, at_start, at_end = (me_ref[n] for n in range(5))
+    slot = me // 4
+    is_even = even == 1
+
+    def before(rows):
+        return jnp.where(is_even, r2[rows, :], r1[rows, :])
+
+    def after(rows):
+        return jnp.where(is_even, r1[rows, :], r2[rows, :])
+
+    def lines(start, count):
+        return slice(start, start + count)
+
+    at_w = 16 * levels
+    at_v = at_w + 64
+    tail = 8 * per_row + 8
+    for h in range(2):
+        for j in range(4):
+            weights[h * 15 + j] = before(lines(at_w + h * 32 + 8 * j, 8))
+        for j in range(3):
+            weights[h * 15 + 12 + j] = after(lines(at_w + h * 32 + 8 * j, 8))
+    for i in range(8):
+        weights[slot * 15 + 4 + i] = w0[lines(8 * i, 8), :]
+        weights[(1 - slot) * 15 + 4 + i] = ry[lines(tail + 8 * i, 8), :]
+    v_before = before(lines(at_v, levels))
+    v_after = after(lines(at_v, levels))
+    for n in range(15):
+        halves = []
+        for h in range(2):
+            own = (h * 15 + n - 1) * levels
+            there = lines((h * 8 + n) * levels, levels)
+            if n == 0:
+                value = before(there)
+            elif n < 8:
+                value = part[lines(own, levels), :] + before(there)
+            elif n == 8:
+                value = part[lines(own, levels), :]
+            else:
+                value = part[lines(own, levels), :] + after(lines((h * 8 + n - 9) * levels, levels))
+            halves.append(value)
+        if n < 4:
+            matrix = v_before[:, n * levels : (n + 1) * levels]
+        elif n < 12:
+            matrix = v1[n - 4]
+        else:
+            matrix = v_after[:, (n - 12) * levels : (n - 11) * levels]
+        result = vertical(matrix, jnp.concatenate(halves, axis=1))
+        state[n] = result[:, :128]
+        state[15 + n] = result[:, 128:]
+    for q in range(8):
+        acc[q * 22 + 7 : q * 22 + 15] = jnp.zeros((8, levels, 128), jnp.float32)
+
+    def spread(n, h, row, tau):
+        tau = tau.astype(jnp.int32)
+        first = row.astype(jnp.int32) - lat_start + 7
+        prods = products(weights[h * 15 + n])
+        sources = [rolled(state[h * 15 + n, kk : kk + 8, :]) for kk in range(0, levels, 8)]
+        add_terms(sources, main_products(prods), acc, (tau ^ me) * 22 + first)
+        add_terms(sources, left_products(prods), acc, (((tau + 7) & 7) ^ me) * 22 + first)
+        add_terms(sources, right_products(prods), acc, (((tau + 1) & 7) ^ me) * 22 + first)
+
+    for h in range(2):
+
+        def own_row(i, _, h=h):
+            mine = slot == h
+            spread(i + 4, h, *(jnp.where(mine, own_tab[i, c], y_tab[i, c]) for c in (2, 3)))
+            return 0
+
+        def before_row(i, _, h=h):
+            spread(i, h, *(jnp.where(is_even, r2_tabs[h][i + 4, c], r1_tabs[h][i + 4, c]) for c in (2, 3)))
+            return 0
+
+        def after_row(i, _, h=h):
+            spread(i + 12, h, *(jnp.where(is_even, r1_tabs[h][i, c], r2_tabs[h][i, c]) for c in (2, 3)))
+            return 0
+
+        lax.fori_loop(0, 8, own_row, 0)
+
+        @pl.when(at_start == 0)
+        def _():
+            lax.fori_loop(0, 4, before_row, 0)
+
+        @pl.when(at_end == 0)
+        def _():
+            lax.fori_loop(0, 3, after_row, 0)
+
+    for q in range(8):
+        outs[q][...] = acc[q * 22 + 7 : q * 22 + 15].reshape(8 * levels, 128)
+
+
+def finish(levels, me_ref, own, pair, across, up, diagonal, v0, out):
+    field = me_ref[0] // 4
+    for i in range(8):
+        rows = slice(i * levels, (i + 1) * levels)
+        mine = own[rows, :] + pair[rows, :] + across[rows, :]
+        other = up[rows, :] + diagonal[rows, :]
+        result = vertical(v0[i], jnp.concatenate([mine, other], axis=1))
+        for kk in range(0, levels, 8):
+            out[pl.ds((field * levels + kk) * 8 + i, 8, stride=8), :] = result[kk : kk + 8, :128]
+            out[pl.ds(((1 - field) * levels + kk) * 8 + i, 8, stride=8), :] = result[kk : kk + 8, 128:]
+
+
+def swap_lon(value, bits):
+    return lax.ppermute(value, "lon", [(i, i ^ bits) for i in range(RING)])
+
+
+def swap_lat(value, odd):
+    count = lax.axis_size("lat")
+    pairs = [(i, i + 1) for i in range(odd, count - 1, 2)]
+    return lax.ppermute(value, "lat", pairs + [(b, a) for a, b in pairs])
+
+
+def ring_body(adjoint_in, lat_weights, lon_weights, depart_rows, depart_blocks, vertical_inverse):
+    fields, levels, lat_rows, points = adjoint_in.shape
+    me = lax.axis_index("lon")
+    band = lax.axis_index("lat")
+    count = lax.axis_size("lat")
+    info = jnp.stack([me, band * lat_rows, 1 - band % 2, band == 0, band == count - 1]).astype(jnp.int32)
+    per_row = levels + 8
+    short = 8 * per_row + 8
+    long = short + 64
+    table_tile = per_row
+    size = adjoint_in.size
+    mx, my, md, w0 = call(
+        functools.partial(assemble, levels),
+        [short, long, short, 64],
+        [smem_whole(5), vmem((fields * levels * 8, 128)), vmem((64, 128)), vmem((64, 128))]
+        + [vmem((2, 8, 1), 3)] * 2,
+        [],
+        size,
+        info,
+        adjoint_in.reshape(-1, points),
+        lat_weights.reshape(-1, points),
+        lon_weights.reshape(-1, points),
+        depart_rows,
+        depart_blocks,
+    )
+    rd, ry, rx = swap_lon(md, 6), swap_lon(my, 4), swap_lon(mx, 2)
+    messages = [mx, rx, ry, rd] + [swap_lon(value, 1) for value in (mx, rx, ry, rd)]
+    lat_size = 16 * levels + 64 + levels + 16
+    part, m1, m2 = call(
+        functools.partial(first_spread, levels),
+        [30 * levels, lat_size, lat_size],
+        [smem_whole(5)]
+        + [vmem(value.shape) for value in messages]
+        + [smem_tile(table_tile)] * 8
+        + [vmem((64, 128)), vmem((8, levels, levels), 3)],
+        [pltpu.VMEM((30, levels, 128), jnp.float32)],
+        8 * size,
+        info,
+        *messages,
+        *messages,
+        w0,
+        vertical_inverse[1],
+    )
+    r1, r2 = swap_lat(m1, 0), swap_lat(m2, 1)
+    last = (lat_size - 16) // 8
+    pieces = call(
+        functools.partial(second_spread, levels),
+        [8 * levels] * 8,
+        [
+            smem_whole(5),
+            vmem((30 * levels, 128)),
+            vmem((lat_size, 128)),
+            vmem((lat_size, 128)),
+            vmem((64, 128)),
+            vmem((long, 128)),
+            vmem((8, levels, levels), 3),
+            smem_tile(table_tile),
+            smem_tile(table_tile),
+        ]
+        + [smem_tile(last), smem_tile(last + 1)] * 2,
+        [
+            pltpu.VMEM((30, levels, 128), jnp.float32),
+            pltpu.VMEM((30, 8, 128), jnp.float32),
+            pltpu.VMEM((8 * 22, levels, 128), jnp.float32),
+        ],
+        16 * size,
+        info,
+        part,
+        r1,
+        r2,
+        w0,
+        ry,
+        vertical_inverse[1],
+        mx,
+        ry,
+        r1,
+        r1,
+        r2,
+        r2,
+    )
+    received = {}
+    for bits in (6, 4, 2):
+        received[bits] = swap_lon(pieces[bits] + swap_lon(pieces[bits + 1], 1), bits)
+    pair = swap_lon(pieces[1], 1)
+    (out,) = call(
+        functools.partial(finish, levels),
+        [fields * levels * 8],
+        [smem_whole(5)] + [vmem((8 * levels, 128))] * 5 + [vmem((8, levels, levels), 3)],
+        [],
+        size,
+        info,
+        pieces[0],
+        pair,
+        received[2],
+        received[4],
+        received[6],
+        vertical_inverse[0],
+    )
+    return out.reshape(adjoint_in.shape)
+
+
 def solution(mesh):
-    return jax.shard_map(
-        body,
-        mesh=mesh,
-        in_specs=(
-            P(None, None, "lat", "lon"),
-            P(None, None, "lat", "lon"),
-            P(None, None, "lat", "lon"),
-            P(None, "lat", "lon"),
-            P(None, "lat", "lon"),
-            P(None, "lat", None, None),
-        ),
-        out_specs=P(None, None, "lat", "lon"),
-        check_vma=False,
+    specs = (
+        P(None, None, "lat", "lon"),
+        P(None, None, "lat", "lon"),
+        P(None, None, "lat", "lon"),
+        P(None, "lat", "lon"),
+        P(None, "lat", "lon"),
+        P(None, "lat", None, None),
     )
+
+    def whole(*args):
+        fields, levels, rows, points = args[0].shape
+        lat, lon = mesh.shape["lat"], mesh.shape["lon"]
+        ring = (fields, lon, rows // lat, points // lon) == (2, RING, 8, 128) and levels % 8 == 0 and levels * 4 == 128
+        body = ring_body if ring else plain_body
+        return jax.shard_map(body, mesh=mesh, in_specs=specs, out_specs=specs[0], check_vma=False)(*args)
+
+    return whole

time: 155 us -> 52.5 us (0.34); the launches traced: 152 us -> 52.2 us
  waiting for transfers between devices: 92.1 us -> 21.9 us
  other arithmetic: 22.9 us -> 0.05 us
  Pallas kernels: 0 us -> 14.1 us
  matrix products: 11.1 us -> 0 us
  starting transfers between devices: 24.5 us -> 14.1 us
    ppermute x16, waiting for transfers between devices: 92.1 us -> 21.9 us  [the longest x14 14.5 us: swap_lon(): return lax.ppermute(value, 'lon', [(i, i ^ bits) for i in range(RING)])]
    pallas_call x0 -> x4, Pallas kernels: none -> 14.1 us  [call(): pl.pallas_call(kernel, grid=(1,), out_shape=outs, in_specs=in_specs, out_...]
    another operation x5 -> x0, other arithmetic: 12.7 us -> none  [spread_local(): stacked = jnp.stack(placed_all, axis=2)]
    dot_general x4 -> x0, matrix products: 11.1 us -> none  [the longest x2 9.75 us: spread_local(): jnp.einsum('emj,fkmjc->fkec', row_onehot, stacked, precision=lax.Precisio...]
    ppermute x16, starting transfers between devices: 24.5 us -> 14.1 us  [the longest x14 8.83 us: swap_lon(): return lax.ppermute(value, 'lon', [(i, i ^ bits) for i in range(RING)])]
    add x11 -> x3, other arithmetic: 5 us -> 0.05 us  [ring_body(): pieces[bits] + swap_lon(pieces[bits + 1], 1)]
    mul x5 -> x0, other arithmetic: 4.53 us -> none  [spread_local(): term = carried * (lat_w[m] * lon_w[o])[None, None]]
    unnamed x4 -> x14, local copies, waits for them, and re-layouts: 0.01 us -> 1.79 us
  transfers between devices with their start and end apart: 16 -> 16, of which waited for: 9 -> 10; matrix products, arithmetic and copies ran while one was open for 0% -> 0% of each run, Pallas kernels for 0% -> 0%
where the time goes in v1:
time: 52.5 us; the launch traced here: 52.2 us
  waiting for transfers between devices  21.9 us (42%)
  Pallas kernels  14.1 us (27%)
  starting transfers between devices  14.1 us (27%)
  local copies, waits for them, and re-layouts  1.89 us (4%)
    ppermute x14, waiting for transfers between devices, swap_lon(): return lax.ppermute(value, 'lon', [(i, i ^ bits) for i in range(RING)])  14.5 us
    pallas_call x4, Pallas kernels, call(): pl.pallas_call(kernel, grid=(1,), out_shape=outs, in_specs=in_specs, out_...  14.1 us
    ppermute x14, starting transfers between devices, swap_lon(): return lax.ppermute(value, 'lon', [(i, i ^ bits) for i in range(RING)])  8.83 us
    ppermute x2, waiting for transfers between devices, swap_lat(): return lax.ppermute(value, 'lat', pairs + [(b, a) for a, b in pairs])  7.44 us
    ppermute x2, starting transfers between devices, swap_lat(): return lax.ppermute(value, 'lat', pairs + [(b, a) for a, b in pairs])  5.3 us
    unnamed x14, local copies, waits for them, and re-layouts  1.79 us
  transfers between devices with their start and end apart: 16, of which 10 were waited for; matrix products, arithmetic and copies ran while one was open for 0% of the time, Pallas kernels for 0%

profile of v1, /device:TPU:8, one launch (start us, length us, event | category | flops | bytes accessed | tf_op | source)
XLA Modules:
  0.0 52.2 jit_solution(11492116765011328360)
XLA Ops:
  0.0 0.0 copy-start.4
  0.0 0.0 copy-start.5
  0.0 0.0 copy-start.1
  0.0 0.0 copy-start.2
  0.0 0.6 %copy-done.4 = s32[2,8,1]{1,2,0:T(1,128)S(1)} copy-done((s32[2,8,1]{1,2,0:T(1,128)S(1)}, s32[2,8,1]{1,2,0:T(1,128)}, u32[]{:S(2)}) %copy-start.4) | copy-done | bytes 88
  0.7 0.1 copy.7.rows
  0.8 0.0 copy-done.5
  0.8 0.1 copy.8.blocks
  0.9 0.1 stack.31.me_ref
  0.9 0.0 copy-done.1
  0.9 0.0 copy-done.2
  0.9 0.0 copy-start
  0.9 0.9 %copy-done = f32[2,32,8,128]{3,2,1,0:T(8,128)S(1)} copy-done((f32[2,32,8,128]{3,2,1,0:T(8,128)S(1)}, f32[2,32,8,128]{3,2,1,0:T(8,128)}, u32[]{:S(2)}) %copy-start) | copy-done | bytes 262168
  1.9 0.0 copy-start.3
  1.9 0.6 %shard_map.64 = (f32[328,128]{1,0:T(8,128)S(1)}, f32[392,128]{1,0:T(8,128)S(1)}, f32[328,128]{1,0:T(8,128)S(1)}, f32[64,128]{1,0:T(8,128)S(1)}) custom-call(s32[5]{0:T(128)S(1)} %stack.31.me_ref, f32[512,128]{1,0:T(8,128)S(1)} %bitcast.13, f32[64,128]{1,0:T(8,128)S(1)} %bitcast.14, f32[64,128]{1,0:T(8,128)S(1)} %bitcast.15, s32[2,8,1]{2,1,0:T(8,128)S(1)} %copy.7.rows, ...), custom_call_target="tpu_custom_call" | custom-call | flops 65536 | bytes 65536 | tf_op jit(solution)/shard_map/pallas_call | solution.py:117
  2.5 1.6 %collective-permute-start.1 = (f32[392,128]{1,0:T(8,128)S(1)}, f32[392,128]{1,0:T(8,128)S(1)}, u32[]{:S(2)}, u32[]{:S(2)}) collective-permute-start(f32[392,128]{1,0:T(8,128)S(1)} %get-tuple-element.21), channel_id=1, source_target_pairs={{0,4},{1,5},{2,6},{3,7},{4,0},{5,1},{6,2},{7,3},{8,12},{9,13},{10,... | collective-permute-start | bytes 602120 | tf_op jit(solution)/shard_map/ppermute | solution.py:385
  4.1 1.4 %collective-permute-start.2 = (f32[328,128]{1,0:T(8,128)S(1)}, f32[328,128]{1,0:T(8,128)S(1)}, u32[]{:S(2)}, u32[]{:S(2)}) collective-permute-start(f32[328,128]{1,0:T(8,128)S(1)} %get-tuple-element.22), channel_id=1, source_target_pairs={{0,6},{1,7},{2,4},{3,5},{4,2},{5,3},{6,0},{7,1},{8,14},{9,15},{10,... | collective-permute-start | bytes 503816 | tf_op jit(solution)/shard_map/ppermute | solution.py:385
  5.5 0.5 %collective-permute-start = (f32[328,128]{1,0:T(8,128)S(1)}, f32[328,128]{1,0:T(8,128)S(1)}, u32[]{:S(2)}, u32[]{:S(2)}) collective-permute-start(f32[328,128]{1,0:T(8,128)S(1)} %get-tuple-element.20.refs_0_.refs_8_.own_tab), channel_id=1, source_target_pairs={{0,2},{1,3},{2,0},{3,1},{4,6},{5,7},{6,4},{7,5},{8,10},{9,11},{10,... | collective-permute-start | bytes 503816 | tf_op jit(solution)/shard_map/ppermute | solution.py:385
  6.1 0.0 collective-permute-start.3
  6.1 6.1 %collective-permute-done.2.refs_3_.refs_11_ = f32[328,128]{1,0:T(8,128)S(1)} collective-permute-done((f32[328,128]{1,0:T(8,128)S(1)}, f32[328,128]{1,0:T(8,128)S(1)}, u32[]{:S(2)}, u32[]{:S(2)}) %collective-permute-start.2) | collective-permute-done | bytes 167968 | tf_op jit(solution)/shard_map/ppermute | solution.py:385
  12.2 0.0 collective-permute-start.6
  12.2 1.2 %collective-permute-done.refs_1_.refs_9_ = f32[328,128]{1,0:T(8,128)S(1)} collective-permute-done((f32[328,128]{1,0:T(8,128)S(1)}, f32[328,128]{1,0:T(8,128)S(1)}, u32[]{:S(2)}, u32[]{:S(2)}) %collective-permute-start) | collective-permute-done | bytes 167968 | tf_op jit(solution)/shard_map/ppermute | solution.py:385
  13.4 0.0 collective-permute-start.4
  13.5 0.0 collective-permute-done.1.refs_2_.refs_10_.ry.y_tab
  13.5 0.5 collective-permute-start.5
  14.0 0.0 copy-done.3
  14.0 0.0 collective-permute-done.3.refs_4_.refs_12_
  14.0 0.0 collective-permute-done.6.refs_7_.refs_15_
  14.0 0.8 %collective-permute-done.4.refs_5_.refs_13_ = f32[328,128]{1,0:T(8,128)S(1)} collective-permute-done((f32[328,128]{1,0:T(8,128)S(1)}, f32[328,128]{1,0:T(8,128)S(1)}, u32[]{:S(2)}, u32[]{:S(2)}) %collective-permute-start.4) | collective-permute-done | bytes 167968 | tf_op jit(solution)/shard_map/ppermute | solution.py:385
  14.9 0.3 collective-permute-done.5.refs_6_.refs_14_
  15.1 7.2 %shard_map.65 = (f32[960,128]{1,0:T(8,128)S(1)}, f32[624,128]{1,0:T(8,128)S(1)}, f32[624,128]{1,0:T(8,128)S(1)}) custom-call(s32[5]{0:T(128)S(1)} %stack.31.me_ref, f32[328,128]{1,0:T(8,128)S(1)} %get-tuple-element.20.refs_0_.refs_8_.own_tab, f32[328,128]{1,0:T(8,128)S(1)} %collective-permute-done.refs_1_.refs_9_, ...), custom_call_target="tpu_custom_call" | custom-call | flops 524288 | bytes 524288 | tf_op jit(solution)/shard_map/pallas_call | solution.py:117
  22.4 0.1 collective-permute-start.7
  22.5 5.2 %collective-permute-start.8 = (f32[624,128]{1,0:T(8,128)S(1)}, f32[624,128]{1,0:T(8,128)S(1)}, u32[]{:S(2)}, u32[]{:S(2)}) collective-permute-start(f32[624,128]{1,0:T(8,128)S(1)} %get-tuple-element.26), channel_id=1, source_target_pairs={{8,16},{16,8},{9,17},{17,9},{10,18},{18,10},{11,19},{19,11},{12,20... | collective-permute-start | bytes 958472 | tf_op jit(solution)/shard_map/ppermute | solution.py:391
  27.7 3.9 %collective-permute-done.7.r1.refs_0_.refs_1_ = f32[624,128]{1,0:T(8,128)S(1)} collective-permute-done((f32[624,128]{1,0:T(8,128)S(1)}, f32[624,128]{1,0:T(8,128)S(1)}, u32[]{:S(2)}, u32[]{:S(2)}) %collective-permute-start.7) | collective-permute-done | bytes 319520 | tf_op jit(solution)/shard_map/ppermute | solution.py:391
  31.6 3.6 %collective-permute-done.8.r2.refs_2_.refs_3_ = f32[624,128]{1,0:T(8,128)S(1)} collective-permute-done((f32[624,128]{1,0:T(8,128)S(1)}, f32[624,128]{1,0:T(8,128)S(1)}, u32[]{:S(2)}, u32[]{:S(2)}) %collective-permute-start.8) | collective-permute-done | bytes 319520 | tf_op jit(solution)/shard_map/ppermute | solution.py:391
  35.1 4.7 %shard_map.66 = (f32[256,128]{1,0:T(8,128)S(1)}, f32[256,128]{1,0:T(8,128)S(1)}, f32[256,128]{1,0:T(8,128)S(1)}, f32[256,128]{1,0:T(8,128)S(1)}, f32[256,128]{1,...) custom-call(s32[5]{0:T(128)S(1)} %stack.31.me_ref, ...), custom_call_target="tpu_custom_call" | custom-call | flops 1048576 | bytes 1048576 | tf_op jit(solution)/shard_map/pallas_call | solution.py:117
  39.9 0.1 collective-permute-start.10
  39.9 0.5 collective-permute-start.12
  40.4 0.1 collective-permute-start.14
  40.5 0.4 collective-permute-start.9
  41.0 0.3 collective-permute-done.10
  41.3 1.1 %collective-permute-start.11 = (f32[256,128]{1,0:T(8,128)S(1)}, f32[256,128]{1,0:T(8,128)S(1)}, u32[]{:S(2)}, u32[]{:S(2)}) collective-permute-start(f32[256,128]{1,0:T(8,128)S(1)} %add.14), channel_id=1, source_target_pairs={{0,2},{1,3},{2,0},{3,1},{4,6},{5,7},{6,4},{7,5},{8,10},{9,11},{10,... | collective-permute-start | bytes 393224 | tf_op jit(solution)/shard_map/ppermute | solution.py:385
  42.4 0.0 collective-permute-done.12
  42.4 1.6 %collective-permute-start.13 = (f32[256,128]{1,0:T(8,128)S(1)}, f32[256,128]{1,0:T(8,128)S(1)}, u32[]{:S(2)}, u32[]{:S(2)}) collective-permute-start(f32[256,128]{1,0:T(8,128)S(1)} %add.15), channel_id=1, source_target_pairs={{0,4},{1,5},{2,6},{3,7},{4,0},{5,1},{6,2},{7,3},{8,12},{9,13},{10,... | collective-permute-start | bytes 393224 | tf_op jit(solution)/shard_map/ppermute | solution.py:385
  44.0 0.0 collective-permute-done.14
  44.1 1.0 %collective-permute-start.15 = (f32[256,128]{1,0:T(8,128)S(1)}, f32[256,128]{1,0:T(8,128)S(1)}, u32[]{:S(2)}, u32[]{:S(2)}) collective-permute-start(f32[256,128]{1,0:T(8,128)S(1)} %add.16), channel_id=1, source_target_pairs={{0,6},{1,7},{2,4},{3,5},{4,2},{5,3},{6,0},{7,1},{8,14},{9,15},{10,... | collective-permute-start | bytes 393224 | tf_op jit(solution)/shard_map/ppermute | solution.py:385
  45.0 0.0 collective-permute-done.9.pair
  45.0 2.5 %collective-permute-done.11.across = f32[256,128]{1,0:T(8,128)S(1)} collective-permute-done((f32[256,128]{1,0:T(8,128)S(1)}, f32[256,128]{1,0:T(8,128)S(1)}, u32[]{:S(2)}, u32[]{:S(2)}) %collective-permute-start.11) | collective-permute-done | bytes 131104 | tf_op jit(solution)/shard_map/ppermute | solution.py:385
  47.5 2.1 %collective-permute-done.13.up = f32[256,128]{1,0:T(8,128)S(1)} collective-permute-done((f32[256,128]{1,0:T(8,128)S(1)}, f32[256,128]{1,0:T(8,128)S(1)}, u32[]{:S(2)}, u32[]{:S(2)}) %collective-permute-start.13) | collective-permute-done | bytes 131104 | tf_op jit(solution)/shard_map/ppermute | solution.py:385
  49.6 1.0 %collective-permute-done.15.diagonal = f32[256,128]{1,0:T(8,128)S(1)} collective-permute-done((f32[256,128]{1,0:T(8,128)S(1)}, f32[256,128]{1,0:T(8,128)S(1)}, u32[]{:S(2)}, u32[]{:S(2)}) %collective-permute-start.15) | collective-permute-done | bytes 131104 | tf_op jit(solution)/shard_map/ppermute | solution.py:385
  50.7 1.5 %shard_map.67 = f32[512,128]{1,0:T(8,128)} custom-call(s32[5]{0:T(128)S(1)} %stack.31.me_ref, f32[256,128]{1,0:T(8,128)S(1)} %get-tuple-element.27.own, f32[256,128]{1,0:T(8,128)S(1)} %collective-permute-done.9.pair, f32[256,128]{1,0:T(8,128)S(1)} %collective-permute-done.11.across, f32[256,128]{1,0:T(8,128)S(1)} %collective-permute-done.13.up, ...), custom_call_target="tpu_custom_call" | custom-call | flops 65536 | bytes 65536 | tf_op jit(solution)/shard_map/pallas_call | solution.py:117
  (4 shorter events, 0.1 us)
Async XLA Ops:
  0.0 0.7 %copy-start.4 = (s32[2,8,1]{1,2,0:T(1,128)S(1)}, s32[2,8,1]{1,2,0:T(1,128)}, u32[]{:S(2)}) copy-start(s32[2,8,1]{1,2,0:T(1,128)} %param.9) | copy-start | bytes 196
  0.0 0.8 %copy-start.5 = (s32[2,8,1]{1,2,0:T(1,128)S(1)}, s32[2,8,1]{1,2,0:T(1,128)}, u32[]{:S(2)}) copy-start(s32[2,8,1]{1,2,0:T(1,128)} %param.10) | copy-start | bytes 196
  0.0 0.9 %copy-start.1 = (f32[2,4,8,128]{3,2,1,0:T(8,128)S(1)}, f32[2,4,8,128]{3,2,1,0:T(8,128)}, u32[]{:S(2)}) copy-start(f32[2,4,8,128]{3,2,1,0:T(8,128)} %param.7) | copy-start | bytes 98308
  0.0 0.9 %copy-start.2 = (f32[2,4,8,128]{3,2,1,0:T(8,128)S(1)}, f32[2,4,8,128]{3,2,1,0:T(8,128)}, u32[]{:S(2)}) copy-start(f32[2,4,8,128]{3,2,1,0:T(8,128)} %param.8) | copy-start | bytes 98308
  0.9 1.0 %copy-start = (f32[2,32,8,128]{3,2,1,0:T(8,128)S(1)}, f32[2,32,8,128]{3,2,1,0:T(8,128)}, u32[]{:S(2)}) copy-start(f32[2,32,8,128]{3,2,1,0:T(8,128)} %param.6) | copy-start | bytes 786436
  1.9 12.1 %copy-start.3 = (f32[2,8,32,32]{3,2,1,0:T(8,128)S(1)}, f32[2,8,32,32]{3,2,1,0:T(8,128)}, u32[]{:S(2)}) copy-start(f32[2,8,32,32]{3,2,1,0:T(8,128)} %param.11) | copy-start | bytes 196612
  2.5 10.9 %collective-permute-start.1 = (f32[392,128]{1,0:T(8,128)S(1)}, f32[392,128]{1,0:T(8,128)S(1)}, u32[]{:S(2)}, u32[]{:S(2)}) collective-permute-start(f32[392,128]{1,0:T(8,128)S(1)} %get-tuple-element.21), channel_id=1, source_target_pairs={{0,4},{1,5},{2,6},{3,7},{4,0},{5,1},{6,2},{7,3},{8,12},{9,13},{10,... | collective-permute-start | bytes 602120 | tf_op jit(solution)/shard_map/ppermute | solution.py:385
  4.1 8.1 %collective-permute-start.2 = (f32[328,128]{1,0:T(8,128)S(1)}, f32[328,128]{1,0:T(8,128)S(1)}, u32[]{:S(2)}, u32[]{:S(2)}) collective-permute-start(f32[328,128]{1,0:T(8,128)S(1)} %get-tuple-element.22), channel_id=1, source_target_pairs={{0,6},{1,7},{2,4},{3,5},{4,2},{5,3},{6,0},{7,1},{8,14},{9,15},{10,... | collective-permute-start | bytes 503816 | tf_op jit(solution)/shard_map/ppermute | solution.py:385
  5.5 7.9 %collective-permute-start = (f32[328,128]{1,0:T(8,128)S(1)}, f32[328,128]{1,0:T(8,128)S(1)}, u32[]{:S(2)}, u32[]{:S(2)}) collective-permute-start(f32[328,128]{1,0:T(8,128)S(1)} %get-tuple-element.20.refs_0_.refs_8_.own_tab), channel_id=1, source_target_pairs={{0,2},{1,3},{2,0},{3,1},{4,6},{5,7},{6,4},{7,5},{8,10},{9,11},{10,... | collective-permute-start | bytes 503816 | tf_op jit(solution)/shard_map/ppermute | solution.py:385
  6.1 7.9 %collective-permute-start.3 = (f32[328,128]{1,0:T(8,128)S(1)}, f32[328,128]{1,0:T(8,128)S(1)}, u32[]{:S(2)}, u32[]{:S(2)}) collective-permute-start(f32[328,128]{1,0:T(8,128)S(1)} %get-tuple-element.20.refs_0_.refs_8_.own_tab), channel_id=1, source_target_pairs={{0,1},{1,0},{2,3},{3,2},{4,5},{5,4},{6,7},{7,6},{8,9},{9,8},{10,11... | collective-permute-start | bytes 503816 | tf_op jit(solution)/shard_map/ppermute | solution.py:385
  12.2 1.8 %collective-permute-start.6 = (f32[328,128]{1,0:T(8,128)S(1)}, f32[328,128]{1,0:T(8,128)S(1)}, u32[]{:S(2)}, u32[]{:S(2)}) collective-permute-start(f32[328,128]{1,0:T(8,128)S(1)} %collective-permute-done.2.refs_3_.refs_11_), channel_id=1, source_target_pairs={{0,1},{1,0},{2,3},{3,2},{4,5},{5,4},{6,7},{7,6},{8,9},{9,8},{10,11... | collective-permute-start | bytes 503816 | tf_op jit(solution)/shard_map/ppermute | solution.py:385
  13.4 1.4 %collective-permute-start.4 = (f32[328,128]{1,0:T(8,128)S(1)}, f32[328,128]{1,0:T(8,128)S(1)}, u32[]{:S(2)}, u32[]{:S(2)}) collective-permute-start(f32[328,128]{1,0:T(8,128)S(1)} %collective-permute-done.refs_1_.refs_9_), channel_id=1, source_target_pairs={{0,1},{1,0},{2,3},{3,2},{4,5},{5,4},{6,7},{7,6},{8,9},{9,8},{10,11... | collective-permute-start | bytes 503816 | tf_op jit(solution)/shard_map/ppermute | solution.py:385
  13.5 1.7 %collective-permute-start.5 = (f32[392,128]{1,0:T(8,128)S(1)}, f32[392,128]{1,0:T(8,128)S(1)}, u32[]{:S(2)}, u32[]{:S(2)}) collective-permute-start(f32[392,128]{1,0:T(8,128)S(1)} %collective-permute-done.1.refs_2_.refs_10_.ry.y_tab), channel_id=1, source_target_pairs={{0,1},{1,0},{2,3},{3,2},{4,5},{5,4},{6,7},{7,6},{8,9},{9,8},{10,11... | collective-permute-start | bytes 602120 | tf_op jit(solution)/shard_map/ppermute | solution.py:385
  22.4 9.2 %collective-permute-start.7 = (f32[624,128]{1,0:T(8,128)S(1)}, f32[624,128]{1,0:T(8,128)S(1)}, u32[]{:S(2)}, u32[]{:S(2)}) collective-permute-start(f32[624,128]{1,0:T(8,128)S(1)} %get-tuple-element.25), channel_id=1, source_target_pairs={{0,8},{16,24},{8,0},{24,16},{1,9},{17,25},{9,1},{25,17},{2,10},{18... | collective-permute-start | bytes 958472 | tf_op jit(solution)/shard_map/ppermute | solution.py:391
  22.5 12.7 %collective-permute-start.8 = (f32[624,128]{1,0:T(8,128)S(1)}, f32[624,128]{1,0:T(8,128)S(1)}, u32[]{:S(2)}, u32[]{:S(2)}) collective-permute-start(f32[624,128]{1,0:T(8,128)S(1)} %get-tuple-element.26), channel_id=1, source_target_pairs={{8,16},{16,8},{9,17},{17,9},{10,18},{18,10},{11,19},{19,11},{12,20... | collective-permute-start | bytes 958472 | tf_op jit(solution)/shard_map/ppermute | solution.py:391
  39.9 1.4 %collective-permute-start.10 = (f32[256,128]{1,0:T(8,128)S(1)}, f32[256,128]{1,0:T(8,128)S(1)}, u32[]{:S(2)}, u32[]{:S(2)}) collective-permute-start(f32[256,128]{1,0:T(8,128)S(1)} %get-tuple-element.30), channel_id=1, source_target_pairs={{0,1},{1,0},{2,3},{3,2},{4,5},{5,4},{6,7},{7,6},{8,9},{9,8},{10,11... | collective-permute-start | bytes 393224 | tf_op jit(solution)/shard_map/ppermute | solution.py:385
  39.9 2.5 %collective-permute-start.12 = (f32[256,128]{1,0:T(8,128)S(1)}, f32[256,128]{1,0:T(8,128)S(1)}, u32[]{:S(2)}, u32[]{:S(2)}) collective-permute-start(f32[256,128]{1,0:T(8,128)S(1)} %get-tuple-element.32), channel_id=1, source_target_pairs={{0,1},{1,0},{2,3},{3,2},{4,5},{5,4},{6,7},{7,6},{8,9},{9,8},{10,11... | collective-permute-start | bytes 393224 | tf_op jit(solution)/shard_map/ppermute | solution.py:385
  40.4 3.6 %collective-permute-start.14 = (f32[256,128]{1,0:T(8,128)S(1)}, f32[256,128]{1,0:T(8,128)S(1)}, u32[]{:S(2)}, u32[]{:S(2)}) collective-permute-start(f32[256,128]{1,0:T(8,128)S(1)} %get-tuple-element.34), channel_id=1, source_target_pairs={{0,1},{1,0},{2,3},{3,2},{4,5},{5,4},{6,7},{7,6},{8,9},{9,8},{10,11... | collective-permute-start | bytes 393224 | tf_op jit(solution)/shard_map/ppermute | solution.py:385
  40.5 4.5 %collective-permute-start.9 = (f32[256,128]{1,0:T(8,128)S(1)}, f32[256,128]{1,0:T(8,128)S(1)}, u32[]{:S(2)}, u32[]{:S(2)}) collective-permute-start(f32[256,128]{1,0:T(8,128)S(1)} %get-tuple-element.28), channel_id=1, source_target_pairs={{0,1},{1,0},{2,3},{3,2},{4,5},{5,4},{6,7},{7,6},{8,9},{9,8},{10,11... | collective-permute-start | bytes 393224 | tf_op jit(solution)/shard_map/ppermute | solution.py:385
  41.3 6.2 %collective-permute-start.11 = (f32[256,128]{1,0:T(8,128)S(1)}, f32[256,128]{1,0:T(8,128)S(1)}, u32[]{:S(2)}, u32[]{:S(2)}) collective-permute-start(f32[256,128]{1,0:T(8,128)S(1)} %add.14), channel_id=1, source_target_pairs={{0,2},{1,3},{2,0},{3,1},{4,6},{5,7},{6,4},{7,5},{8,10},{9,11},{10,... | collective-permute-start | bytes 393224 | tf_op jit(solution)/shard_map/ppermute | solution.py:385
  42.4 7.2 %collective-permute-start.13 = (f32[256,128]{1,0:T(8,128)S(1)}, f32[256,128]{1,0:T(8,128)S(1)}, u32[]{:S(2)}, u32[]{:S(2)}) collective-permute-start(f32[256,128]{1,0:T(8,128)S(1)} %add.15), channel_id=1, source_target_pairs={{0,4},{1,5},{2,6},{3,7},{4,0},{5,1},{6,2},{7,3},{8,12},{9,13},{10,... | collective-permute-start | bytes 393224 | tf_op jit(solution)/shard_map/ppermute | solution.py:385
  44.1 6.6 %collective-permute-start.15 = (f32[256,128]{1,0:T(8,128)S(1)}, f32[256,128]{1,0:T(8,128)S(1)}, u32[]{:S(2)}, u32[]{:S(2)}) collective-permute-start(f32[256,128]{1,0:T(8,128)S(1)} %add.16), channel_id=1, source_target_pairs={{0,6},{1,7},{2,4},{3,5},{4,2},{5,3},{6,0},{7,1},{8,14},{9,15},{10,... | collective-permute-start | bytes 393224 | tf_op jit(solution)/shard_map/ppermute | solution.py:385

commit v2 on v1

--- a/solution.py
+++ b/solution.py
@@ -135,26 +135,16 @@
     return [turned[o][0:4] * turned[o][4 + o : 5 + o] for o in range(NODES)]
 
 
-def lanes_in(low, high):
-    lane = lax.broadcasted_iota(jnp.int32, (4, 128), 1)
-    return ((lane >= low) & (lane < high)).astype(jnp.float32)
-
-
-def main_products(prods):
-    return [
-        (0, prods[0] * lanes_in(0, 127)),
-        (1, prods[1]),
-        (2, prods[2] * lanes_in(1, 128)),
-        (3, prods[3] * lanes_in(2, 128)),
-    ]
-
-
-def left_products(prods):
-    return [(0, prods[0] * lanes_in(127, 128))]
-
-
-def right_products(prods):
-    return [(2, prods[2] * lanes_in(0, 1)), (3, prods[3] * lanes_in(0, 2))]
+def lane_masks():
+    lane = lax.broadcasted_iota(jnp.int32, (8, 128), 1)
+    node = lax.broadcasted_iota(jnp.int32, (8, 128), 0)
+    first = jnp.maximum(node - 1, 0)
+    stay = (lane >= first) & (lane < jnp.where(node == 0, 127, 128))
+    return [value.astype(jnp.float32) for value in (stay, (node == 0) & (lane == 127), (node >= 2) & (lane < first))]
+
+
+def masked(prods, mask, nodes):
+    return [(o, prods[o] * mask[o : o + 1]) for o in nodes]
 
 
 def add_terms(sources, terms, target, first):
@@ -201,39 +191,28 @@
 
 def first_spread(levels, me_ref, *refs):
     messages, tables = refs[0:8], refs[8:16]
-    w0, v1, part, m1, m2, acc = refs[16:]
+    w0, v1, part, m1, m2, acc, masks = refs[16:]
     per_row = levels + 8
     me, lat_start, even = me_ref[0], me_ref[1], me_ref[2]
     slot = me // 4
     acc[...] = jnp.zeros_like(acc)
+    stay, back, on = lane_masks()
+    for n, mask in enumerate((stay, back, jnp.zeros_like(stay), on)):
+        masks[n] = mask
     for message, table in zip(messages, tables):
 
         def row(i, _, message=message, table=table):
             first = table[i, 0].astype(jnp.int32) - lat_start + LOW
             tau = table[i, 1].astype(jnp.int32)
             delta = (tau - me) & 3
+            block = (tau + jnp.where(delta == 1, 7, jnp.where(delta == 3, 1, 0))) & 7
             base = pl.multiple_of(i * per_row, 8)
-
-            def work(which, block):
-                prods = which(products(message[pl.ds(base + levels, 8), :]))
-                sources = [rolled(message[pl.ds(base + kk, 8), :]) for kk in range(0, levels, 8)]
-                add_terms(sources, prods, acc, (block // 4) * 15 + first)
-
-            @pl.when(delta == 0)
-            def _():
-                work(main_products, tau)
-
-            @pl.when(delta == 1)
-            def _():
-                work(left_products, (tau + 7) & 7)
-
-            @pl.when(delta == 3)
-            def _():
-                work(right_products, (tau + 1) & 7)
-
+            terms = masked(products(message[pl.ds(base + levels, 8), :]), masks[delta], range(NODES))
+            sources = [rolled(message[pl.ds(base + kk, 8), :]) for kk in range(0, levels, 8)]
+            add_terms(sources, terms, acc, (block // 4) * 15 + first)
             return 0
 
-        lax.fori_loop(0, 8, row, 0)
+        lax.fori_loop(0, 8, row, 0, unroll=True)
     part[...] = acc[...].reshape(part.shape)
 
     def write(out, part_row, count, row):
@@ -331,14 +310,16 @@
     for q in range(8):
         acc[q * 22 + 7 : q * 22 + 15] = jnp.zeros((8, levels, 128), jnp.float32)
 
+    stay, back, on = lane_masks()
+
     def spread(n, h, row, tau):
         tau = tau.astype(jnp.int32)
         first = row.astype(jnp.int32) - lat_start + 7
         prods = products(weights[h * 15 + n])
         sources = [rolled(state[h * 15 + n, kk : kk + 8, :]) for kk in range(0, levels, 8)]
-        add_terms(sources, main_products(prods), acc, (tau ^ me) * 22 + first)
-        add_terms(sources, left_products(prods), acc, (((tau + 7) & 7) ^ me) * 22 + first)
-        add_terms(sources, right_products(prods), acc, (((tau + 1) & 7) ^ me) * 22 + first)
+        add_terms(sources, masked(prods, stay, range(NODES)), acc, (tau ^ me) * 22 + first)
+        add_terms(sources, masked(prods, back, (0,)), acc, (((tau + 7) & 7) ^ me) * 22 + first)
+        add_terms(sources, masked(prods, on, (2, 3)), acc, (((tau + 1) & 7) ^ me) * 22 + first)
 
     for h in range(2):
 
@@ -355,15 +336,15 @@
             spread(i + 12, h, *(jnp.where(is_even, r1_tabs[h][i, c], r2_tabs[h][i, c]) for c in (2, 3)))
             return 0
 
-        lax.fori_loop(0, 8, own_row, 0)
+        lax.fori_loop(0, 8, own_row, 0, unroll=True)
 
         @pl.when(at_start == 0)
         def _():
-            lax.fori_loop(0, 4, before_row, 0)
+            lax.fori_loop(0, 4, before_row, 0, unroll=True)
 
         @pl.when(at_end == 0)
         def _():
-            lax.fori_loop(0, 3, after_row, 0)
+            lax.fori_loop(0, 3, after_row, 0, unroll=True)
 
     for q in range(8):
         outs[q][...] = acc[q * 22 + 7 : q * 22 + 15].reshape(8 * levels, 128)
@@ -426,7 +407,7 @@
         + [vmem(value.shape) for value in messages]
         + [smem_tile(table_tile)] * 8
         + [vmem((64, 128)), vmem((8, levels, levels), 3)],
-        [pltpu.VMEM((30, levels, 128), jnp.float32)],
+        [pltpu.VMEM((30, levels, 128), jnp.float32), pltpu.VMEM((4, 8, 128), jnp.float32)],
         8 * size,
         info,
         *messages,

time: 52.5 us -> 46.5 us (0.89)
  Pallas kernels: 14.1 us -> 7.63 us
  waiting for transfers between devices: 21.9 us -> 22.5 us
    pallas_call x4, Pallas kernels: 14.1 us -> 7.63 us  [call(): pl.pallas_call(kernel, grid=(1,), out_shape=outs, in_specs=in_specs, out_...]
  transfers between devices with their start and end apart: 16 -> 16, of which waited for: 10 -> 9; matrix products, arithmetic and copies ran while one was open for 0% -> 0% of each run, Pallas kernels for 0% -> 0%
where the time goes in v2:
time: 46.5 us; the launch traced here: 46.1 us
  waiting for transfers between devices  22.5 us (48%)
  starting transfers between devices  14 us (30%)
  Pallas kernels  7.63 us (16%)
  local copies, waits for them, and re-layouts  1.89 us (4%)
    ppermute x14, waiting for transfers between devices, swap_lon(): return lax.ppermute(value, 'lon', [(i, i ^ bits) for i in range(RING)])  14.8 us
    ppermute x14, starting transfers between devices, swap_lon(): return lax.ppermute(value, 'lon', [(i, i ^ bits) for i in range(RING)])  8.83 us
    ppermute x2, waiting for transfers between devices, swap_lat(): return lax.ppermute(value, 'lat', pairs + [(b, a) for a, b in pairs])  7.68 us
    pallas_call x4, Pallas kernels, call(): pl.pallas_call(kernel, grid=(1,), out_shape=outs, in_specs=in_specs, out_...  7.63 us
    ppermute x2, starting transfers between devices, swap_lat(): return lax.ppermute(value, 'lat', pairs + [(b, a) for a, b in pairs])  5.12 us
    unnamed x14, local copies, waits for them, and re-layouts  1.79 us
  transfers between devices with their start and end apart: 16, of which 9 were waited for; matrix products, arithmetic and copies ran while one was open for 0% of the time, Pallas kernels for 0%

profile of v2, /device:TPU:8, one launch (start us, length us, event | category | flops | bytes accessed | tf_op | source)
XLA Modules:
  0.0 46.1 jit_solution(3806747100702428011)
XLA Ops:
  0.0 0.0 copy-start.4
  0.0 0.0 copy-start.5
  0.0 0.0 copy-start.1
  0.0 0.0 copy-start.2
  0.0 0.6 %copy-done.4 = s32[2,8,1]{1,2,0:T(1,128)S(1)} copy-done((s32[2,8,1]{1,2,0:T(1,128)S(1)}, s32[2,8,1]{1,2,0:T(1,128)}, u32[]{:S(2)}) %copy-start.4) | copy-done | bytes 88
  0.7 0.1 copy.7.rows
  0.8 0.0 copy-done.5
  0.8 0.1 copy.8.blocks
  0.9 0.1 stack.31.me_ref
  0.9 0.0 copy-done.1
  0.9 0.0 copy-done.2
  0.9 0.0 copy-start
  0.9 0.9 %copy-done = f32[2,32,8,128]{3,2,1,0:T(8,128)S(1)} copy-done((f32[2,32,8,128]{3,2,1,0:T(8,128)S(1)}, f32[2,32,8,128]{3,2,1,0:T(8,128)}, u32[]{:S(2)}) %copy-start) | copy-done | bytes 262168
  1.9 0.0 copy-start.3
  1.9 0.6 %shard_map.64 = (f32[328,128]{1,0:T(8,128)S(1)}, f32[392,128]{1,0:T(8,128)S(1)}, f32[328,128]{1,0:T(8,128)S(1)}, f32[64,128]{1,0:T(8,128)S(1)}) custom-call(s32[5]{0:T(128)S(1)} %stack.31.me_ref, f32[512,128]{1,0:T(8,128)S(1)} %bitcast.13, f32[64,128]{1,0:T(8,128)S(1)} %bitcast.14, f32[64,128]{1,0:T(8,128)S(1)} %bitcast.15, s32[2,8,1]{2,1,0:T(8,128)S(1)} %copy.7.rows, ...), custom_call_target="tpu_custom_call" | custom-call | flops 65536 | bytes 65536 | tf_op jit(solution)/shard_map/pallas_call | solution.py:117
  2.5 1.6 %collective-permute-start.1 = (f32[392,128]{1,0:T(8,128)S(1)}, f32[392,128]{1,0:T(8,128)S(1)}, u32[]{:S(2)}, u32[]{:S(2)}) collective-permute-start(f32[392,128]{1,0:T(8,128)S(1)} %get-tuple-element.21), channel_id=1, source_target_pairs={{0,4},{1,5},{2,6},{3,7},{4,0},{5,1},{6,2},{7,3},{8,12},{9,13},{10,... | collective-permute-start | bytes 602120 | tf_op jit(solution)/shard_map/ppermute | solution.py:366
  4.1 1.4 %collective-permute-start.2 = (f32[328,128]{1,0:T(8,128)S(1)}, f32[328,128]{1,0:T(8,128)S(1)}, u32[]{:S(2)}, u32[]{:S(2)}) collective-permute-start(f32[328,128]{1,0:T(8,128)S(1)} %get-tuple-element.22), channel_id=1, source_target_pairs={{0,6},{1,7},{2,4},{3,5},{4,2},{5,3},{6,0},{7,1},{8,14},{9,15},{10,... | collective-permute-start | bytes 503816 | tf_op jit(solution)/shard_map/ppermute | solution.py:366
  5.5 0.5 %collective-permute-start = (f32[328,128]{1,0:T(8,128)S(1)}, f32[328,128]{1,0:T(8,128)S(1)}, u32[]{:S(2)}, u32[]{:S(2)}) collective-permute-start(f32[328,128]{1,0:T(8,128)S(1)} %get-tuple-element.20.refs_0_.refs_8_.own_tab), channel_id=1, source_target_pairs={{0,2},{1,3},{2,0},{3,1},{4,6},{5,7},{6,4},{7,5},{8,10},{9,11},{10,... | collective-permute-start | bytes 503816 | tf_op jit(solution)/shard_map/ppermute | solution.py:366
  6.1 0.0 collective-permute-start.3
  6.1 6.1 %collective-permute-done.2.refs_3_.refs_11_ = f32[328,128]{1,0:T(8,128)S(1)} collective-permute-done((f32[328,128]{1,0:T(8,128)S(1)}, f32[328,128]{1,0:T(8,128)S(1)}, u32[]{:S(2)}, u32[]{:S(2)}) %collective-permute-start.2) | collective-permute-done | bytes 167968 | tf_op jit(solution)/shard_map/ppermute | solution.py:366
  12.2 0.0 collective-permute-start.6
  12.2 1.2 %collective-permute-done.refs_1_.refs_9_ = f32[328,128]{1,0:T(8,128)S(1)} collective-permute-done((f32[328,128]{1,0:T(8,128)S(1)}, f32[328,128]{1,0:T(8,128)S(1)}, u32[]{:S(2)}, u32[]{:S(2)}) %collective-permute-start) | collective-permute-done | bytes 167968 | tf_op jit(solution)/shard_map/ppermute | solution.py:366
  13.4 0.0 collective-permute-start.4
  13.5 0.0 collective-permute-done.1.refs_2_.refs_10_.ry.y_tab
  13.5 0.5 %collective-permute-start.5 = (f32[392,128]{1,0:T(8,128)S(1)}, f32[392,128]{1,0:T(8,128)S(1)}, u32[]{:S(2)}, u32[]{:S(2)}) collective-permute-start(f32[392,128]{1,0:T(8,128)S(1)} %collective-permute-done.1.refs_2_.refs_10_.ry.y_tab), channel_id=1, source_target_pairs={{0,1},{1,0},{2,3},{3,2},{4,5},{5,4},{6,7},{7,6},{8,9},{9,8},{10,11... | collective-permute-start | bytes 602120 | tf_op jit(solution)/shard_map/ppermute | solution.py:366
  14.0 0.0 copy-done.3
  14.0 0.0 collective-permute-done.3.refs_4_.refs_12_
  14.0 0.0 collective-permute-done.6.refs_7_.refs_15_
  14.0 0.8 %collective-permute-done.4.refs_5_.refs_13_ = f32[328,128]{1,0:T(8,128)S(1)} collective-permute-done((f32[328,128]{1,0:T(8,128)S(1)}, f32[328,128]{1,0:T(8,128)S(1)}, u32[]{:S(2)}, u32[]{:S(2)}) %collective-permute-start.4) | collective-permute-done | bytes 167968 | tf_op jit(solution)/shard_map/ppermute | solution.py:366
  14.9 0.3 collective-permute-done.5.refs_6_.refs_14_
  15.1 2.7 %shard_map.65 = (f32[960,128]{1,0:T(8,128)S(1)}, f32[624,128]{1,0:T(8,128)S(1)}, f32[624,128]{1,0:T(8,128)S(1)}) custom-call(s32[5]{0:T(128)S(1)} %stack.31.me_ref, f32[328,128]{1,0:T(8,128)S(1)} %get-tuple-element.20.refs_0_.refs_8_.own_tab, f32[328,128]{1,0:T(8,128)S(1)} %collective-permute-done.refs_1_.refs_9_, ...), custom_call_target="tpu_custom_call" | custom-call | flops 524288 | bytes 524288 | tf_op jit(solution)/shard_map/pallas_call | solution.py:117
  17.8 0.4 collective-permute-start.7
  18.2 4.7 %collective-permute-start.8 = (f32[624,128]{1,0:T(8,128)S(1)}, f32[624,128]{1,0:T(8,128)S(1)}, u32[]{:S(2)}, u32[]{:S(2)}) collective-permute-start(f32[624,128]{1,0:T(8,128)S(1)} %get-tuple-element.26), channel_id=1, source_target_pairs={{8,16},{16,8},{9,17},{17,9},{10,18},{18,10},{11,19},{19,11},{12,20... | collective-permute-start | bytes 958472 | tf_op jit(solution)/shard_map/ppermute | solution.py:372
  23.0 4.7 %collective-permute-done.7.r1.refs_0_.refs_1_ = f32[624,128]{1,0:T(8,128)S(1)} collective-permute-done((f32[624,128]{1,0:T(8,128)S(1)}, f32[624,128]{1,0:T(8,128)S(1)}, u32[]{:S(2)}, u32[]{:S(2)}) %collective-permute-start.7) | collective-permute-done | bytes 319520 | tf_op jit(solution)/shard_map/ppermute | solution.py:372
  27.6 3.0 %collective-permute-done.8.r2.refs_2_.refs_3_ = f32[624,128]{1,0:T(8,128)S(1)} collective-permute-done((f32[624,128]{1,0:T(8,128)S(1)}, f32[624,128]{1,0:T(8,128)S(1)}, u32[]{:S(2)}, u32[]{:S(2)}) %collective-permute-start.8) | collective-permute-done | bytes 319520 | tf_op jit(solution)/shard_map/ppermute | solution.py:372
  30.6 2.8 %shard_map.66 = (f32[256,128]{1,0:T(8,128)S(1)}, f32[256,128]{1,0:T(8,128)S(1)}, f32[256,128]{1,0:T(8,128)S(1)}, f32[256,128]{1,0:T(8,128)S(1)}, f32[256,128]{1,...) custom-call(s32[5]{0:T(128)S(1)} %stack.31.me_ref, ...), custom_call_target="tpu_custom_call" | custom-call | flops 1048576 | bytes 1048576 | tf_op jit(solution)/shard_map/pallas_call | solution.py:117
  33.5 0.1 collective-permute-start.10
  33.6 0.5 %collective-permute-start.12 = (f32[256,128]{1,0:T(8,128)S(1)}, f32[256,128]{1,0:T(8,128)S(1)}, u32[]{:S(2)}, u32[]{:S(2)}) collective-permute-start(f32[256,128]{1,0:T(8,128)S(1)} %get-tuple-element.32), channel_id=1, source_target_pairs={{0,1},{1,0},{2,3},{3,2},{4,5},{5,4},{6,7},{7,6},{8,9},{9,8},{10,11... | collective-permute-start | bytes 393224 | tf_op jit(solution)/shard_map/ppermute | solution.py:366
  34.1 0.1 collective-permute-start.14
  34.1 0.4 collective-permute-start.9
  34.6 0.3 collective-permute-done.10
  34.9 1.6 %collective-permute-start.11 = (f32[256,128]{1,0:T(8,128)S(1)}, f32[256,128]{1,0:T(8,128)S(1)}, u32[]{:S(2)}, u32[]{:S(2)}) collective-permute-start(f32[256,128]{1,0:T(8,128)S(1)} %add.14), channel_id=1, source_target_pairs={{0,2},{1,3},{2,0},{3,1},{4,6},{5,7},{6,4},{7,5},{8,10},{9,11},{10,... | collective-permute-start | bytes 393224 | tf_op jit(solution)/shard_map/ppermute | solution.py:366
  36.5 0.0 collective-permute-done.12
  36.5 1.6 %collective-permute-start.13 = (f32[256,128]{1,0:T(8,128)S(1)}, f32[256,128]{1,0:T(8,128)S(1)}, u32[]{:S(2)}, u32[]{:S(2)}) collective-permute-start(f32[256,128]{1,0:T(8,128)S(1)} %add.15), channel_id=1, source_target_pairs={{0,4},{1,5},{2,6},{3,7},{4,0},{5,1},{6,2},{7,3},{8,12},{9,13},{10,... | collective-permute-start | bytes 393224 | tf_op jit(solution)/shard_map/ppermute | solution.py:366
  38.1 0.0 collective-permute-done.14
  38.1 0.6 %collective-permute-start.15 = (f32[256,128]{1,0:T(8,128)S(1)}, f32[256,128]{1,0:T(8,128)S(1)}, u32[]{:S(2)}, u32[]{:S(2)}) collective-permute-start(f32[256,128]{1,0:T(8,128)S(1)} %add.16), channel_id=1, source_target_pairs={{0,6},{1,7},{2,4},{3,5},{4,2},{5,3},{6,0},{7,1},{8,14},{9,15},{10,... | collective-permute-start | bytes 393224 | tf_op jit(solution)/shard_map/ppermute | solution.py:366
  38.6 0.0 collective-permute-done.9.pair
  38.7 2.1 %collective-permute-done.11.across = f32[256,128]{1,0:T(8,128)S(1)} collective-permute-done((f32[256,128]{1,0:T(8,128)S(1)}, f32[256,128]{1,0:T(8,128)S(1)}, u32[]{:S(2)}, u32[]{:S(2)}) %collective-permute-start.11) | collective-permute-done | bytes 131104 | tf_op jit(solution)/shard_map/ppermute | solution.py:366
  40.7 3.9 %collective-permute-done.13.up = f32[256,128]{1,0:T(8,128)S(1)} collective-permute-done((f32[256,128]{1,0:T(8,128)S(1)}, f32[256,128]{1,0:T(8,128)S(1)}, u32[]{:S(2)}, u32[]{:S(2)}) %collective-permute-start.13) | collective-permute-done | bytes 131104 | tf_op jit(solution)/shard_map/ppermute | solution.py:366
  44.6 0.0 collective-permute-done.15.diagonal
  44.6 1.5 %shard_map.67 = f32[512,128]{1,0:T(8,128)} custom-call(s32[5]{0:T(128)S(1)} %stack.31.me_ref, f32[256,128]{1,0:T(8,128)S(1)} %get-tuple-element.27.own, f32[256,128]{1,0:T(8,128)S(1)} %collective-permute-done.9.pair, f32[256,128]{1,0:T(8,128)S(1)} %collective-permute-done.11.across, f32[256,128]{1,0:T(8,128)S(1)} %collective-permute-done.13.up, ...), custom_call_target="tpu_custom_call" | custom-call | flops 65536 | bytes 65536 | tf_op jit(solution)/shard_map/pallas_call | solution.py:117
  (4 shorter events, 0.1 us)
Async XLA Ops:
  0.0 0.7 %copy-start.4 = (s32[2,8,1]{1,2,0:T(1,128)S(1)}, s32[2,8,1]{1,2,0:T(1,128)}, u32[]{:S(2)}) copy-start(s32[2,8,1]{1,2,0:T(1,128)} %param.9) | copy-start | bytes 196
  0.0 0.8 %copy-start.5 = (s32[2,8,1]{1,2,0:T(1,128)S(1)}, s32[2,8,1]{1,2,0:T(1,128)}, u32[]{:S(2)}) copy-start(s32[2,8,1]{1,2,0:T(1,128)} %param.10) | copy-start | bytes 196
  0.0 0.9 %copy-start.1 = (f32[2,4,8,128]{3,2,1,0:T(8,128)S(1)}, f32[2,4,8,128]{3,2,1,0:T(8,128)}, u32[]{:S(2)}) copy-start(f32[2,4,8,128]{3,2,1,0:T(8,128)} %param.7) | copy-start | bytes 98308
  0.0 0.9 %copy-start.2 = (f32[2,4,8,128]{3,2,1,0:T(8,128)S(1)}, f32[2,4,8,128]{3,2,1,0:T(8,128)}, u32[]{:S(2)}) copy-start(f32[2,4,8,128]{3,2,1,0:T(8,128)} %param.8) | copy-start | bytes 98308
  0.9 1.0 %copy-start = (f32[2,32,8,128]{3,2,1,0:T(8,128)S(1)}, f32[2,32,8,128]{3,2,1,0:T(8,128)}, u32[]{:S(2)}) copy-start(f32[2,32,8,128]{3,2,1,0:T(8,128)} %param.6) | copy-start | bytes 786436
  1.9 12.1 %copy-start.3 = (f32[2,8,32,32]{3,2,1,0:T(8,128)S(1)}, f32[2,8,32,32]{3,2,1,0:T(8,128)}, u32[]{:S(2)}) copy-start(f32[2,8,32,32]{3,2,1,0:T(8,128)} %param.11) | copy-start | bytes 196612
  2.5 10.9 %collective-permute-start.1 = (f32[392,128]{1,0:T(8,128)S(1)}, f32[392,128]{1,0:T(8,128)S(1)}, u32[]{:S(2)}, u32[]{:S(2)}) collective-permute-start(f32[392,128]{1,0:T(8,128)S(1)} %get-tuple-element.21), channel_id=1, source_target_pairs={{0,4},{1,5},{2,6},{3,7},{4,0},{5,1},{6,2},{7,3},{8,12},{9,13},{10,... | collective-permute-start | bytes 602120 | tf_op jit(solution)/shard_map/ppermute | solution.py:366
  4.1 8.1 %collective-permute-start.2 = (f32[328,128]{1,0:T(8,128)S(1)}, f32[328,128]{1,0:T(8,128)S(1)}, u32[]{:S(2)}, u32[]{:S(2)}) collective-permute-start(f32[328,128]{1,0:T(8,128)S(1)} %get-tuple-element.22), channel_id=1, source_target_pairs={{0,6},{1,7},{2,4},{3,5},{4,2},{5,3},{6,0},{7,1},{8,14},{9,15},{10,... | collective-permute-start | bytes 503816 | tf_op jit(solution)/shard_map/ppermute | solution.py:366
  5.5 7.9 %collective-permute-start = (f32[328,128]{1,0:T(8,128)S(1)}, f32[328,128]{1,0:T(8,128)S(1)}, u32[]{:S(2)}, u32[]{:S(2)}) collective-permute-start(f32[328,128]{1,0:T(8,128)S(1)} %get-tuple-element.20.refs_0_.refs_8_.own_tab), channel_id=1, source_target_pairs={{0,2},{1,3},{2,0},{3,1},{4,6},{5,7},{6,4},{7,5},{8,10},{9,11},{10,... | collective-permute-start | bytes 503816 | tf_op jit(solution)/shard_map/ppermute | solution.py:366
  6.1 7.9 %collective-permute-start.3 = (f32[328,128]{1,0:T(8,128)S(1)}, f32[328,128]{1,0:T(8,128)S(1)}, u32[]{:S(2)}, u32[]{:S(2)}) collective-permute-start(f32[328,128]{1,0:T(8,128)S(1)} %get-tuple-element.20.refs_0_.refs_8_.own_tab), channel_id=1, source_target_pairs={{0,1},{1,0},{2,3},{3,2},{4,5},{5,4},{6,7},{7,6},{8,9},{9,8},{10,11... | collective-permute-start | bytes 503816 | tf_op jit(solution)/shard_map/ppermute | solution.py:366
  12.2 1.8 %collective-permute-start.6 = (f32[328,128]{1,0:T(8,128)S(1)}, f32[328,128]{1,0:T(8,128)S(1)}, u32[]{:S(2)}, u32[]{:S(2)}) collective-permute-start(f32[328,128]{1,0:T(8,128)S(1)} %collective-permute-done.2.refs_3_.refs_11_), channel_id=1, source_target_pairs={{0,1},{1,0},{2,3},{3,2},{4,5},{5,4},{6,7},{7,6},{8,9},{9,8},{10,11... | collective-permute-start | bytes 503816 | tf_op jit(solution)/shard_map/ppermute | solution.py:366
  13.4 1.4 %collective-permute-start.4 = (f32[328,128]{1,0:T(8,128)S(1)}, f32[328,128]{1,0:T(8,128)S(1)}, u32[]{:S(2)}, u32[]{:S(2)}) collective-permute-start(f32[328,128]{1,0:T(8,128)S(1)} %collective-permute-done.refs_1_.refs_9_), channel_id=1, source_target_pairs={{0,1},{1,0},{2,3},{3,2},{4,5},{5,4},{6,7},{7,6},{8,9},{9,8},{10,11... | collective-permute-start | bytes 503816 | tf_op jit(solution)/shard_map/ppermute | solution.py:366
  13.5 1.7 %collective-permute-start.5 = (f32[392,128]{1,0:T(8,128)S(1)}, f32[392,128]{1,0:T(8,128)S(1)}, u32[]{:S(2)}, u32[]{:S(2)}) collective-permute-start(f32[392,128]{1,0:T(8,128)S(1)} %collective-permute-done.1.refs_2_.refs_10_.ry.y_tab), channel_id=1, source_target_pairs={{0,1},{1,0},{2,3},{3,2},{4,5},{5,4},{6,7},{7,6},{8,9},{9,8},{10,11... | collective-permute-start | bytes 602120 | tf_op jit(solution)/shard_map/ppermute | solution.py:366
  17.8 9.8 %collective-permute-start.7 = (f32[624,128]{1,0:T(8,128)S(1)}, f32[624,128]{1,0:T(8,128)S(1)}, u32[]{:S(2)}, u32[]{:S(2)}) collective-permute-start(f32[624,128]{1,0:T(8,128)S(1)} %get-tuple-element.25), channel_id=1, source_target_pairs={{0,8},{16,24},{8,0},{24,16},{1,9},{17,25},{9,1},{25,17},{2,10},{18... | collective-permute-start | bytes 958472 | tf_op jit(solution)/shard_map/ppermute | solution.py:372
  18.2 12.4 %collective-permute-start.8 = (f32[624,128]{1,0:T(8,128)S(1)}, f32[624,128]{1,0:T(8,128)S(1)}, u32[]{:S(2)}, u32[]{:S(2)}) collective-permute-start(f32[624,128]{1,0:T(8,128)S(1)} %get-tuple-element.26), channel_id=1, source_target_pairs={{8,16},{16,8},{9,17},{17,9},{10,18},{18,10},{11,19},{19,11},{12,20... | collective-permute-start | bytes 958472 | tf_op jit(solution)/shard_map/ppermute | solution.py:372
  33.5 1.4 %collective-permute-start.10 = (f32[256,128]{1,0:T(8,128)S(1)}, f32[256,128]{1,0:T(8,128)S(1)}, u32[]{:S(2)}, u32[]{:S(2)}) collective-permute-start(f32[256,128]{1,0:T(8,128)S(1)} %get-tuple-element.30), channel_id=1, source_target_pairs={{0,1},{1,0},{2,3},{3,2},{4,5},{5,4},{6,7},{7,6},{8,9},{9,8},{10,11... | collective-permute-start | bytes 393224 | tf_op jit(solution)/shard_map/ppermute | solution.py:366
  33.6 2.9 %collective-permute-start.12 = (f32[256,128]{1,0:T(8,128)S(1)}, f32[256,128]{1,0:T(8,128)S(1)}, u32[]{:S(2)}, u32[]{:S(2)}) collective-permute-start(f32[256,128]{1,0:T(8,128)S(1)} %get-tuple-element.32), channel_id=1, source_target_pairs={{0,1},{1,0},{2,3},{3,2},{4,5},{5,4},{6,7},{7,6},{8,9},{9,8},{10,11... | collective-permute-start | bytes 393224 | tf_op jit(solution)/shard_map/ppermute | solution.py:366
  34.1 4.0 %collective-permute-start.14 = (f32[256,128]{1,0:T(8,128)S(1)}, f32[256,128]{1,0:T(8,128)S(1)}, u32[]{:S(2)}, u32[]{:S(2)}) collective-permute-start(f32[256,128]{1,0:T(8,128)S(1)} %get-tuple-element.34), channel_id=1, source_target_pairs={{0,1},{1,0},{2,3},{3,2},{4,5},{5,4},{6,7},{7,6},{8,9},{9,8},{10,11... | collective-permute-start | bytes 393224 | tf_op jit(solution)/shard_map/ppermute | solution.py:366
  34.1 4.5 %collective-permute-start.9 = (f32[256,128]{1,0:T(8,128)S(1)}, f32[256,128]{1,0:T(8,128)S(1)}, u32[]{:S(2)}, u32[]{:S(2)}) collective-permute-start(f32[256,128]{1,0:T(8,128)S(1)} %get-tuple-element.28), channel_id=1, source_target_pairs={{0,1},{1,0},{2,3},{3,2},{4,5},{5,4},{6,7},{7,6},{8,9},{9,8},{10,11... | collective-permute-start | bytes 393224 | tf_op jit(solution)/shard_map/ppermute | solution.py:366
  34.9 5.8 %collective-permute-start.11 = (f32[256,128]{1,0:T(8,128)S(1)}, f32[256,128]{1,0:T(8,128)S(1)}, u32[]{:S(2)}, u32[]{:S(2)}) collective-permute-start(f32[256,128]{1,0:T(8,128)S(1)} %add.14), channel_id=1, source_target_pairs={{0,2},{1,3},{2,0},{3,1},{4,6},{5,7},{6,4},{7,5},{8,10},{9,11},{10,... | collective-permute-start | bytes 393224 | tf_op jit(solution)/shard_map/ppermute | solution.py:366
  36.5 8.1 %collective-permute-start.13 = (f32[256,128]{1,0:T(8,128)S(1)}, f32[256,128]{1,0:T(8,128)S(1)}, u32[]{:S(2)}, u32[]{:S(2)}) collective-permute-start(f32[256,128]{1,0:T(8,128)S(1)} %add.15), channel_id=1, source_target_pairs={{0,4},{1,5},{2,6},{3,7},{4,0},{5,1},{6,2},{7,3},{8,12},{9,13},{10,... | collective-permute-start | bytes 393224 | tf_op jit(solution)/shard_map/ppermute | solution.py:366
  38.1 6.5 %collective-permute-start.15 = (f32[256,128]{1,0:T(8,128)S(1)}, f32[256,128]{1,0:T(8,128)S(1)}, u32[]{:S(2)}, u32[]{:S(2)}) collective-permute-start(f32[256,128]{1,0:T(8,128)S(1)} %add.16), channel_id=1, source_target_pairs={{0,6},{1,7},{2,4},{3,5},{4,2},{5,3},{6,0},{7,1},{8,14},{9,15},{10,... | collective-permute-start | bytes 393224 | tf_op jit(solution)/shard_map/ppermute | solution.py:366

commit v3 on v2

v3 whole, which is shorter than its diff:
```python
import functools

import jax
import jax.numpy as jnp
from jax import lax
from jax.experimental import pallas as pl
from jax.experimental.pallas import tpu as pltpu
from jax.sharding import PartitionSpec as P

R = 2
H = 2
NODES = 4
RING = 8
LOW = H + 1
HIGH = H + 2
VMEM_LIMIT = 48 * 1024 * 1024


def shifted(array, axis, by):
    size = lax.axis_size(axis)
    return lax.ppermute(array, axis, [(i, (i + by) % size) for i in range(size)])


def from_behind(value, axis, steps):
    count = lax.axis_size(axis)
    leading, last = (max(0, -steps), min(count, count - steps))
    return lax.ppermute(value, axis, [(source, source + steps) for source in range(leading, last)])


def spread_local(carried, lat_w, lon_w, row_table, block_table, lat_start, own_block, cycle_size):
    fields, levels, lat_rows, points = carried.shape
    ext_rows = lat_rows + LOW + HIGH
    block_count = 2 * R + 3
    width = block_count * points
    rel_row = row_table - lat_start + LOW
    rel_block = (block_table - own_block + R) % cycle_size
    target = lax.broadcasted_iota(jnp.int32, (ext_rows, 4, lat_rows), 0)
    node = lax.broadcasted_iota(jnp.int32, (ext_rows, 4, lat_rows), 1)
    row_onehot = (target == rel_row[None, None, :] + node).astype(jnp.float32)
    placed_all = []
    for m in range(4):
        lon_row = jnp.zeros((fields, levels, lat_rows, points + 3), jnp.float32)
        for o in range(4):
            term = carried * (lat_w[m] * lon_w[o])[None, None]
            lon_row = lon_row + jnp.pad(term, ((0, 0), (0, 0), (0, 0), (o, 3 - o)))
        placed = jnp.zeros((fields, levels, lat_rows, width), jnp.float32)
        for d in range(2 * R + 1):
            left = (d + 1) * points - 1
            right = width - left - (points + 3)
            selected = (rel_block == d).astype(jnp.float32)[None, None, :, None]
            placed = placed + selected * jnp.pad(lon_row, ((0, 0), (0, 0), (0, 0), (left, right)))
        placed_all.append(placed)
    stacked = jnp.stack(placed_all, axis=2)
    return jnp.einsum("emj,fkmjc->fkec", row_onehot, stacked, precision=lax.Precision.HIGHEST)


def cycle_total(buffer, points):
    block_count = 2 * R + 3
    pieces = [buffer[..., q * points : (q + 1) * points] for q in range(block_count)]
    summed = pieces[R + 1]
    for q in range(block_count):
        if q != R + 1:
            summed = summed + shifted(pieces[q], "lon", q - R - 1)
    return summed


def fold_rims(buffer, lat_rows):
    upper = buffer[:, :, :LOW]
    lower = buffer[:, :, LOW + lat_rows :]
    interior = buffer[:, :, LOW : LOW + lat_rows]
    from_after = from_behind(upper, "lat", -1)
    from_before = from_behind(lower, "lat", 1)
    interior = interior + jnp.pad(from_after, ((0, 0), (0, 0), (lat_rows - LOW, 0), (0, 0)))
    interior = interior + jnp.pad(from_before, ((0, 0), (0, 0), (0, lat_rows - HIGH), (0, 0)))
    return interior


def plain_body(adjoint_in, lat_weights, lon_weights, depart_rows, depart_blocks, vertical_inverse):
    fields, levels, lat_rows, points = adjoint_in.shape
    cycle_size = lax.axis_size("lon")
    own_block = lax.axis_index("lon")
    lat_start = lax.axis_index("lat") * lat_rows
    carried = adjoint_in
    for s in (1, 0):
        partial_value = spread_local(
            carried,
            lat_weights[s],
            lon_weights[s],
            depart_rows[s, :, 0],
            depart_blocks[s, :, 0],
            lat_start,
            own_block,
            cycle_size,
        )
        gathered_rows = cycle_total(partial_value, points)
        interior = fold_rims(gathered_rows, lat_rows)
        carried = jnp.einsum(
            "imk,fmip->fkip", vertical_inverse[s], interior, precision=lax.Precision.HIGHEST
        )
    return carried


def vmem(shape, rank=2):
    return pl.BlockSpec(shape, lambda i: (0,) * rank, memory_space=pltpu.VMEM)


def smem_tile(tile):
    return pl.BlockSpec((8, 128), lambda i: (tile, 0), memory_space=pltpu.SMEM)


def smem_whole(size):
    return pl.BlockSpec((size,), lambda i: (0,), memory_space=pltpu.SMEM)


def call(kernel, out_rows, in_specs, scratch, cost, *args):
    sizes = [n if isinstance(n, tuple) else (n, jnp.float32) for n in out_rows]
    outs = [jax.ShapeDtypeStruct((n, 128), dtype) for n, dtype in sizes]
    return pl.pallas_call(
        kernel,
        grid=(1,),
        out_shape=outs,
        in_specs=in_specs,
        out_specs=[vmem((n, 128)) for n, _ in sizes],
        scratch_shapes=scratch,
        compiler_params=pltpu.CompilerParams(vmem_limit_bytes=VMEM_LIMIT),
        cost_estimate=pl.CostEstimate(flops=cost, bytes_accessed=cost, transcendentals=0),
    )(*args)


def rolled(value):
    return [pltpu.roll(value, 127, 1), value, pltpu.roll(value, 1, 1), pltpu.roll(value, 2, 1)]


def products(weights):
    turned = rolled(weights)
    return [turned[o][0:4] * turned[o][4 + o : 5 + o] for o in range(NODES)]


def lane_masks():
    lane = lax.broadcasted_iota(jnp.int32, (8, 128), 1)
    node = lax.broadcasted_iota(jnp.int32, (8, 128), 0)
    first = jnp.maximum(node - 1, 0)
    stay = (lane >= first) & (lane < jnp.where(node == 0, 127, 128))
    return [value.astype(jnp.float32) for value in (stay, (node == 0) & (lane == 127), (node >= 2) & (lane < first))]


def masked(prods, mask, nodes):
    return [(o, prods[o] * mask[o : o + 1]) for o in nodes]


def add_terms(sources, terms, target, first):
    for m in range(NODES):
        for kk, turned in enumerate(sources):
            total = None
            for o, weight in terms:
                term = turned[o] * weight[m : m + 1]
                total = term if total is None else total + term
            target[first + m, 8 * kk : 8 * kk + 8, :] += total


def assemble(levels, rows, blocks, adj, lat_w, lon_w, v, own, other, e1, e2, *scratch):
    tables, lat0, lon0, v1, sems = scratch
    field, even = lax.axis_index("lon") // 4, 1 - lax.axis_index("lat") % 2
    per_field = 8 * levels
    sem = iter(range(16))

    def copy(source, target):
        return pltpu.make_async_copy(source, target, sems.at[next(sem)])

    small = [copy(rows, tables.at[0]), copy(blocks, tables.at[1])]
    small += [copy(lat_w.at[pl.ds(0, 32)], lat0), copy(lon_w.at[pl.ds(0, 32)], lon0), copy(v.at[1], v1)]
    large = []
    for out, which in ((own, field), (other, 1 - field)):
        large.append(copy(adj.at[pl.ds(pl.multiple_of(which * per_field, per_field), per_field)], out.at[pl.ds(0, per_field)]))
        large.append(copy(lat_w.at[pl.ds(32, 32)], out.at[pl.ds(per_field, 32)]))
        large.append(copy(lon_w.at[pl.ds(32, 32)], out.at[pl.ds(per_field + 32, 32)]))
    for each in small + large:
        each.start()
    for each in small:
        each.wait()
    table = jnp.concatenate([tables[0], tables[1], tables[0], tables[1]], axis=0).astype(jnp.float32)
    for out, first in ((own, per_field + 64), (other, per_field + 64), (e1, 32 + levels), (e2, 32 + levels)):
        out[first : first + 8, 0:8] = table
    low = jnp.concatenate([v1[j] for j in range(4)], axis=1)
    high = jnp.concatenate([v1[j + 4] for j in range(4)], axis=1)
    for out, takes_high in ((e1, even == 1), (e2, even == 0)):
        first = jnp.where(takes_high, 4, 0)
        for i in range(4):
            out[8 * i : 8 * i + 4, :] = lat0[pl.ds(first + i, 4, stride=8), :]
            out[8 * i + 4 : 8 * i + 8, :] = lon0[pl.ds(first + i, 4, stride=8), :]
        out[32 : 32 + levels, :] = jnp.where(takes_high, high, low)
    for each in large:
        each.wait()


def rim_data(levels, me_ref, own_tile, lat_w, lon_w, e1, e2, v, after_this, pack, matrices1, matrices0):
    even = me_ref[2] == 1
    for i in range(8):
        pack[32 + 8 * i : 36 + 8 * i, :] = lat_w[pl.ds(i, 4, stride=8), :]
        pack[36 + 8 * i : 40 + 8 * i, :] = lon_w[pl.ds(i, 4, stride=8), :]
    pack[0:32, :] = jnp.where(even, e2[0:32, :], e1[0:32, :])
    pack[96:120, :] = jnp.where(even, e1[0:24, :], e2[0:24, :])
    tab = slice(32 + levels, 40 + levels)
    before = pltpu.roll(jnp.where(even, e2[tab, :], e1[tab, :]), 124, 1)
    after = pltpu.roll(jnp.where(even, e1[tab, :], e2[tab, :]), 12, 1)
    lane = lax.broadcasted_iota(jnp.int32, (8, 128), 1)
    pack[120:128, :] = jnp.where(lane < 4, before, jnp.where(lane < 12, pltpu.roll(own_tile[...], 4, 1), after))

    def turned(four):
        value = four.T
        high = value.astype(jnp.bfloat16).astype(jnp.float32)
        low = value - high
        return jnp.concatenate([high, low, high, low], axis=1).astype(jnp.bfloat16)

    def four(s, first):
        return jnp.concatenate([v[s, first + j] for j in range(4)], axis=1)

    at_v = slice(32, 32 + levels)
    matrices1[0 : 4 * levels, :] = turned(jnp.where(even, e2[at_v, :], e1[at_v, :]))
    matrices1[4 * levels : 8 * levels, :] = turned(four(1, 0))
    matrices1[8 * levels : 12 * levels, :] = turned(four(1, 4))
    matrices1[12 * levels : 16 * levels, :] = turned(jnp.where(even, e1[at_v, :], e2[at_v, :]))
    matrices0[0 : 4 * levels, :] = turned(four(0, 0))
    matrices0[4 * levels : 8 * levels, :] = turned(four(0, 4))


def first_spread(levels, me_ref, *refs):
    messages, tables = refs[0:8], refs[8:16]
    part, m1, m2, acc, masks = refs[16:]
    per_field = 8 * levels
    me, lat_start, even = me_ref[0], me_ref[1], me_ref[2]
    acc[...] = jnp.zeros_like(acc)
    stay, back, on = lane_masks()
    for n, mask in enumerate((stay, back, jnp.zeros_like(stay), on)):
        masks[n] = mask
    for message, table in zip(messages, tables):

        def row(i, _, message=message, table=table):
            first = table[1, i].astype(jnp.int32) - lat_start + LOW
            tau = table[3, i].astype(jnp.int32)
            delta = (tau - me) & 3
            block = (tau + jnp.where(delta == 1, 7, jnp.where(delta == 3, 1, 0))) & 7
            weights = message[pl.ds(per_field + i, 8, stride=8), :]
            terms = masked(products(weights), masks[delta], range(NODES))
            sources = [rolled(message[pl.ds(8 * kk + i, 8, stride=8), :]) for kk in range(0, levels, 8)]
            add_terms(sources, terms, acc, (block // 4) * 15 + first)
            return 0

        lax.fori_loop(0, 8, row, 0, unroll=True)
    part[...] = acc[...].reshape(part.shape)

    def write(out, part_row, count):
        for h in range(2):
            out[h * 8 * levels : (h * 8 + count) * levels, :] = acc[
                h * 15 + part_row : h * 15 + part_row + count
            ].reshape(count * levels, 128)

    @pl.when(even == 1)
    def _():
        write(m1, 7, 8)
        write(m2, 0, 6)

    @pl.when(even == 0)
    def _():
        write(m2, 7, 8)
        write(m1, 0, 6)


def vertical(matrix, column):
    high = column.astype(jnp.bfloat16)
    low = (column - high.astype(jnp.float32)).astype(jnp.bfloat16)
    return jnp.dot(matrix, jnp.concatenate([high, high, low, low], axis=0), preferred_element_type=jnp.float32)


def second_spread(levels, me_ref, part, r1, r2, own_pack, y_pack, matrices, own_tab, y_tab, *refs):
    outs, (state, acc) = refs[0:8], refs[8:]
    me, lat_start, even, at_start, at_end = (me_ref[n] for n in range(5))
    slot = me // 4
    is_even = even == 1
    for n in range(15):
        halves = []
        for h in range(2):
            own = slice((h * 15 + n - 1) * levels, (h * 15 + n) * levels)
            b = slice((h * 8 + n) * levels, (h * 8 + n + 1) * levels)
            a = slice((h * 8 + n - 9) * levels, (h * 8 + n - 8) * levels)
            if n == 0:
                value = jnp.where(is_even, r2[b, :], r1[b, :])
            elif n < 8:
                value = part[own, :] + jnp.where(is_even, r2[b, :], r1[b, :])
            elif n == 8:
                value = part[own, :]
            else:
                value = part[own, :] + jnp.where(is_even, r1[a, :], r2[a, :])
            halves.append(value)
        result = vertical(matrices[n * levels : (n + 1) * levels, :], jnp.concatenate(halves, axis=1))
        state[n] = result[:, :128]
        state[15 + n] = result[:, 128:]
    for q in range(8):
        acc[q * 22 + 7 : q * 22 + 15] = jnp.zeros((8, levels, 128), jnp.float32)
    stay, back, on = lane_masks()

    def spread(n, h):
        mine = slot == h
        tau = jnp.where(mine, own_tab[2, n], y_tab[2, n]).astype(jnp.int32)
        first = jnp.where(mine, own_tab[0, n], y_tab[0, n]).astype(jnp.int32) - lat_start + 7
        at = slice(8 * n, 8 * n + 8)
        prods = products(jnp.where(mine, own_pack[at, :], y_pack[at, :]))
        sources = [rolled(state[h * 15 + n, kk : kk + 8, :]) for kk in range(0, levels, 8)]
        add_terms(sources, masked(prods, stay, range(NODES)), acc, (tau ^ me) * 22 + first)
        add_terms(sources, masked(prods, back, (0,)), acc, (((tau + 7) & 7) ^ me) * 22 + first)
        add_terms(sources, masked(prods, on, (2, 3)), acc, (((tau + 1) & 7) ^ me) * 22 + first)

    for n in range(4, 12):
        for h in range(2):
            spread(n, h)

    @pl.when(at_start == 0)
    def _():
        for n in range(4):
            for h in range(2):
                spread(n, h)

    @pl.when(at_end == 0)
    def _():
        for n in range(12, 15):
            for h in range(2):
                spread(n, h)

    for q in range(8):
        outs[q][...] = acc[q * 22 + 7 : q * 22 + 15].reshape(8 * levels, 128)


def finish(levels, me_ref, own, pair, across, up, diagonal, matrices, out):
    field = me_ref[0] // 4
    for i in range(8):
        rows = slice(i * levels, (i + 1) * levels)
        mine = own[rows, :] + pair[rows, :] + across[rows, :]
        other = up[rows, :] + diagonal[rows, :]
        result = vertical(matrices[rows, :], jnp.concatenate([mine, other], axis=1))
        for kk in range(0, levels, 8):
            out[pl.ds((field * levels + kk) * 8 + i, 8, stride=8), :] = result[kk : kk + 8, :128]
            out[pl.ds(((1 - field) * levels + kk) * 8 + i, 8, stride=8), :] = result[kk : kk + 8, 128:]


def swap_lon(value, bits):
    return lax.ppermute(value, "lon", [(i, i ^ bits) for i in range(RING)])


def swap_lat(value, odd):
    count = lax.axis_size("lat")
    pairs = [(i, i + 1) for i in range(odd, count - 1, 2)]
    return lax.ppermute(value, "lat", pairs + [(b, a) for a, b in pairs])


def ring_body(adjoint_in, lat_weights, lon_weights, depart_rows, depart_blocks, vertical_inverse):
    fields, levels, lat_rows, points = adjoint_in.shape
    me = lax.axis_index("lon")
    band = lax.axis_index("lat")
    count = lax.axis_size("lat")
    info = jnp.stack([me, band * lat_rows, 1 - band % 2, band == 0, band == count - 1]).astype(jnp.int32)
    per_field = 8 * levels
    size = adjoint_in.size
    message = per_field + 64 + 8
    side = 32 + levels + 8
    adjoint = adjoint_in.reshape(-1, points)
    lat_w, lon_w = lat_weights.reshape(-1, points), lon_weights.reshape(-1, points)
    sizes = [message, message, side, side]
    arguments = depart_rows[:, :, 0], depart_blocks[:, :, 0], adjoint, lat_w, lon_w, vertical_inverse
    own, other, e1, e2 = pl.pallas_call(
        functools.partial(assemble, levels),
        out_shape=[pltpu.VMEM((n, points), jnp.float32) for n in sizes],
        in_specs=[pl.BlockSpec(memory_space=pltpu.HBM)] * 6,
        out_specs=[pl.BlockSpec(memory_space=pltpu.VMEM)] * 4,
        scratch_shapes=[
            pltpu.VMEM((2, 2, 8), jnp.int32),
            pltpu.VMEM((32, points), jnp.float32),
            pltpu.VMEM((32, points), jnp.float32),
            pltpu.VMEM((8, levels, levels), jnp.float32),
            pltpu.SemaphoreType.DMA((16,)),
        ],
        compiler_params=pltpu.CompilerParams(vmem_limit_bytes=VMEM_LIMIT),
    )(*(pltpu.with_memory_space_constraint(value, pltpu.HBM) for value in arguments))
    far = {6: swap_lon(other, 6), 4: swap_lon(other, 4), 2: swap_lon(own, 2)}
    tile = pl.BlockSpec((8, 128), lambda i: (message // 8 - 1, 0), memory_space=pltpu.VMEM)
    e1, e2 = swap_lat(e1, 0), swap_lat(e2, 1)
    far[2], e1, e2 = lax.optimization_barrier((far[2], e1, e2))
    messages = [own, far[2], far[4], far[6]]
    messages = messages + [swap_lon(value, 1) for value in messages]
    part, m1, m2 = call(
        functools.partial(first_spread, levels),
        [30 * levels, 16 * levels, 16 * levels],
        [smem_whole(5)] + [vmem((message, 128))] * 8 + [smem_tile(message // 8 - 1)] * 8,
        [pltpu.VMEM((30, levels, 128), jnp.float32), pltpu.VMEM((4, 8, 128), jnp.float32)],
        8 * size,
        info,
        *messages,
        *messages,
    )
    r1, r2 = swap_lat(m1, 0), swap_lat(m2, 1)
    pack, matrices1, matrices0 = call(
        functools.partial(rim_data, levels),
        [128, (16 * levels, jnp.bfloat16), (8 * levels, jnp.bfloat16)],
        [smem_whole(5), tile, vmem((64, 128)), vmem((64, 128)), vmem((side, 128)), vmem((side, 128))]
        + [vmem(vertical_inverse.shape, 4), vmem((8, 128))],
        [],
        size,
        info,
        own,
        lat_w,
        lon_w,
        e1,
        e2,
        vertical_inverse,
        part,
    )
    y_pack = swap_lon(pack, 4)
    pieces = call(
        functools.partial(second_spread, levels),
        [8 * levels] * 8,
        [smem_whole(5), vmem((30 * levels, 128))]
        + [vmem((16 * levels, 128))] * 2
        + [vmem((128, 128))] * 2
        + [vmem((16 * levels, 128))]
        + [smem_tile(15)] * 2,
        [pltpu.VMEM((30, levels, 128), jnp.float32), pltpu.VMEM((8 * 22, levels, 128), jnp.float32)],
        16 * size,
        info,
        part,
        r1,
        r2,
        pack,
        y_pack,
        matrices1,
        pack,
        y_pack,
    )
    received = {}
    for bits in (6, 4, 2):
        received[bits] = swap_lon(pieces[bits] + swap_lon(pieces[bits + 1], 1), bits)
    pair = swap_lon(pieces[1], 1)
    (out,) = call(
        functools.partial(finish, levels),
        [fields * levels * 8],
        [smem_whole(5)] + [vmem((8 * levels, 128))] * 6,
        [],
        size,
        info,
        pieces[0],
        pair,
        received[2],
        received[4],
        received[6],
        matrices0,
    )
    return out.reshape(adjoint_in.shape)


def solution(mesh):
    specs = (
        P(None, None, "lat", "lon"),
        P(None, None, "lat", "lon"),
        P(None, None, "lat", "lon"),
        P(None, "lat", "lon"),
        P(None, "lat", "lon"),
        P(None, "lat", None, None),
    )

    def whole(*args):
        fields, levels, rows, points = args[0].shape
        lat, lon = mesh.shape["lat"], mesh.shape["lon"]
        ring = (fields, lon, rows // lat, points // lon) == (2, RING, 8, 128) and levels % 8 == 0 and levels * 4 == 128
        body = ring_body if ring else plain_body
        return jax.shard_map(body, mesh=mesh, in_specs=specs, out_specs=specs[0], check_vma=False)(*args)

    return whole
```

time: 46.5 us -> 44.5 us (0.957)
  waiting for transfers between devices: 22.5 us -> 15.1 us
  starting transfers between devices: 14 us -> 19.6 us
  local copies, waits for them, and re-layouts: 1.89 us -> 0.09 us
  Pallas kernels: 7.63 us -> 9.15 us
    ppermute x2 -> x4, waiting for transfers between devices: 7.68 us -> 2.43 us  [swap_lat(): return lax.ppermute(value, 'lat', pairs + [(b, a) for a, b in pairs])]
    ppermute x2 -> x4, starting transfers between devices: 5.12 us -> 10.2 us  [swap_lat(): return lax.ppermute(value, 'lat', pairs + [(b, a) for a, b in pairs])]
    ppermute x14 -> x15, waiting for transfers between devices: 14.8 us -> 12.7 us  [swap_lon(): return lax.ppermute(value, 'lon', [(i, i ^ bits) for i in range(RING)])]
    unnamed x14 -> x6, local copies, waits for them, and re-layouts: 1.79 us -> 0.01 us
    pallas_call x0 -> x1, Pallas kernels: none -> 1.27 us  [ring_body(): pl.pallas_call(functools.partial(assemble, levels), out_shape=[pltpu.VMEM...]
    ppermute x14 -> x15, starting transfers between devices: 8.83 us -> 9.47 us  [swap_lon(): return lax.ppermute(value, 'lon', [(i, i ^ bits) for i in range(RING)])]
  transfers between devices with their start and end apart: 16 -> 19, of which waited for: 9 -> 10; matrix products, arithmetic and copies ran while one was open for 0% -> 0% of each run, Pallas kernels for 0% -> 3%
where the time goes in v3:
time: 44.5 us; the launch traced here: 44.2 us
  starting transfers between devices  19.6 us (44%)
  waiting for transfers between devices  15.1 us (34%)
  Pallas kernels  9.15 us (21%)
    ppermute x15, waiting for transfers between devices, swap_lon(): return lax.ppermute(value, 'lon', [(i, i ^ bits) for i in range(RING)])  12.7 us
    ppermute x4, starting transfers between devices, swap_lat(): return lax.ppermute(value, 'lat', pairs + [(b, a) for a, b in pairs])  10.2 us
    ppermute x15, starting transfers between devices, swap_lon(): return lax.ppermute(value, 'lon', [(i, i ^ bits) for i in range(RING)])  9.47 us
    pallas_call x4, Pallas kernels, call(): pl.pallas_call(kernel, grid=(1,), out_shape=outs, in_specs=in_specs, out_...  7.88 us
    ppermute x4, waiting for transfers between devices, swap_lat(): return lax.ppermute(value, 'lat', pairs + [(b, a) for a, b in pairs])  2.43 us
    pallas_call x1, Pallas kernels, ring_body(): pl.pallas_call(functools.partial(assemble, levels), out_shape=[pltpu.VMEM...  1.27 us
  transfers between devices with their start and end apart: 19, of which 10 were waited for; matrix products, arithmetic and copies ran while one was open for 0% of the time, Pallas kernels for 3%

profile of v3, /device:TPU:8, one launch (start us, length us, event | category | flops | bytes accessed | tf_op | source)
XLA Modules:
  0.0 44.2 jit_solution(1484986805567116022)
XLA Ops:
  0.0 1.3 %shard_map.64 = (f32[328,128]{1,0:T(8,128)S(1)}, f32[328,128]{1,0:T(8,128)S(1)}, f32[72,128]{1,0:T(8,128)S(1)}, f32[72,128]{1,0:T(8,128)S(1)}) custom-call(s32[2,8]{1,0:T(2,128)} %bitcast.16, s32[2,8]{1,0:T(2,128)} %bitcast.17, f32[512,128]{1,0:T(8,128)} %bitcast.15, f32[64,128]{1,0:T(8,128)} %bitcast.11, f32[64,128]{1,0:T(8,128)} %bitcast.13, ...), custom_call_target="tpu_custom_call" | custom-call | tf_op jit(solution)/shard_map/pallas_call | solution.py:369
  1.3 1.6 %collective-permute-start = (f32[328,128]{1,0:T(8,128)S(1)}, f32[328,128]{1,0:T(8,128)S(1)}, u32[]{:S(2)}, u32[]{:S(2)}) collective-permute-start(f32[328,128]{1,0:T(8,128)S(1)} %get-tuple-element.26.refs_0_.refs_8_.own_tile), channel_id=1, source_target_pairs={{0,2},{1,3},{2,0},{3,1},{4,6},{5,7},{6,4},{7,5},{8,10},{9,11},{10,... | collective-permute-start | bytes 503816 | tf_op jit(solution)/shard_map/ppermute | solution.py:346
  2.8 1.5 %collective-permute-start.4 = (f32[328,128]{1,0:T(8,128)S(1)}, f32[328,128]{1,0:T(8,128)S(1)}, u32[]{:S(2)}, u32[]{:S(2)}) collective-permute-start(f32[328,128]{1,0:T(8,128)S(1)} %get-tuple-element.30), channel_id=1, source_target_pairs={{0,6},{1,7},{2,4},{3,5},{4,2},{5,3},{6,0},{7,1},{8,14},{9,15},{10,... | collective-permute-start | bytes 503816 | tf_op jit(solution)/shard_map/ppermute | solution.py:346
  4.3 0.5 %collective-permute-start.3 = (f32[328,128]{1,0:T(8,128)S(1)}, f32[328,128]{1,0:T(8,128)S(1)}, u32[]{:S(2)}, u32[]{:S(2)}) collective-permute-start(f32[328,128]{1,0:T(8,128)S(1)} %get-tuple-element.30), channel_id=1, source_target_pairs={{0,4},{1,5},{2,6},{3,7},{4,0},{5,1},{6,2},{7,3},{8,12},{9,13},{10,... | collective-permute-start | bytes 503816 | tf_op jit(solution)/shard_map/ppermute | solution.py:346
  4.8 0.0 collective-permute-start.1
  4.8 5.0 %collective-permute-start.2 = (f32[72,128]{1,0:T(8,128)S(1)}, f32[72,128]{1,0:T(8,128)S(1)}, u32[]{:S(2)}, u32[]{:S(2)}) collective-permute-start(f32[72,128]{1,0:T(8,128)S(1)} %get-tuple-element.28), channel_id=1, source_target_pairs={{8,16},{16,8},{9,17},{17,9},{10,18},{18,10},{11,19},{19,11},{12,20... | collective-permute-start | bytes 110600 | tf_op jit(solution)/shard_map/ppermute | solution.py:352
  9.9 0.0 collective-permute-done.1.e1
  9.9 0.1 collective-permute-start.5
  10.0 1.8 %collective-permute-done.2.e2 = f32[72,128]{1,0:T(8,128)S(1)} collective-permute-done((f32[72,128]{1,0:T(8,128)S(1)}, f32[72,128]{1,0:T(8,128)S(1)}, u32[]{:S(2)}, u32[]{:S(2)}) %collective-permute-start.2) | collective-permute-done | bytes 36896 | tf_op jit(solution)/shard_map/ppermute | solution.py:352
  11.8 0.0 collective-permute-done.refs_1_.refs_9_
  11.8 0.2 collective-permute-done.4.refs_3_.refs_11_
  12.0 0.0 collective-permute-start.8
  12.0 1.4 %collective-permute-done.3.refs_2_.refs_10_ = f32[328,128]{1,0:T(8,128)S(1)} collective-permute-done((f32[328,128]{1,0:T(8,128)S(1)}, f32[328,128]{1,0:T(8,128)S(1)}, u32[]{:S(2)}, u32[]{:S(2)}) %collective-permute-start.3) | collective-permute-done | bytes 167968 | tf_op jit(solution)/shard_map/ppermute | solution.py:346
  13.4 0.0 collective-permute-start.7
  13.4 0.5 %collective-permute-start.6 = (f32[328,128]{1,0:T(8,128)S(1)}, f32[328,128]{1,0:T(8,128)S(1)}, u32[]{:S(2)}, u32[]{:S(2)}) collective-permute-start(f32[328,128]{1,0:T(8,128)S(1)} %collective-permute-done.refs_1_.refs_9_), channel_id=1, source_target_pairs={{0,1},{1,0},{2,3},{3,2},{4,5},{5,4},{6,7},{7,6},{8,9},{9,8},{10,11... | collective-permute-start | bytes 503816 | tf_op jit(solution)/shard_map/ppermute | solution.py:346
  13.9 0.1 stack.31.me_ref
  14.0 0.0 copy-start
  14.0 0.0 copy-start.1
  14.0 0.0 copy-start.2
  14.0 0.0 collective-permute-done.5.refs_4_.refs_12_
  14.0 0.0 collective-permute-done.8.refs_7_.refs_15_
  14.0 0.8 %collective-permute-done.7.refs_6_.refs_14_ = f32[328,128]{1,0:T(8,128)S(1)} collective-permute-done((f32[328,128]{1,0:T(8,128)S(1)}, f32[328,128]{1,0:T(8,128)S(1)}, u32[]{:S(2)}, u32[]{:S(2)}) %collective-permute-start.7) | collective-permute-done | bytes 167968 | tf_op jit(solution)/shard_map/ppermute | solution.py:346
  14.8 0.2 collective-permute-done.6.refs_5_.refs_13_
  15.0 2.6 %shard_map.65 = (f32[960,128]{1,0:T(8,128)S(1)}, f32[512,128]{1,0:T(8,128)S(1)}, f32[512,128]{1,0:T(8,128)S(1)}) custom-call(s32[5]{0:T(128)S(1)} %stack.31.me_ref, f32[328,128]{1,0:T(8,128)S(1)} %get-tuple-element.26.refs_0_.refs_8_.own_tile, f32[328,128]{1,0:T(8,128)S(1)} %collective-permute-done.refs_1_.refs_9_, ...), custom_call_target="tpu_custom_call" | custom-call | flops 524288 | bytes 524288 | tf_op jit(solution)/shard_map/pallas_call | solution.py:118
  17.7 0.5 %collective-permute-start.9 = (f32[512,128]{1,0:T(8,128)S(1)}, f32[512,128]{1,0:T(8,128)S(1)}, u32[]{:S(2)}, u32[]{:S(2)}) collective-permute-start(f32[512,128]{1,0:T(8,128)S(1)} %get-tuple-element.32), channel_id=1, source_target_pairs={{0,8},{16,24},{8,0},{24,16},{1,9},{17,25},{9,1},{25,17},{2,10},{18... | collective-permute-start | bytes 786440 | tf_op jit(solution)/shard_map/ppermute | solution.py:352
  18.2 4.6 %collective-permute-start.10 = (f32[512,128]{1,0:T(8,128)S(1)}, f32[512,128]{1,0:T(8,128)S(1)}, u32[]{:S(2)}, u32[]{:S(2)}) collective-permute-start(f32[512,128]{1,0:T(8,128)S(1)} %get-tuple-element.33), channel_id=1, source_target_pairs={{8,16},{16,8},{9,17},{17,9},{10,18},{18,10},{11,19},{19,11},{12,20... | collective-permute-start | bytes 786440 | tf_op jit(solution)/shard_map/ppermute | solution.py:352
  22.8 0.0 copy-done
  22.8 0.0 copy-done.1
  22.8 0.0 copy-done.2
  22.8 1.5 %shard_map.66 = (f32[128,128]{1,0:T(8,128)S(1)}, bf16[512,128]{1,0:T(8,128)(2,1)S(1)}, bf16[256,128]{1,0:T(8,128)(2,1)S(1)}) custom-call(s32[5]{0:T(128)S(1)} %stack.31.me_ref, f32[328,128]{1,0:T(8,128)S(1)} %get-tuple-element.26.refs_0_.refs_8_.own_tile, f32[64,128]{1,0:T(8,128)S(1)} %bitcast.12, f32[64,128]{1,0:T(8,128)S(1)} %bitcast.14, ...), custom_call_target="tpu_custom_call" | custom-call | flops 65536 | bytes 65536 | tf_op jit(solution)/shard_map/pallas_call | solution.py:118
  24.3 0.6 %collective-permute-start.11 = (f32[128,128]{1,0:T(8,128)S(1)}, f32[128,128]{1,0:T(8,128)S(1)}, u32[]{:S(2)}, u32[]{:S(2)}) collective-permute-start(f32[128,128]{1,0:T(8,128)S(1)} %get-tuple-element.36.own_pack.own_tab), channel_id=1, source_target_pairs={{0,4},{1,5},{2,6},{3,7},{4,0},{5,1},{6,2},{7,3},{8,12},{9,13},{10,... | collective-permute-start | bytes 196616 | tf_op jit(solution)/shard_map/ppermute | solution.py:346
  24.9 3.8 %collective-permute-done.11.y_pack.y_tab = f32[128,128]{1,0:T(8,128)S(1)} collective-permute-done((f32[128,128]{1,0:T(8,128)S(1)}, f32[128,128]{1,0:T(8,128)S(1)}, u32[]{:S(2)}, u32[]{:S(2)}) %collective-permute-start.11) | collective-permute-done | bytes 65568 | tf_op jit(solution)/shard_map/ppermute | solution.py:346
  28.6 0.0 collective-permute-done.9.r1
  28.6 0.6 %collective-permute-done.10.r2 = f32[512,128]{1,0:T(8,128)S(1)} collective-permute-done((f32[512,128]{1,0:T(8,128)S(1)}, f32[512,128]{1,0:T(8,128)S(1)}, u32[]{:S(2)}, u32[]{:S(2)}) %collective-permute-start.10) | collective-permute-done | bytes 262176 | tf_op jit(solution)/shard_map/ppermute | solution.py:352
  29.2 2.3 %shard_map.67 = (f32[256,128]{1,0:T(8,128)S(1)}, f32[256,128]{1,0:T(8,128)S(1)}, f32[256,128]{1,0:T(8,128)S(1)}, f32[256,128]{1,0:T(8,128)S(1)}, f32[256,128]{1,...) custom-call(s32[5]{0:T(128)S(1)} %stack.31.me_ref, ...), custom_call_target="tpu_custom_call" | custom-call | flops 1048576 | bytes 1048576 | tf_op jit(solution)/shard_map/pallas_call | solution.py:118
  31.6 0.1 collective-permute-start.13
  31.6 0.5 %collective-permute-start.15 = (f32[256,128]{1,0:T(8,128)S(1)}, f32[256,128]{1,0:T(8,128)S(1)}, u32[]{:S(2)}, u32[]{:S(2)}) collective-permute-start(f32[256,128]{1,0:T(8,128)S(1)} %get-tuple-element.43), channel_id=1, source_target_pairs={{0,1},{1,0},{2,3},{3,2},{4,5},{5,4},{6,7},{7,6},{8,9},{9,8},{10,11... | collective-permute-start | bytes 393224 | tf_op jit(solution)/shard_map/ppermute | solution.py:346
  32.1 0.1 collective-permute-start.17
  32.2 0.4 collective-permute-start.12
  32.6 0.3 collective-permute-done.13
  33.0 1.6 %collective-permute-start.14 = (f32[256,128]{1,0:T(8,128)S(1)}, f32[256,128]{1,0:T(8,128)S(1)}, u32[]{:S(2)}, u32[]{:S(2)}) collective-permute-start(f32[256,128]{1,0:T(8,128)S(1)} %add.14), channel_id=1, source_target_pairs={{0,2},{1,3},{2,0},{3,1},{4,6},{5,7},{6,4},{7,5},{8,10},{9,11},{10,... | collective-permute-start | bytes 393224 | tf_op jit(solution)/shard_map/ppermute | solution.py:346
  34.5 0.0 collective-permute-done.15
  34.6 0.6 %collective-permute-start.16 = (f32[256,128]{1,0:T(8,128)S(1)}, f32[256,128]{1,0:T(8,128)S(1)}, u32[]{:S(2)}, u32[]{:S(2)}) collective-permute-start(f32[256,128]{1,0:T(8,128)S(1)} %add.15), channel_id=1, source_target_pairs={{0,4},{1,5},{2,6},{3,7},{4,0},{5,1},{6,2},{7,3},{8,12},{9,13},{10,... | collective-permute-start | bytes 393224 | tf_op jit(solution)/shard_map/ppermute | solution.py:346
  35.1 0.0 collective-permute-done.17
  35.2 1.6 %collective-permute-start.18 = (f32[256,128]{1,0:T(8,128)S(1)}, f32[256,128]{1,0:T(8,128)S(1)}, u32[]{:S(2)}, u32[]{:S(2)}) collective-permute-start(f32[256,128]{1,0:T(8,128)S(1)} %add.16), channel_id=1, source_target_pairs={{0,6},{1,7},{2,4},{3,5},{4,2},{5,3},{6,0},{7,1},{8,14},{9,15},{10,... | collective-permute-start | bytes 393224 | tf_op jit(solution)/shard_map/ppermute | solution.py:346
  36.7 0.0 collective-permute-done.12.pair
  36.7 2.1 %collective-permute-done.14.across = f32[256,128]{1,0:T(8,128)S(1)} collective-permute-done((f32[256,128]{1,0:T(8,128)S(1)}, f32[256,128]{1,0:T(8,128)S(1)}, u32[]{:S(2)}, u32[]{:S(2)}) %collective-permute-start.14) | collective-permute-done | bytes 131104 | tf_op jit(solution)/shard_map/ppermute | solution.py:346
  38.8 3.9 %collective-permute-done.16.up = f32[256,128]{1,0:T(8,128)S(1)} collective-permute-done((f32[256,128]{1,0:T(8,128)S(1)}, f32[256,128]{1,0:T(8,128)S(1)}, u32[]{:S(2)}, u32[]{:S(2)}) %collective-permute-start.16) | collective-permute-done | bytes 131104 | tf_op jit(solution)/shard_map/ppermute | solution.py:346
  42.7 0.0 collective-permute-done.18.diagonal
  42.7 1.5 %shard_map.68 = f32[512,128]{1,0:T(8,128)} custom-call(s32[5]{0:T(128)S(1)} %stack.31.me_ref, f32[256,128]{1,0:T(8,128)S(1)} %get-tuple-element.38.own, f32[256,128]{1,0:T(8,128)S(1)} %collective-permute-done.12.pair, f32[256,128]{1,0:T(8,128)S(1)} %collective-permute-done.14.across, f32[256,128]{1,0:T(8,128)S(1)} %collective-permute-done.16.up, ...), custom_call_target="tpu_custom_call" | custom-call | flops 65536 | bytes 65536 | tf_op jit(solution)/shard_map/pallas_call | solution.py:118
  (3 shorter events, 0.0 us)
Async XLA Ops:
  1.3 10.5 %collective-permute-start = (f32[328,128]{1,0:T(8,128)S(1)}, f32[328,128]{1,0:T(8,128)S(1)}, u32[]{:S(2)}, u32[]{:S(2)}) collective-permute-start(f32[328,128]{1,0:T(8,128)S(1)} %get-tuple-element.26.refs_0_.refs_8_.own_tile), channel_id=1, source_target_pairs={{0,2},{1,3},{2,0},{3,1},{4,6},{5,7},{6,4},{7,5},{8,10},{9,11},{10,... | collective-permute-start | bytes 503816 | tf_op jit(solution)/shard_map/ppermute | solution.py:346
  2.8 9.2 %collective-permute-start.4 = (f32[328,128]{1,0:T(8,128)S(1)}, f32[328,128]{1,0:T(8,128)S(1)}, u32[]{:S(2)}, u32[]{:S(2)}) collective-permute-start(f32[328,128]{1,0:T(8,128)S(1)} %get-tuple-element.30), channel_id=1, source_target_pairs={{0,6},{1,7},{2,4},{3,5},{4,2},{5,3},{6,0},{7,1},{8,14},{9,15},{10,... | collective-permute-start | bytes 503816 | tf_op jit(solution)/shard_map/ppermute | solution.py:346
  4.3 9.1 %collective-permute-start.3 = (f32[328,128]{1,0:T(8,128)S(1)}, f32[328,128]{1,0:T(8,128)S(1)}, u32[]{:S(2)}, u32[]{:S(2)}) collective-permute-start(f32[328,128]{1,0:T(8,128)S(1)} %get-tuple-element.30), channel_id=1, source_target_pairs={{0,4},{1,5},{2,6},{3,7},{4,0},{5,1},{6,2},{7,3},{8,12},{9,13},{10,... | collective-permute-start | bytes 503816 | tf_op jit(solution)/shard_map/ppermute | solution.py:346
  4.8 5.1 %collective-permute-start.1 = (f32[72,128]{1,0:T(8,128)S(1)}, f32[72,128]{1,0:T(8,128)S(1)}, u32[]{:S(2)}, u32[]{:S(2)}) collective-permute-start(f32[72,128]{1,0:T(8,128)S(1)} %get-tuple-element.27), channel_id=1, source_target_pairs={{0,8},{16,24},{8,0},{24,16},{1,9},{17,25},{9,1},{25,17},{2,10},{18... | collective-permute-start | bytes 110600 | tf_op jit(solution)/shard_map/ppermute | solution.py:352
  4.8 7.0 %collective-permute-start.2 = (f32[72,128]{1,0:T(8,128)S(1)}, f32[72,128]{1,0:T(8,128)S(1)}, u32[]{:S(2)}, u32[]{:S(2)}) collective-permute-start(f32[72,128]{1,0:T(8,128)S(1)} %get-tuple-element.28), channel_id=1, source_target_pairs={{8,16},{16,8},{9,17},{17,9},{10,18},{18,10},{11,19},{19,11},{12,20... | collective-permute-start | bytes 110600 | tf_op jit(solution)/shard_map/ppermute | solution.py:352
  9.9 4.1 %collective-permute-start.5 = (f32[328,128]{1,0:T(8,128)S(1)}, f32[328,128]{1,0:T(8,128)S(1)}, u32[]{:S(2)}, u32[]{:S(2)}) collective-permute-start(f32[328,128]{1,0:T(8,128)S(1)} %get-tuple-element.26.refs_0_.refs_8_.own_tile), channel_id=1, source_target_pairs={{0,1},{1,0},{2,3},{3,2},{4,5},{5,4},{6,7},{7,6},{8,9},{9,8},{10,11... | collective-permute-start | bytes 503816 | tf_op jit(solution)/shard_map/ppermute | solution.py:346
  12.0 2.0 %collective-permute-start.8 = (f32[328,128]{1,0:T(8,128)S(1)}, f32[328,128]{1,0:T(8,128)S(1)}, u32[]{:S(2)}, u32[]{:S(2)}) collective-permute-start(f32[328,128]{1,0:T(8,128)S(1)} %collective-permute-done.4.refs_3_.refs_11_), channel_id=1, source_target_pairs={{0,1},{1,0},{2,3},{3,2},{4,5},{5,4},{6,7},{7,6},{8,9},{9,8},{10,11... | collective-permute-start | bytes 503816 | tf_op jit(solution)/shard_map/ppermute | solution.py:346
  13.4 1.4 %collective-permute-start.7 = (f32[328,128]{1,0:T(8,128)S(1)}, f32[328,128]{1,0:T(8,128)S(1)}, u32[]{:S(2)}, u32[]{:S(2)}) collective-permute-start(f32[328,128]{1,0:T(8,128)S(1)} %collective-permute-done.3.refs_2_.refs_10_), channel_id=1, source_target_pairs={{0,1},{1,0},{2,3},{3,2},{4,5},{5,4},{6,7},{7,6},{8,9},{9,8},{10,11... | collective-permute-start | bytes 503816 | tf_op jit(solution)/shard_map/ppermute | solution.py:346
  13.4 1.6 %collective-permute-start.6 = (f32[328,128]{1,0:T(8,128)S(1)}, f32[328,128]{1,0:T(8,128)S(1)}, u32[]{:S(2)}, u32[]{:S(2)}) collective-permute-start(f32[328,128]{1,0:T(8,128)S(1)} %collective-permute-done.refs_1_.refs_9_), channel_id=1, source_target_pairs={{0,1},{1,0},{2,3},{3,2},{4,5},{5,4},{6,7},{7,6},{8,9},{9,8},{10,11... | collective-permute-start | bytes 503816 | tf_op jit(solution)/shard_map/ppermute | solution.py:346
  14.0 8.8 %copy-start = (f32[2,8,32,32]{3,2,1,0:T(8,128)S(1)}, f32[2,8,32,32]{3,2,1,0:T(8,128)}, u32[]{:S(2)}) copy-start(f32[2,8,32,32]{3,2,1,0:T(8,128)} %v.3) | copy-start | bytes 196612
  14.0 8.8 %copy-start.1 = (f32[2,4,8,128]{3,2,1,0:T(8,128)S(1)}, f32[2,4,8,128]{3,2,1,0:T(8,128)}, u32[]{:S(2)}) copy-start(f32[2,4,8,128]{3,2,1,0:T(8,128)} %param.7) | copy-start | bytes 98308
  14.0 8.8 %copy-start.2 = (f32[2,4,8,128]{3,2,1,0:T(8,128)S(1)}, f32[2,4,8,128]{3,2,1,0:T(8,128)}, u32[]{:S(2)}) copy-start(f32[2,4,8,128]{3,2,1,0:T(8,128)} %param.8) | copy-start | bytes 98308
  17.7 11.0 %collective-permute-start.9 = (f32[512,128]{1,0:T(8,128)S(1)}, f32[512,128]{1,0:T(8,128)S(1)}, u32[]{:S(2)}, u32[]{:S(2)}) collective-permute-start(f32[512,128]{1,0:T(8,128)S(1)} %get-tuple-element.32), channel_id=1, source_target_pairs={{0,8},{16,24},{8,0},{24,16},{1,9},{17,25},{9,1},{25,17},{2,10},{18... | collective-permute-start | bytes 786440 | tf_op jit(solution)/shard_map/ppermute | solution.py:352
  18.2 11.1 %collective-permute-start.10 = (f32[512,128]{1,0:T(8,128)S(1)}, f32[512,128]{1,0:T(8,128)S(1)}, u32[]{:S(2)}, u32[]{:S(2)}) collective-permute-start(f32[512,128]{1,0:T(8,128)S(1)} %get-tuple-element.33), channel_id=1, source_target_pairs={{8,16},{16,8},{9,17},{17,9},{10,18},{18,10},{11,19},{19,11},{12,20... | collective-permute-start | bytes 786440 | tf_op jit(solution)/shard_map/ppermute | solution.py:352
  24.3 4.3 %collective-permute-start.11 = (f32[128,128]{1,0:T(8,128)S(1)}, f32[128,128]{1,0:T(8,128)S(1)}, u32[]{:S(2)}, u32[]{:S(2)}) collective-permute-start(f32[128,128]{1,0:T(8,128)S(1)} %get-tuple-element.36.own_pack.own_tab), channel_id=1, source_target_pairs={{0,4},{1,5},{2,6},{3,7},{4,0},{5,1},{6,2},{7,3},{8,12},{9,13},{10,... | collective-permute-start | bytes 196616 | tf_op jit(solution)/shard_map/ppermute | solution.py:346
  31.6 1.4 %collective-permute-start.13 = (f32[256,128]{1,0:T(8,128)S(1)}, f32[256,128]{1,0:T(8,128)S(1)}, u32[]{:S(2)}, u32[]{:S(2)}) collective-permute-start(f32[256,128]{1,0:T(8,128)S(1)} %get-tuple-element.41), channel_id=1, source_target_pairs={{0,1},{1,0},{2,3},{3,2},{4,5},{5,4},{6,7},{7,6},{8,9},{9,8},{10,11... | collective-permute-start | bytes 393224 | tf_op jit(solution)/shard_map/ppermute | solution.py:346
  31.6 2.9 %collective-permute-start.15 = (f32[256,128]{1,0:T(8,128)S(1)}, f32[256,128]{1,0:T(8,128)S(1)}, u32[]{:S(2)}, u32[]{:S(2)}) collective-permute-start(f32[256,128]{1,0:T(8,128)S(1)} %get-tuple-element.43), channel_id=1, source_target_pairs={{0,1},{1,0},{2,3},{3,2},{4,5},{5,4},{6,7},{7,6},{8,9},{9,8},{10,11... | collective-permute-start | bytes 393224 | tf_op jit(solution)/shard_map/ppermute | solution.py:346
  32.1 3.0 %collective-permute-start.17 = (f32[256,128]{1,0:T(8,128)S(1)}, f32[256,128]{1,0:T(8,128)S(1)}, u32[]{:S(2)}, u32[]{:S(2)}) collective-permute-start(f32[256,128]{1,0:T(8,128)S(1)} %get-tuple-element.45), channel_id=1, source_target_pairs={{0,1},{1,0},{2,3},{3,2},{4,5},{5,4},{6,7},{7,6},{8,9},{9,8},{10,11... | collective-permute-start | bytes 393224 | tf_op jit(solution)/shard_map/ppermute | solution.py:346
  32.2 4.5 %collective-permute-start.12 = (f32[256,128]{1,0:T(8,128)S(1)}, f32[256,128]{1,0:T(8,128)S(1)}, u32[]{:S(2)}, u32[]{:S(2)}) collective-permute-start(f32[256,128]{1,0:T(8,128)S(1)} %get-tuple-element.39), channel_id=1, source_target_pairs={{0,1},{1,0},{2,3},{3,2},{4,5},{5,4},{6,7},{7,6},{8,9},{9,8},{10,11... | collective-permute-start | bytes 393224 | tf_op jit(solution)/shard_map/ppermute | solution.py:346
  33.0 5.8 %collective-permute-start.14 = (f32[256,128]{1,0:T(8,128)S(1)}, f32[256,128]{1,0:T(8,128)S(1)}, u32[]{:S(2)}, u32[]{:S(2)}) collective-permute-start(f32[256,128]{1,0:T(8,128)S(1)} %add.14), channel_id=1, source_target_pairs={{0,2},{1,3},{2,0},{3,1},{4,6},{5,7},{6,4},{7,5},{8,10},{9,11},{10,... | collective-permute-start | bytes 393224 | tf_op jit(solution)/shard_map/ppermute | solution.py:346
  34.6 8.1 %collective-permute-start.16 = (f32[256,128]{1,0:T(8,128)S(1)}, f32[256,128]{1,0:T(8,128)S(1)}, u32[]{:S(2)}, u32[]{:S(2)}) collective-permute-start(f32[256,128]{1,0:T(8,128)S(1)} %add.15), channel_id=1, source_target_pairs={{0,4},{1,5},{2,6},{3,7},{4,0},{5,1},{6,2},{7,3},{8,12},{9,13},{10,... | collective-permute-start | bytes 393224 | tf_op jit(solution)/shard_map/ppermute | solution.py:346
  35.2 7.6 %collective-permute-start.18 = (f32[256,128]{1,0:T(8,128)S(1)}, f32[256,128]{1,0:T(8,128)S(1)}, u32[]{:S(2)}, u32[]{:S(2)}) collective-permute-start(f32[256,128]{1,0:T(8,128)S(1)} %add.16), channel_id=1, source_target_pairs={{0,6},{1,7},{2,4},{3,5},{4,2},{5,3},{6,0},{7,1},{8,14},{9,15},{10,... | collective-permute-start | bytes 393224 | tf_op jit(solution)/shard_map/ppermute | solution.py:346

commit v4 on v3

--- a/solution.py
+++ b/solution.py
@@ -112,15 +112,14 @@
     return pl.BlockSpec((size,), lambda i: (0,), memory_space=pltpu.SMEM)
 
 
-def call(kernel, out_rows, in_specs, scratch, cost, *args):
-    sizes = [n if isinstance(n, tuple) else (n, jnp.float32) for n in out_rows]
-    outs = [jax.ShapeDtypeStruct((n, 128), dtype) for n, dtype in sizes]
+def call(kernel, outs, in_specs, scratch, cost, *args):
+    outs = [((n, 128), jnp.float32) if isinstance(n, int) else n for n in outs]
     return pl.pallas_call(
         kernel,
         grid=(1,),
-        out_shape=outs,
+        out_shape=[jax.ShapeDtypeStruct(*out) for out in outs],
         in_specs=in_specs,
-        out_specs=[vmem((n, 128)) for n, _ in sizes],
+        out_specs=[vmem(shape, len(shape)) for shape, _ in outs],
         scratch_shapes=scratch,
         compiler_params=pltpu.CompilerParams(vmem_limit_bytes=VMEM_LIMIT),
         cost_estimate=pl.CostEstimate(flops=cost, bytes_accessed=cost, transcendentals=0),
@@ -224,12 +223,9 @@
     matrices0[4 * levels : 8 * levels, :] = turned(four(0, 4))
 
 
-def first_spread(levels, me_ref, *refs):
-    messages, tables = refs[0:8], refs[8:16]
-    part, m1, m2, acc, masks = refs[16:]
+def spread_messages(levels, me_ref, messages, tables, acc, masks):
     per_field = 8 * levels
-    me, lat_start, even = me_ref[0], me_ref[1], me_ref[2]
-    acc[...] = jnp.zeros_like(acc)
+    me, lat_start = me_ref[0], me_ref[1]
     stay, back, on = lane_masks()
     for n, mask in enumerate((stay, back, jnp.zeros_like(stay), on)):
         masks[n] = mask
@@ -247,7 +243,19 @@
             return 0
 
         lax.fori_loop(0, 8, row, 0, unroll=True)
-    part[...] = acc[...].reshape(part.shape)
+
+
+def first_spread_own(levels, me_ref, *refs):
+    messages, tables, (acc, masks) = refs[0:4], refs[4:8], refs[8:]
+    acc[...] = jnp.zeros_like(acc)
+    spread_messages(levels, me_ref, messages, tables, acc, masks)
+
+
+def first_spread_other(levels, me_ref, *refs):
+    messages, tables, (before, acc, m1, m2, masks) = refs[0:4], refs[4:8], refs[8:]
+    acc[...] = before[...]
+    spread_messages(levels, me_ref, messages, tables, acc, masks)
+    even = me_ref[2]
 
     def write(out, part_row, count):
         for h in range(2):
@@ -272,62 +280,61 @@
     return jnp.dot(matrix, jnp.concatenate([high, high, low, low], axis=0), preferred_element_type=jnp.float32)
 
 
-def second_spread(levels, me_ref, part, r1, r2, own_pack, y_pack, matrices, own_tab, y_tab, *refs):
-    outs, (state, acc) = refs[0:8], refs[8:]
-    me, lat_start, even, at_start, at_end = (me_ref[n] for n in range(5))
+def spread_half(levels, upper, me_ref, part, received, own_pack, y_pack, matrices, own_tab, y_tab, state, acc):
+    me, lat_start, at_start, at_end = me_ref[0], me_ref[1], me_ref[3], me_ref[4]
     slot = me // 4
-    is_even = even == 1
-    for n in range(15):
+    base = 8 * upper
+
+    def exists(j):
+        n = base + j
+        there = (n < 15) & ((at_start == 0) | (n >= 4)) if j < 4 else n < 15
+        return there & ((at_end == 0) | (n < 12)) if j >= 4 else there
+
+    for j in range(8):
         halves = []
         for h in range(2):
-            own = slice((h * 15 + n - 1) * levels, (h * 15 + n) * levels)
-            b = slice((h * 8 + n) * levels, (h * 8 + n + 1) * levels)
-            a = slice((h * 8 + n - 9) * levels, (h * 8 + n - 8) * levels)
-            if n == 0:
-                value = jnp.where(is_even, r2[b, :], r1[b, :])
-            elif n < 8:
-                value = part[own, :] + jnp.where(is_even, r2[b, :], r1[b, :])
-            elif n == 8:
-                value = part[own, :]
+            sent = received[pl.ds(pl.multiple_of((h * 8 + j - upper) * levels, levels) if j else h * 8 * levels, levels), :]
+            if j == 0:
+                value = jnp.where(upper == 1, part[h * 15 + 7], sent)
             else:
-                value = part[own, :] + jnp.where(is_even, r1[a, :], r2[a, :])
+                value = part[h * 15 + base + j - 1] + sent
+            if j == 7:
+                value = jnp.where(upper == 1, 0.0, value)
             halves.append(value)
-        result = vertical(matrices[n * levels : (n + 1) * levels, :], jnp.concatenate(halves, axis=1))
-        state[n] = result[:, :128]
-        state[15 + n] = result[:, 128:]
+        matrix = matrices[pl.ds(pl.multiple_of((base + j) * levels, levels), levels), :]
+        result = vertical(matrix, jnp.concatenate(halves, axis=1))
+        state[j] = result[:, :128]
+        state[8 + j] = result[:, 128:]
     for q in range(8):
         acc[q * 22 + 7 : q * 22 + 15] = jnp.zeros((8, levels, 128), jnp.float32)
     stay, back, on = lane_masks()
-
-    def spread(n, h):
-        mine = slot == h
-        tau = jnp.where(mine, own_tab[2, n], y_tab[2, n]).astype(jnp.int32)
-        first = jnp.where(mine, own_tab[0, n], y_tab[0, n]).astype(jnp.int32) - lat_start + 7
-        at = slice(8 * n, 8 * n + 8)
-        prods = products(jnp.where(mine, own_pack[at, :], y_pack[at, :]))
-        sources = [rolled(state[h * 15 + n, kk : kk + 8, :]) for kk in range(0, levels, 8)]
-        add_terms(sources, masked(prods, stay, range(NODES)), acc, (tau ^ me) * 22 + first)
-        add_terms(sources, masked(prods, back, (0,)), acc, (((tau + 7) & 7) ^ me) * 22 + first)
-        add_terms(sources, masked(prods, on, (2, 3)), acc, (((tau + 1) & 7) ^ me) * 22 + first)
-
-    for n in range(4, 12):
+    for j in range(8):
+        n = base + j
+        there = exists(j)
+        at = pl.ds(pl.multiple_of(8 * n, 8), 8)
         for h in range(2):
-            spread(n, h)
-
-    @pl.when(at_start == 0)
-    def _():
-        for n in range(4):
-            for h in range(2):
-                spread(n, h)
-
-    @pl.when(at_end == 0)
-    def _():
-        for n in range(12, 15):
-            for h in range(2):
-                spread(n, h)
-
-    for q in range(8):
-        outs[q][...] = acc[q * 22 + 7 : q * 22 + 15].reshape(8 * levels, 128)
+            mine = slot == h
+            tau = jnp.where(there, jnp.where(mine, own_tab[2, n], y_tab[2, n]).astype(jnp.int32), 0)
+            first = jnp.where(mine, own_tab[0, n], y_tab[0, n]).astype(jnp.int32) - lat_start + 7
+            first = jnp.where(there, first, 7)
+            prods = products(jnp.where(there, jnp.where(mine, own_pack[at, :], y_pack[at, :]), 0.0))
+            sources = [rolled(state[h * 8 + j, kk : kk + 8, :]) for kk in range(0, levels, 8)]
+            add_terms(sources, masked(prods, stay, range(NODES)), acc, (tau ^ me) * 22 + first)
+            add_terms(sources, masked(prods, back, (0,)), acc, (((tau + 7) & 7) ^ me) * 22 + first)
+            add_terms(sources, masked(prods, on, (2, 3)), acc, (((tau + 1) & 7) ^ me) * 22 + first)
+
+
+def second_spread_early(levels, me_ref, *refs):
+    (acc, state), refs = refs[-2:], refs[:-2]
+    spread_half(levels, me_ref[2], me_ref, *refs, state, acc)
+
+
+def second_spread_late(levels, me_ref, *refs):
+    (before, *outs, state, acc), refs = refs[7:], refs[:7]
+    spread_half(levels, 1 - me_ref[2], me_ref, *refs, state, acc)
+    for q, out in enumerate(outs):
+        rows = slice(q * 22 + 7, q * 22 + 15)
+        out[...] = (acc[rows] + before[rows]).reshape(8 * levels, 128)
 
 
 def finish(levels, me_ref, own, pair, across, up, diagonal, matrices, out):
@@ -386,22 +393,36 @@
     far[2], e1, e2 = lax.optimization_barrier((far[2], e1, e2))
     messages = [own, far[2], far[4], far[6]]
     messages = messages + [swap_lon(value, 1) for value in messages]
-    part, m1, m2 = call(
-        functools.partial(first_spread, levels),
-        [30 * levels, 16 * levels, 16 * levels],
-        [smem_whole(5)] + [vmem((message, 128))] * 8 + [smem_tile(message // 8 - 1)] * 8,
-        [pltpu.VMEM((30, levels, 128), jnp.float32), pltpu.VMEM((4, 8, 128), jnp.float32)],
+    table = smem_tile(message // 8 - 1)
+    masks = pltpu.VMEM((4, 8, 128), jnp.float32)
+    partial = ((30, levels, 128), jnp.float32)
+    (part,) = call(
+        functools.partial(first_spread_own, levels),
+        [partial],
+        [smem_whole(5)] + [vmem((message, 128))] * 4 + [table] * 4,
+        [masks],
         8 * size,
         info,
-        *messages,
-        *messages,
+        *messages[:4],
+        *messages[:4],
+    )
+    part, m1, m2 = call(
+        functools.partial(first_spread_other, levels),
+        [partial, 16 * levels, 16 * levels],
+        [smem_whole(5)] + [vmem((message, 128))] * 4 + [table] * 4 + [vmem(partial[0], 3)],
+        [masks],
+        8 * size,
+        info,
+        *messages[4:],
+        *messages[4:],
+        part,
     )
     r1, r2 = swap_lat(m1, 0), swap_lat(m2, 1)
     pack, matrices1, matrices0 = call(
         functools.partial(rim_data, levels),
-        [128, (16 * levels, jnp.bfloat16), (8 * levels, jnp.bfloat16)],
+        [128, ((16 * levels, 128), jnp.bfloat16), ((8 * levels, 128), jnp.bfloat16)],
         [smem_whole(5), tile, vmem((64, 128)), vmem((64, 128)), vmem((side, 128)), vmem((side, 128))]
-        + [vmem(vertical_inverse.shape, 4), vmem((8, 128))],
+        + [vmem(vertical_inverse.shape, 4), vmem((8, levels, 128), 3)],
         [],
         size,
         info,
@@ -414,25 +435,25 @@
         part,
     )
     y_pack = swap_lon(pack, 4)
+    half_specs = [smem_whole(5), vmem(partial[0], 3), vmem((16 * levels, 128)), vmem((128, 128)), vmem((128, 128))]
+    half_specs += [vmem((16 * levels, 128)), smem_tile(15), smem_tile(15)]
+    spread_shape = ((8 * 22, levels, 128), jnp.float32)
+    state = pltpu.VMEM((16, levels, 128), jnp.float32)
+    (early,) = call(
+        functools.partial(second_spread_early, levels),
+        [spread_shape],
+        half_specs,
+        [state],
+        8 * size,
+        *(info, part, r1, pack, y_pack, matrices1, pack, y_pack),
+    )
     pieces = call(
-        functools.partial(second_spread, levels),
+        functools.partial(second_spread_late, levels),
         [8 * levels] * 8,
-        [smem_whole(5), vmem((30 * levels, 128))]
-        + [vmem((16 * levels, 128))] * 2
-        + [vmem((128, 128))] * 2
-        + [vmem((16 * levels, 128))]
-        + [smem_tile(15)] * 2,
-        [pltpu.VMEM((30, levels, 128), jnp.float32), pltpu.VMEM((8 * 22, levels, 128), jnp.float32)],
-        16 * size,
-        info,
-        part,
-        r1,
-        r2,
-        pack,
-        y_pack,
-        matrices1,
-        pack,
-        y_pack,
+        half_specs + [vmem(spread_shape[0], 3)],
+        [state, pltpu.VMEM(*spread_shape)],
+        8 * size,
+        *(info, part, r2, pack, y_pack, matrices1, pack, y_pack, early),
     )
     received = {}
     for bits in (6, 4, 2):

time: 44.5 us -> 44.3 us (level)
  waiting for transfers between devices: 15.1 us -> 13.5 us
  Pallas kernels: 9.15 us -> 10.7 us
    pallas_call x4 -> x6, Pallas kernels: 7.88 us -> 9.36 us  [call(): pl.pallas_call(kernel, grid=(1,), out_shape=[jax.ShapeDtypeStruct(*out) f...]
    ppermute x15, waiting for transfers between devices: 12.7 us -> 11.7 us  [swap_lon(): return lax.ppermute(value, 'lon', [(i, i ^ bits) for i in range(RING)])]
    ppermute x4, waiting for transfers between devices: 2.43 us -> 1.84 us  [swap_lat(): return lax.ppermute(value, 'lat', pairs + [(b, a) for a, b in pairs])]
  transfers between devices with their start and end apart: 19 -> 19, of which waited for: 10 -> 7; matrix products, arithmetic and copies ran while one was open for 0% -> 0% of each run, Pallas kernels for 3% -> 11%
where the time goes in v4:
time: 44.3 us; the launch traced here: 44.1 us
  starting transfers between devices  19.6 us (44%)
  waiting for transfers between devices  13.5 us (30%)
  Pallas kernels  10.7 us (24%)
    ppermute x15, waiting for transfers between devices, swap_lon(): return lax.ppermute(value, 'lon', [(i, i ^ bits) for i in range(RING)])  11.7 us
    ppermute x4, starting transfers between devices, swap_lat(): return lax.ppermute(value, 'lat', pairs + [(b, a) for a, b in pairs])  10.2 us
    ppermute x15, starting transfers between devices, swap_lon(): return lax.ppermute(value, 'lon', [(i, i ^ bits) for i in range(RING)])  9.47 us
    pallas_call x6, Pallas kernels, call(): pl.pallas_call(kernel, grid=(1,), out_shape=[jax.ShapeDtypeStruct(*out) f...  9.36 us
    ppermute x4, waiting for transfers between devices, swap_lat(): return lax.ppermute(value, 'lat', pairs + [(b, a) for a, b in pairs])  1.84 us
    pallas_call x1, Pallas kernels, ring_body(): pl.pallas_call(functools.partial(assemble, levels), out_shape=[pltpu.VMEM...  1.29 us
  transfers between devices with their start and end apart: 19, of which 7 were waited for; matrix products, arithmetic and copies ran while one was open for 0% of the time, Pallas kernels for 11%

profile of v4, /device:TPU:8, one launch (start us, length us, event | category | flops | bytes accessed | tf_op | source)
XLA Modules:
  0.0 44.1 jit_solution(14920359021991339410)
XLA Ops:
  0.0 0.0 copy-start
  0.0 0.0 copy-start.2
  0.0 0.0 copy-start.1
  0.0 1.3 %shard_map.64 = (f32[328,128]{1,0:T(8,128)S(1)}, f32[328,128]{1,0:T(8,128)S(1)}, f32[72,128]{1,0:T(8,128)S(1)}, f32[72,128]{1,0:T(8,128)S(1)}) custom-call(s32[2,8]{1,0:T(2,128)} %bitcast.16, s32[2,8]{1,0:T(2,128)} %bitcast.17, f32[512,128]{1,0:T(8,128)} %bitcast.15, f32[64,128]{1,0:T(8,128)} %bitcast.11, f32[64,128]{1,0:T(8,128)} %bitcast.13, ...), custom_call_target="tpu_custom_call" | custom-call | tf_op jit(solution)/shard_map/pallas_call | solution.py:376
  1.3 1.6 %collective-permute-start.1 = (f32[328,128]{1,0:T(8,128)S(1)}, f32[328,128]{1,0:T(8,128)S(1)}, u32[]{:S(2)}, u32[]{:S(2)}) collective-permute-start(f32[328,128]{1,0:T(8,128)S(1)} %get-tuple-element.26.refs_0_.refs_4_.own_tile), channel_id=1, source_target_pairs={{0,2},{1,3},{2,0},{3,1},{4,6},{5,7},{6,4},{7,5},{8,10},{9,11},{10,... | collective-permute-start | bytes 503816 | tf_op jit(solution)/shard_map/ppermute | solution.py:353
  2.9 1.5 %collective-permute-start.7 = (f32[328,128]{1,0:T(8,128)S(1)}, f32[328,128]{1,0:T(8,128)S(1)}, u32[]{:S(2)}, u32[]{:S(2)}) collective-permute-start(f32[328,128]{1,0:T(8,128)S(1)} %get-tuple-element.30), channel_id=1, source_target_pairs={{0,6},{1,7},{2,4},{3,5},{4,2},{5,3},{6,0},{7,1},{8,14},{9,15},{10,... | collective-permute-start | bytes 503816 | tf_op jit(solution)/shard_map/ppermute | solution.py:353
  4.4 0.5 %collective-permute-start.5 = (f32[328,128]{1,0:T(8,128)S(1)}, f32[328,128]{1,0:T(8,128)S(1)}, u32[]{:S(2)}, u32[]{:S(2)}) collective-permute-start(f32[328,128]{1,0:T(8,128)S(1)} %get-tuple-element.30), channel_id=1, source_target_pairs={{0,4},{1,5},{2,6},{3,7},{4,0},{5,1},{6,2},{7,3},{8,12},{9,13},{10,... | collective-permute-start | bytes 503816 | tf_op jit(solution)/shard_map/ppermute | solution.py:353
  4.9 0.0 collective-permute-start.2
  4.9 5.0 %collective-permute-start.3 = (f32[72,128]{1,0:T(8,128)S(1)}, f32[72,128]{1,0:T(8,128)S(1)}, u32[]{:S(2)}, u32[]{:S(2)}) collective-permute-start(f32[72,128]{1,0:T(8,128)S(1)} %get-tuple-element.28), channel_id=1, source_target_pairs={{8,16},{16,8},{9,17},{17,9},{10,18},{18,10},{11,19},{19,11},{12,20... | collective-permute-start | bytes 110600 | tf_op jit(solution)/shard_map/ppermute | solution.py:359
  9.9 0.0 collective-permute-done.2.e1
  9.9 0.1 collective-permute-start
  10.0 1.8 %collective-permute-done.3.e2 = f32[72,128]{1,0:T(8,128)S(1)} collective-permute-done((f32[72,128]{1,0:T(8,128)S(1)}, f32[72,128]{1,0:T(8,128)S(1)}, u32[]{:S(2)}, u32[]{:S(2)}) %collective-permute-start.3) | collective-permute-done | bytes 36896 | tf_op jit(solution)/shard_map/ppermute | solution.py:359
  11.8 0.0 collective-permute-done.1.refs_1_.refs_5_
  11.8 0.2 collective-permute-done.7.refs_3_.refs_7_
  12.1 0.0 collective-permute-start.8
  12.1 1.4 %collective-permute-done.5.refs_2_.refs_6_ = f32[328,128]{1,0:T(8,128)S(1)} collective-permute-done((f32[328,128]{1,0:T(8,128)S(1)}, f32[328,128]{1,0:T(8,128)S(1)}, u32[]{:S(2)}, u32[]{:S(2)}) %collective-permute-start.5) | collective-permute-done | bytes 167968 | tf_op jit(solution)/shard_map/ppermute | solution.py:353
  13.4 0.0 collective-permute-start.6
  13.4 0.5 %collective-permute-start.4 = (f32[328,128]{1,0:T(8,128)S(1)}, f32[328,128]{1,0:T(8,128)S(1)}, u32[]{:S(2)}, u32[]{:S(2)}) collective-permute-start(f32[328,128]{1,0:T(8,128)S(1)} %collective-permute-done.1.refs_1_.refs_5_), channel_id=1, source_target_pairs={{0,1},{1,0},{2,3},{3,2},{4,5},{5,4},{6,7},{7,6},{8,9},{9,8},{10,11... | collective-permute-start | bytes 503816 | tf_op jit(solution)/shard_map/ppermute | solution.py:353
  13.9 0.1 stack.31.me_ref
  14.0 1.6 %shard_map.65.refs_8_ = f32[30,32,128]{2,1,0:T(8,128)S(1)} custom-call(s32[5]{0:T(128)S(1)} %stack.31.me_ref, f32[328,128]{1,0:T(8,128)S(1)} %get-tuple-element.26.refs_0_.refs_4_.own_tile, f32[328,128]{1,0:T(8,128)S(1)} %collective-permute-done.1.refs_1_.refs_5_, f32[328,128]{1,0:T(8,128)S(1)} %collective-permute-done.5.refs_2_.refs_6_, ...), custom_call_target="tpu_custom_call" | custom-call | flops 524288 | bytes 524288 | tf_op jit(solution)/shard_map/pallas_call | solution.py:117
  15.6 0.0 collective-permute-done.refs_0_.refs_4_
  15.6 0.0 collective-permute-done.8.refs_3_.refs_7_
  15.6 0.0 collective-permute-done.6.refs_2_.refs_6_
  15.6 0.0 collective-permute-done.4.refs_1_.refs_5_
  15.7 1.6 %shard_map.66 = (f32[30,32,128]{2,1,0:T(8,128)S(1)}, f32[512,128]{1,0:T(8,128)S(1)}, f32[512,128]{1,0:T(8,128)S(1)}) custom-call(s32[5]{0:T(128)S(1)} %stack.31.me_ref, f32[328,128]{1,0:T(8,128)S(1)} %collective-permute-done.refs_0_.refs_4_, f32[328,128]{1,0:T(8,128)S(1)} %collective-permute-done.4.refs_1_.refs_5_, ...), custom_call_target="tpu_custom_call" | custom-call | flops 524288 | bytes 524288 | tf_op jit(solution)/shard_map/pallas_call | solution.py:117
  17.3 0.5 %collective-permute-start.11 = (f32[512,128]{1,0:T(8,128)S(1)}, f32[512,128]{1,0:T(8,128)S(1)}, u32[]{:S(2)}, u32[]{:S(2)}) collective-permute-start(f32[512,128]{1,0:T(8,128)S(1)} %get-tuple-element.37), channel_id=1, source_target_pairs={{0,8},{16,24},{8,0},{24,16},{1,9},{17,25},{9,1},{25,17},{2,10},{18... | collective-permute-start | bytes 786440 | tf_op jit(solution)/shard_map/ppermute | solution.py:359
  17.8 4.6 %collective-permute-start.9 = (f32[512,128]{1,0:T(8,128)S(1)}, f32[512,128]{1,0:T(8,128)S(1)}, u32[]{:S(2)}, u32[]{:S(2)}) collective-permute-start(f32[512,128]{1,0:T(8,128)S(1)} %get-tuple-element.32), channel_id=1, source_target_pairs={{8,16},{16,8},{9,17},{17,9},{10,18},{18,10},{11,19},{19,11},{12,20... | collective-permute-start | bytes 786440 | tf_op jit(solution)/shard_map/ppermute | solution.py:359
  22.4 0.0 copy-done
  22.4 0.0 copy-done.2
  22.4 0.0 copy-done.1
  22.4 1.5 %shard_map.67 = (f32[128,128]{1,0:T(8,128)S(1)}, bf16[512,128]{1,0:T(8,128)(2,1)S(1)}, bf16[256,128]{1,0:T(8,128)(2,1)S(1)}) custom-call(s32[5]{0:T(128)S(1)} %stack.31.me_ref, f32[328,128]{1,0:T(8,128)S(1)} %get-tuple-element.26.refs_0_.refs_4_.own_tile, f32[64,128]{1,0:T(8,128)S(1)} %bitcast.12, f32[64,128]{1,0:T(8,128)S(1)} %bitcast.14, ...), custom_call_target="tpu_custom_call" | custom-call | flops 65536 | bytes 65536 | tf_op jit(solution)/shard_map/pallas_call | solution.py:117
  23.9 0.6 %collective-permute-start.10 = (f32[128,128]{1,0:T(8,128)S(1)}, f32[128,128]{1,0:T(8,128)S(1)}, u32[]{:S(2)}, u32[]{:S(2)}) collective-permute-start(f32[128,128]{1,0:T(8,128)S(1)} %get-tuple-element.35.refs_2_.refs_5_), channel_id=1, source_target_pairs={{0,4},{1,5},{2,6},{3,7},{4,0},{5,1},{6,2},{7,3},{8,12},{9,13},{10,... | collective-permute-start | bytes 196616 | tf_op jit(solution)/shard_map/ppermute | solution.py:353
  24.5 3.8 %collective-permute-done.10.refs_3_.refs_6_ = f32[128,128]{1,0:T(8,128)S(1)} collective-permute-done((f32[128,128]{1,0:T(8,128)S(1)}, f32[128,128]{1,0:T(8,128)S(1)}, u32[]{:S(2)}, u32[]{:S(2)}) %collective-permute-start.10) | collective-permute-done | bytes 65568 | tf_op jit(solution)/shard_map/ppermute | solution.py:353
  28.3 0.0 collective-permute-done.11.refs_1_
  28.3 1.6 %shard_map.68.refs_7_ = f32[176,32,128]{2,1,0:T(8,128)S(1)} custom-call(s32[5]{0:T(128)S(1)} %stack.31.me_ref, f32[30,32,128]{2,1,0:T(8,128)S(1)} %get-tuple-element.31.after_this.refs_0_, f32[512,128]{1,0:T(8,128)S(1)} %collective-permute-done.11.refs_1_, f32[128,128]{1,0:T(8,128)S(1)} %get-tuple-element.35.refs_2_.refs_5_, ...), custom_call_target="tpu_custom_call" | custom-call | flops 524288 | bytes 524288 | tf_op jit(solution)/shard_map/pallas_call | solution.py:117
  29.8 0.0 collective-permute-done.9.refs_1_
  29.8 1.6 %shard_map.69 = (f32[256,128]{1,0:T(8,128)S(1)}, f32[256,128]{1,0:T(8,128)S(1)}, f32[256,128]{1,0:T(8,128)S(1)}, f32[256,128]{1,0:T(8,128)S(1)}, f32[256,128]{1,...) custom-call(s32[5]{0:T(128)S(1)} %stack.31.me_ref, ...), custom_call_target="tpu_custom_call" | custom-call | flops 524288 | bytes 524288 | tf_op jit(solution)/shard_map/pallas_call | solution.py:117
  31.5 0.1 collective-permute-start.13
  31.6 0.5 %collective-permute-start.15 = (f32[256,128]{1,0:T(8,128)S(1)}, f32[256,128]{1,0:T(8,128)S(1)}, u32[]{:S(2)}, u32[]{:S(2)}) collective-permute-start(f32[256,128]{1,0:T(8,128)S(1)} %get-tuple-element.43), channel_id=1, source_target_pairs={{0,1},{1,0},{2,3},{3,2},{4,5},{5,4},{6,7},{7,6},{8,9},{9,8},{10,11... | collective-permute-start | bytes 393224 | tf_op jit(solution)/shard_map/ppermute | solution.py:353
  32.1 0.1 collective-permute-start.17
  32.2 0.4 collective-permute-start.12
  32.6 0.3 collective-permute-done.13
  32.9 1.6 %collective-permute-start.14 = (f32[256,128]{1,0:T(8,128)S(1)}, f32[256,128]{1,0:T(8,128)S(1)}, u32[]{:S(2)}, u32[]{:S(2)}) collective-permute-start(f32[256,128]{1,0:T(8,128)S(1)} %add.14), channel_id=1, source_target_pairs={{0,2},{1,3},{2,0},{3,1},{4,6},{5,7},{6,4},{7,5},{8,10},{9,11},{10,... | collective-permute-start | bytes 393224 | tf_op jit(solution)/shard_map/ppermute | solution.py:353
  34.5 0.0 collective-permute-done.15
  34.5 0.6 %collective-permute-start.16 = (f32[256,128]{1,0:T(8,128)S(1)}, f32[256,128]{1,0:T(8,128)S(1)}, u32[]{:S(2)}, u32[]{:S(2)}) collective-permute-start(f32[256,128]{1,0:T(8,128)S(1)} %add.15), channel_id=1, source_target_pairs={{0,4},{1,5},{2,6},{3,7},{4,0},{5,1},{6,2},{7,3},{8,12},{9,13},{10,... | collective-permute-start | bytes 393224 | tf_op jit(solution)/shard_map/ppermute | solution.py:353
  35.1 0.0 collective-permute-done.17
  35.1 1.6 %collective-permute-start.18 = (f32[256,128]{1,0:T(8,128)S(1)}, f32[256,128]{1,0:T(8,128)S(1)}, u32[]{:S(2)}, u32[]{:S(2)}) collective-permute-start(f32[256,128]{1,0:T(8,128)S(1)} %add.16), channel_id=1, source_target_pairs={{0,6},{1,7},{2,4},{3,5},{4,2},{5,3},{6,0},{7,1},{8,14},{9,15},{10,... | collective-permute-start | bytes 393224 | tf_op jit(solution)/shard_map/ppermute | solution.py:353
  36.7 0.0 collective-permute-done.12.pair
  36.7 2.1 %collective-permute-done.14.across = f32[256,128]{1,0:T(8,128)S(1)} collective-permute-done((f32[256,128]{1,0:T(8,128)S(1)}, f32[256,128]{1,0:T(8,128)S(1)}, u32[]{:S(2)}, u32[]{:S(2)}) %collective-permute-start.14) | collective-permute-done | bytes 131104 | tf_op jit(solution)/shard_map/ppermute | solution.py:353
  38.7 3.9 %collective-permute-done.16.up = f32[256,128]{1,0:T(8,128)S(1)} collective-permute-done((f32[256,128]{1,0:T(8,128)S(1)}, f32[256,128]{1,0:T(8,128)S(1)}, u32[]{:S(2)}, u32[]{:S(2)}) %collective-permute-start.16) | collective-permute-done | bytes 131104 | tf_op jit(solution)/shard_map/ppermute | solution.py:353
  42.7 0.0 collective-permute-done.18.diagonal
  42.7 1.5 %shard_map.70 = f32[512,128]{1,0:T(8,128)} custom-call(s32[5]{0:T(128)S(1)} %stack.31.me_ref, f32[256,128]{1,0:T(8,128)S(1)} %get-tuple-element.38.own, f32[256,128]{1,0:T(8,128)S(1)} %collective-permute-done.12.pair, f32[256,128]{1,0:T(8,128)S(1)} %collective-permute-done.14.across, f32[256,128]{1,0:T(8,128)S(1)} %collective-permute-done.16.up, ...), custom_call_target="tpu_custom_call" | custom-call | flops 65536 | bytes 65536 | tf_op jit(solution)/shard_map/pallas_call | solution.py:117
  (3 shorter events, 0.0 us)
Async XLA Ops:
  0.0 22.4 %copy-start = (f32[2,8,32,32]{3,2,1,0:T(8,128)S(1)}, f32[2,8,32,32]{3,2,1,0:T(8,128)}, u32[]{:S(2)}) copy-start(f32[2,8,32,32]{3,2,1,0:T(8,128)} %v.3) | copy-start | bytes 196612
  0.0 22.4 %copy-start.2 = (f32[2,4,8,128]{3,2,1,0:T(8,128)S(1)}, f32[2,4,8,128]{3,2,1,0:T(8,128)}, u32[]{:S(2)}) copy-start(f32[2,4,8,128]{3,2,1,0:T(8,128)} %param.8) | copy-start | bytes 98308
  0.0 22.4 %copy-start.1 = (f32[2,4,8,128]{3,2,1,0:T(8,128)S(1)}, f32[2,4,8,128]{3,2,1,0:T(8,128)}, u32[]{:S(2)}) copy-start(f32[2,4,8,128]{3,2,1,0:T(8,128)} %param.7) | copy-start | bytes 98308
  1.3 10.5 %collective-permute-start.1 = (f32[328,128]{1,0:T(8,128)S(1)}, f32[328,128]{1,0:T(8,128)S(1)}, u32[]{:S(2)}, u32[]{:S(2)}) collective-permute-start(f32[328,128]{1,0:T(8,128)S(1)} %get-tuple-element.26.refs_0_.refs_4_.own_tile), channel_id=1, source_target_pairs={{0,2},{1,3},{2,0},{3,1},{4,6},{5,7},{6,4},{7,5},{8,10},{9,11},{10,... | collective-permute-start | bytes 503816 | tf_op jit(solution)/shard_map/ppermute | solution.py:353
  2.9 9.2 %collective-permute-start.7 = (f32[328,128]{1,0:T(8,128)S(1)}, f32[328,128]{1,0:T(8,128)S(1)}, u32[]{:S(2)}, u32[]{:S(2)}) collective-permute-start(f32[328,128]{1,0:T(8,128)S(1)} %get-tuple-element.30), channel_id=1, source_target_pairs={{0,6},{1,7},{2,4},{3,5},{4,2},{5,3},{6,0},{7,1},{8,14},{9,15},{10,... | collective-permute-start | bytes 503816 | tf_op jit(solution)/shard_map/ppermute | solution.py:353
  4.4 9.1 %collective-permute-start.5 = (f32[328,128]{1,0:T(8,128)S(1)}, f32[328,128]{1,0:T(8,128)S(1)}, u32[]{:S(2)}, u32[]{:S(2)}) collective-permute-start(f32[328,128]{1,0:T(8,128)S(1)} %get-tuple-element.30), channel_id=1, source_target_pairs={{0,4},{1,5},{2,6},{3,7},{4,0},{5,1},{6,2},{7,3},{8,12},{9,13},{10,... | collective-permute-start | bytes 503816 | tf_op jit(solution)/shard_map/ppermute | solution.py:353
  4.9 5.1 %collective-permute-start.2 = (f32[72,128]{1,0:T(8,128)S(1)}, f32[72,128]{1,0:T(8,128)S(1)}, u32[]{:S(2)}, u32[]{:S(2)}) collective-permute-start(f32[72,128]{1,0:T(8,128)S(1)} %get-tuple-element.27), channel_id=1, source_target_pairs={{0,8},{16,24},{8,0},{24,16},{1,9},{17,25},{9,1},{25,17},{2,10},{18... | collective-permute-start | bytes 110600 | tf_op jit(solution)/shard_map/ppermute | solution.py:359
  4.9 7.0 %collective-permute-start.3 = (f32[72,128]{1,0:T(8,128)S(1)}, f32[72,128]{1,0:T(8,128)S(1)}, u32[]{:S(2)}, u32[]{:S(2)}) collective-permute-start(f32[72,128]{1,0:T(8,128)S(1)} %get-tuple-element.28), channel_id=1, source_target_pairs={{8,16},{16,8},{9,17},{17,9},{10,18},{18,10},{11,19},{19,11},{12,20... | collective-permute-start | bytes 110600 | tf_op jit(solution)/shard_map/ppermute | solution.py:359
  9.9 5.7 %collective-permute-start = (f32[328,128]{1,0:T(8,128)S(1)}, f32[328,128]{1,0:T(8,128)S(1)}, u32[]{:S(2)}, u32[]{:S(2)}) collective-permute-start(f32[328,128]{1,0:T(8,128)S(1)} %get-tuple-element.26.refs_0_.refs_4_.own_tile), channel_id=1, source_target_pairs={{0,1},{1,0},{2,3},{3,2},{4,5},{5,4},{6,7},{7,6},{8,9},{9,8},{10,11... | collective-permute-start | bytes 503816 | tf_op jit(solution)/shard_map/ppermute | solution.py:353
  12.1 3.6 %collective-permute-start.8 = (f32[328,128]{1,0:T(8,128)S(1)}, f32[328,128]{1,0:T(8,128)S(1)}, u32[]{:S(2)}, u32[]{:S(2)}) collective-permute-start(f32[328,128]{1,0:T(8,128)S(1)} %collective-permute-done.7.refs_3_.refs_7_), channel_id=1, source_target_pairs={{0,1},{1,0},{2,3},{3,2},{4,5},{5,4},{6,7},{7,6},{8,9},{9,8},{10,11... | collective-permute-start | bytes 503816 | tf_op jit(solution)/shard_map/ppermute | solution.py:353
  13.4 2.2 %collective-permute-start.6 = (f32[328,128]{1,0:T(8,128)S(1)}, f32[328,128]{1,0:T(8,128)S(1)}, u32[]{:S(2)}, u32[]{:S(2)}) collective-permute-start(f32[328,128]{1,0:T(8,128)S(1)} %collective-permute-done.5.refs_2_.refs_6_), channel_id=1, source_target_pairs={{0,1},{1,0},{2,3},{3,2},{4,5},{5,4},{6,7},{7,6},{8,9},{9,8},{10,11... | collective-permute-start | bytes 503816 | tf_op jit(solution)/shard_map/ppermute | solution.py:353
  13.4 2.2 %collective-permute-start.4 = (f32[328,128]{1,0:T(8,128)S(1)}, f32[328,128]{1,0:T(8,128)S(1)}, u32[]{:S(2)}, u32[]{:S(2)}) collective-permute-start(f32[328,128]{1,0:T(8,128)S(1)} %collective-permute-done.1.refs_1_.refs_5_), channel_id=1, source_target_pairs={{0,1},{1,0},{2,3},{3,2},{4,5},{5,4},{6,7},{7,6},{8,9},{9,8},{10,11... | collective-permute-start | bytes 503816 | tf_op jit(solution)/shard_map/ppermute | solution.py:353
  17.3 11.0 %collective-permute-start.11 = (f32[512,128]{1,0:T(8,128)S(1)}, f32[512,128]{1,0:T(8,128)S(1)}, u32[]{:S(2)}, u32[]{:S(2)}) collective-permute-start(f32[512,128]{1,0:T(8,128)S(1)} %get-tuple-element.37), channel_id=1, source_target_pairs={{0,8},{16,24},{8,0},{24,16},{1,9},{17,25},{9,1},{25,17},{2,10},{18... | collective-permute-start | bytes 786440 | tf_op jit(solution)/shard_map/ppermute | solution.py:359
  17.8 12.0 %collective-permute-start.9 = (f32[512,128]{1,0:T(8,128)S(1)}, f32[512,128]{1,0:T(8,128)S(1)}, u32[]{:S(2)}, u32[]{:S(2)}) collective-permute-start(f32[512,128]{1,0:T(8,128)S(1)} %get-tuple-element.32), channel_id=1, source_target_pairs={{8,16},{16,8},{9,17},{17,9},{10,18},{18,10},{11,19},{19,11},{12,20... | collective-permute-start | bytes 786440 | tf_op jit(solution)/shard_map/ppermute | solution.py:359
  23.9 4.3 %collective-permute-start.10 = (f32[128,128]{1,0:T(8,128)S(1)}, f32[128,128]{1,0:T(8,128)S(1)}, u32[]{:S(2)}, u32[]{:S(2)}) collective-permute-start(f32[128,128]{1,0:T(8,128)S(1)} %get-tuple-element.35.refs_2_.refs_5_), channel_id=1, source_target_pairs={{0,4},{1,5},{2,6},{3,7},{4,0},{5,1},{6,2},{7,3},{8,12},{9,13},{10,... | collective-permute-start | bytes 196616 | tf_op jit(solution)/shard_map/ppermute | solution.py:353
  31.5 1.4 %collective-permute-start.13 = (f32[256,128]{1,0:T(8,128)S(1)}, f32[256,128]{1,0:T(8,128)S(1)}, u32[]{:S(2)}, u32[]{:S(2)}) collective-permute-start(f32[256,128]{1,0:T(8,128)S(1)} %get-tuple-element.41), channel_id=1, source_target_pairs={{0,1},{1,0},{2,3},{3,2},{4,5},{5,4},{6,7},{7,6},{8,9},{9,8},{10,11... | collective-permute-start | bytes 393224 | tf_op jit(solution)/shard_map/ppermute | solution.py:353
  31.6 2.9 %collective-permute-start.15 = (f32[256,128]{1,0:T(8,128)S(1)}, f32[256,128]{1,0:T(8,128)S(1)}, u32[]{:S(2)}, u32[]{:S(2)}) collective-permute-start(f32[256,128]{1,0:T(8,128)S(1)} %get-tuple-element.43), channel_id=1, source_target_pairs={{0,1},{1,0},{2,3},{3,2},{4,5},{5,4},{6,7},{7,6},{8,9},{9,8},{10,11... | collective-permute-start | bytes 393224 | tf_op jit(solution)/shard_map/ppermute | solution.py:353
  32.1 3.0 %collective-permute-start.17 = (f32[256,128]{1,0:T(8,128)S(1)}, f32[256,128]{1,0:T(8,128)S(1)}, u32[]{:S(2)}, u32[]{:S(2)}) collective-permute-start(f32[256,128]{1,0:T(8,128)S(1)} %get-tuple-element.45), channel_id=1, source_target_pairs={{0,1},{1,0},{2,3},{3,2},{4,5},{5,4},{6,7},{7,6},{8,9},{9,8},{10,11... | collective-permute-start | bytes 393224 | tf_op jit(solution)/shard_map/ppermute | solution.py:353
  32.2 4.5 %collective-permute-start.12 = (f32[256,128]{1,0:T(8,128)S(1)}, f32[256,128]{1,0:T(8,128)S(1)}, u32[]{:S(2)}, u32[]{:S(2)}) collective-permute-start(f32[256,128]{1,0:T(8,128)S(1)} %get-tuple-element.39), channel_id=1, source_target_pairs={{0,1},{1,0},{2,3},{3,2},{4,5},{5,4},{6,7},{7,6},{8,9},{9,8},{10,11... | collective-permute-start | bytes 393224 | tf_op jit(solution)/shard_map/ppermute | solution.py:353
  32.9 5.8 %collective-permute-start.14 = (f32[256,128]{1,0:T(8,128)S(1)}, f32[256,128]{1,0:T(8,128)S(1)}, u32[]{:S(2)}, u32[]{:S(2)}) collective-permute-start(f32[256,128]{1,0:T(8,128)S(1)} %add.14), channel_id=1, source_target_pairs={{0,2},{1,3},{2,0},{3,1},{4,6},{5,7},{6,4},{7,5},{8,10},{9,11},{10,... | collective-permute-start | bytes 393224 | tf_op jit(solution)/shard_map/ppermute | solution.py:353
  34.5 8.1 %collective-permute-start.16 = (f32[256,128]{1,0:T(8,128)S(1)}, f32[256,128]{1,0:T(8,128)S(1)}, u32[]{:S(2)}, u32[]{:S(2)}) collective-permute-start(f32[256,128]{1,0:T(8,128)S(1)} %add.15), channel_id=1, source_target_pairs={{0,4},{1,5},{2,6},{3,7},{4,0},{5,1},{6,2},{7,3},{8,12},{9,13},{10,... | collective-permute-start | bytes 393224 | tf_op jit(solution)/shard_map/ppermute | solution.py:353
  35.1 7.6 %collective-permute-start.18 = (f32[256,128]{1,0:T(8,128)S(1)}, f32[256,128]{1,0:T(8,128)S(1)}, u32[]{:S(2)}, u32[]{:S(2)}) collective-permute-start(f32[256,128]{1,0:T(8,128)S(1)} %add.16), channel_id=1, source_target_pairs={{0,6},{1,7},{2,4},{3,5},{4,2},{5,3},{6,0},{7,1},{8,14},{9,15},{10,... | collective-permute-start | bytes 393224 | tf_op jit(solution)/shard_map/ppermute | solution.py:353

commit v5 on v4

--- a/solution.py
+++ b/solution.py
@@ -108,10 +108,6 @@
     return pl.BlockSpec((8, 128), lambda i: (tile, 0), memory_space=pltpu.SMEM)
 
 
-def smem_whole(size):
-    return pl.BlockSpec((size,), lambda i: (0,), memory_space=pltpu.SMEM)
-
-
 def call(kernel, outs, in_specs, scratch, cost, *args):
     outs = [((n, 128), jnp.float32) if isinstance(n, int) else n for n in outs]
     return pl.pallas_call(
@@ -126,6 +122,10 @@
     )(*args)
 
 
+def even_band():
+    return 1 - lax.axis_index("lat") % 2
+
+
 def rolled(value):
     return [pltpu.roll(value, 127, 1), value, pltpu.roll(value, 1, 1), pltpu.roll(value, 2, 1)]
 
@@ -159,7 +159,7 @@
 
 def assemble(levels, rows, blocks, adj, lat_w, lon_w, v, own, other, e1, e2, *scratch):
     tables, lat0, lon0, v1, sems = scratch
-    field, even = lax.axis_index("lon") // 4, 1 - lax.axis_index("lat") % 2
+    field, even = lax.axis_index("lon") // 4, even_band()
     per_field = 8 * levels
     sem = iter(range(16))
 
@@ -192,8 +192,8 @@
         each.wait()
 
 
-def rim_data(levels, me_ref, own_tile, lat_w, lon_w, e1, e2, v, after_this, pack, matrices1, matrices0):
-    even = me_ref[2] == 1
+def rim_data(levels, own_tile, lat_w, lon_w, e1, e2, v, after_this, pack, matrices1, matrices0):
+    even = even_band() == 1
     for i in range(8):
         pack[32 + 8 * i : 36 + 8 * i, :] = lat_w[pl.ds(i, 4, stride=8), :]
         pack[36 + 8 * i : 40 + 8 * i, :] = lon_w[pl.ds(i, 4, stride=8), :]
@@ -223,9 +223,9 @@
     matrices0[4 * levels : 8 * levels, :] = turned(four(0, 4))
 
 
-def spread_messages(levels, me_ref, messages, tables, acc, masks):
+def spread_messages(levels, messages, tables, acc, masks):
     per_field = 8 * levels
-    me, lat_start = me_ref[0], me_ref[1]
+    me, lat_start = lax.axis_index("lon"), 8 * lax.axis_index("lat")
     stay, back, on = lane_masks()
     for n, mask in enumerate((stay, back, jnp.zeros_like(stay), on)):
         masks[n] = mask
@@ -245,17 +245,17 @@
         lax.fori_loop(0, 8, row, 0, unroll=True)
 
 
-def first_spread_own(levels, me_ref, *refs):
+def first_spread_own(levels, *refs):
     messages, tables, (acc, masks) = refs[0:4], refs[4:8], refs[8:]
     acc[...] = jnp.zeros_like(acc)
-    spread_messages(levels, me_ref, messages, tables, acc, masks)
-
-
-def first_spread_other(levels, me_ref, *refs):
+    spread_messages(levels, messages, tables, acc, masks)
+
+
+def first_spread_other(levels, *refs):
     messages, tables, (before, acc, m1, m2, masks) = refs[0:4], refs[4:8], refs[8:]
     acc[...] = before[...]
-    spread_messages(levels, me_ref, messages, tables, acc, masks)
-    even = me_ref[2]
+    spread_messages(levels, messages, tables, acc, masks)
+    even = even_band()
 
     def write(out, part_row, count):
         for h in range(2):
@@ -280,15 +280,16 @@
     return jnp.dot(matrix, jnp.concatenate([high, high, low, low], axis=0), preferred_element_type=jnp.float32)
 
 
-def spread_half(levels, upper, me_ref, part, received, own_pack, y_pack, matrices, own_tab, y_tab, state, acc):
-    me, lat_start, at_start, at_end = me_ref[0], me_ref[1], me_ref[3], me_ref[4]
+def spread_half(levels, upper, part, received, own_pack, y_pack, matrices, own_tab, y_tab, state, acc):
+    me, band = lax.axis_index("lon"), lax.axis_index("lat")
+    lat_start, at_start, at_end = 8 * band, band == 0, band == lax.axis_size("lat") - 1
     slot = me // 4
     base = 8 * upper
 
     def exists(j):
         n = base + j
-        there = (n < 15) & ((at_start == 0) | (n >= 4)) if j < 4 else n < 15
-        return there & ((at_end == 0) | (n < 12)) if j >= 4 else there
+        there = (n < 15) & (~at_start | (n >= 4)) if j < 4 else n < 15
+        return there & (~at_end | (n < 12)) if j >= 4 else there
 
     for j in range(8):
         halves = []
@@ -324,21 +325,21 @@
             add_terms(sources, masked(prods, on, (2, 3)), acc, (((tau + 1) & 7) ^ me) * 22 + first)
 
 
-def second_spread_early(levels, me_ref, *refs):
+def second_spread_early(levels, *refs):
     (acc, state), refs = refs[-2:], refs[:-2]
-    spread_half(levels, me_ref[2], me_ref, *refs, state, acc)
-
-
-def second_spread_late(levels, me_ref, *refs):
+    spread_half(levels, even_band(), *refs, state, acc)
+
+
+def second_spread_late(levels, *refs):
     (before, *outs, state, acc), refs = refs[7:], refs[:7]
-    spread_half(levels, 1 - me_ref[2], me_ref, *refs, state, acc)
+    spread_half(levels, 1 - even_band(), *refs, state, acc)
     for q, out in enumerate(outs):
         rows = slice(q * 22 + 7, q * 22 + 15)
         out[...] = (acc[rows] + before[rows]).reshape(8 * levels, 128)
 
 
-def finish(levels, me_ref, own, pair, across, up, diagonal, matrices, out):
-    field = me_ref[0] // 4
+def finish(levels, own, pair, across, up, diagonal, matrices, out):
+    field = lax.axis_index("lon") // 4
     for i in range(8):
         rows = slice(i * levels, (i + 1) * levels)
         mine = own[rows, :] + pair[rows, :] + across[rows, :]
@@ -361,10 +362,6 @@
 
 def ring_body(adjoint_in, lat_weights, lon_weights, depart_rows, depart_blocks, vertical_inverse):
     fields, levels, lat_rows, points = adjoint_in.shape
-    me = lax.axis_index("lon")
-    band = lax.axis_index("lat")
-    count = lax.axis_size("lat")
-    info = jnp.stack([me, band * lat_rows, 1 - band % 2, band == 0, band == count - 1]).astype(jnp.int32)
     per_field = 8 * levels
     size = adjoint_in.size
     message = per_field + 64 + 8
@@ -387,10 +384,10 @@
         ],
         compiler_params=pltpu.CompilerParams(vmem_limit_bytes=VMEM_LIMIT),
     )(*(pltpu.with_memory_space_constraint(value, pltpu.HBM) for value in arguments))
-    far = {6: swap_lon(other, 6), 4: swap_lon(other, 4), 2: swap_lon(own, 2)}
+    far = {2: swap_lon(own, 2), 4: swap_lon(other, 4), 6: swap_lon(other, 6)}
     tile = pl.BlockSpec((8, 128), lambda i: (message // 8 - 1, 0), memory_space=pltpu.VMEM)
     e1, e2 = swap_lat(e1, 0), swap_lat(e2, 1)
-    far[2], e1, e2 = lax.optimization_barrier((far[2], e1, e2))
+    far[4], e1, e2 = lax.optimization_barrier((far[4], e1, e2))
     messages = [own, far[2], far[4], far[6]]
     messages = messages + [swap_lon(value, 1) for value in messages]
     table = smem_tile(message // 8 - 1)
@@ -399,20 +396,18 @@
     (part,) = call(
         functools.partial(first_spread_own, levels),
         [partial],
-        [smem_whole(5)] + [vmem((message, 128))] * 4 + [table] * 4,
+        [vmem((message, 128))] * 4 + [table] * 4,
         [masks],
         8 * size,
-        info,
         *messages[:4],
         *messages[:4],
     )
     part, m1, m2 = call(
         functools.partial(first_spread_other, levels),
         [partial, 16 * levels, 16 * levels],
-        [smem_whole(5)] + [vmem((message, 128))] * 4 + [table] * 4 + [vmem(partial[0], 3)],
+        [vmem((message, 128))] * 4 + [table] * 4 + [vmem(partial[0], 3)],
         [masks],
         8 * size,
-        info,
         *messages[4:],
         *messages[4:],
         part,
@@ -421,11 +416,10 @@
     pack, matrices1, matrices0 = call(
         functools.partial(rim_data, levels),
         [128, ((16 * levels, 128), jnp.bfloat16), ((8 * levels, 128), jnp.bfloat16)],
-        [smem_whole(5), tile, vmem((64, 128)), vmem((64, 128)), vmem((side, 128)), vmem((side, 128))]
+        [tile, vmem((64, 128)), vmem((64, 128)), vmem((side, 128)), vmem((side, 128))]
         + [vmem(vertical_inverse.shape, 4), vmem((8, levels, 128), 3)],
         [],
         size,
-        info,
         own,
         lat_w,
         lon_w,
@@ -435,7 +429,7 @@
         part,
     )
     y_pack = swap_lon(pack, 4)
-    half_specs = [smem_whole(5), vmem(partial[0], 3), vmem((16 * levels, 128)), vmem((128, 128)), vmem((128, 128))]
+    half_specs = [vmem(partial[0], 3), vmem((16 * levels, 128)), vmem((128, 128)), vmem((128, 128))]
     half_specs += [vmem((16 * levels, 128)), smem_tile(15), smem_tile(15)]
     spread_shape = ((8 * 22, levels, 128), jnp.float32)
     state = pltpu.VMEM((16, levels, 128), jnp.float32)
@@ -445,7 +439,7 @@
         half_specs,
         [state],
         8 * size,
-        *(info, part, r1, pack, y_pack, matrices1, pack, y_pack),
+        *(part, r1, pack, y_pack, matrices1, pack, y_pack),
     )
     pieces = call(
         functools.partial(second_spread_late, levels),
@@ -453,7 +447,7 @@
         half_specs + [vmem(spread_shape[0], 3)],
         [state, pltpu.VMEM(*spread_shape)],
         8 * size,
-        *(info, part, r2, pack, y_pack, matrices1, pack, y_pack, early),
+        *(part, r2, pack, y_pack, matrices1, pack, y_pack, early),
     )
     received = {}
     for bits in (6, 4, 2):
@@ -462,10 +456,9 @@
     (out,) = call(
         functools.partial(finish, levels),
         [fields * levels * 8],
-        [smem_whole(5)] + [vmem((8 * levels, 128))] * 6,
+        [vmem((8 * levels, 128))] * 6,
         [],
         size,
-        info,
         pieces[0],
         pair,
         received[2],

time: 44.3 us -> 41.3 us (0.932)
  waiting for transfers between devices: 13.5 us -> 10.9 us
  Pallas kernels: 10.7 us -> 9.48 us
  starting transfers between devices: 19.6 us -> 20.5 us
    ppermute x15, waiting for transfers between devices: 11.7 us -> 9.09 us  [swap_lon(): return lax.ppermute(value, 'lon', [(i, i ^ bits) for i in range(RING)])]
    pallas_call x6, Pallas kernels: 9.36 us -> 8.19 us  [call(): pl.pallas_call(kernel, grid=(1,), out_shape=[jax.ShapeDtypeStruct(*out) f...]
    ppermute x15, starting transfers between devices: 9.47 us -> 10.5 us  [swap_lon(): return lax.ppermute(value, 'lon', [(i, i ^ bits) for i in range(RING)])]
  transfers between devices with their start and end apart: 19 -> 19, of which waited for: 7 -> 5; matrix products, arithmetic and copies ran while one was open for 0% -> 0% of each run, Pallas kernels for 11% -> 10%
where the time goes in v5:
time: 41.3 us; the launch traced here: 41.2 us
  starting transfers between devices  20.5 us (50%)
  waiting for transfers between devices  10.9 us (26%)
  Pallas kernels  9.48 us (23%)
    ppermute x15, starting transfers between devices, swap_lon(): return lax.ppermute(value, 'lon', [(i, i ^ bits) for i in range(RING)])  10.5 us
    ppermute x4, starting transfers between devices, swap_lat(): return lax.ppermute(value, 'lat', pairs + [(b, a) for a, b in pairs])  9.96 us
    ppermute x15, waiting for transfers between devices, swap_lon(): return lax.ppermute(value, 'lon', [(i, i ^ bits) for i in range(RING)])  9.09 us
    pallas_call x6, Pallas kernels, call(): pl.pallas_call(kernel, grid=(1,), out_shape=[jax.ShapeDtypeStruct(*out) f...  8.19 us
    ppermute x4, waiting for transfers between devices, swap_lat(): return lax.ppermute(value, 'lat', pairs + [(b, a) for a, b in pairs])  1.84 us
    pallas_call x1, Pallas kernels, ring_body(): pl.pallas_call(functools.partial(assemble, levels), out_shape=[pltpu.VMEM...  1.29 us
  transfers between devices with their start and end apart: 19, of which 5 were waited for; matrix products, arithmetic and copies ran while one was open for 0% of the time, Pallas kernels for 10%

profile of v5, /device:TPU:8, one launch (start us, length us, event | category | flops | bytes accessed | tf_op | source)
XLA Modules:
  0.0 41.2 jit_solution(5191427892835913534)
XLA Ops:
  0.0 0.0 copy-start
  0.0 0.0 copy-start.2
  0.0 0.0 copy-start.1
  0.0 1.3 %shard_map.64 = (f32[328,128]{1,0:T(8,128)S(1)}, f32[328,128]{1,0:T(8,128)S(1)}, f32[72,128]{1,0:T(8,128)S(1)}, f32[72,128]{1,0:T(8,128)S(1)}) custom-call(s32[2,8]{1,0:T(2,128)} %bitcast.11, s32[2,8]{1,0:T(2,128)} %bitcast.12, f32[512,128]{1,0:T(8,128)} %bitcast.10, f32[64,128]{1,0:T(8,128)} %bitcast.6, f32[64,128]{1,0:T(8,128)} %bitcast.8, f32[2,8,32,32]{3,2,1,0:T(8,128)} %v.3), custom_call_target="tpu_custom_call" | custom-call | tf_op jit(solution)/shard_map/pallas_call | solution.py:373
  1.3 1.6 %collective-permute-start.3 = (f32[328,128]{1,0:T(8,128)S(1)}, f32[328,128]{1,0:T(8,128)S(1)}, u32[]{:S(2)}, u32[]{:S(2)}) collective-permute-start(f32[328,128]{1,0:T(8,128)S(1)} %get-tuple-element.27), channel_id=1, source_target_pairs={{0,4},{1,5},{2,6},{3,7},{4,0},{5,1},{6,2},{7,3},{8,12},{9,13},{10,... | collective-permute-start | bytes 503816 | tf_op jit(solution)/shard_map/ppermute | solution.py:354
  2.9 1.4 %collective-permute-start.7 = (f32[328,128]{1,0:T(8,128)S(1)}, f32[328,128]{1,0:T(8,128)S(1)}, u32[]{:S(2)}, u32[]{:S(2)}) collective-permute-start(f32[328,128]{1,0:T(8,128)S(1)} %get-tuple-element.27), channel_id=1, source_target_pairs={{0,6},{1,7},{2,4},{3,5},{4,2},{5,3},{6,0},{7,1},{8,14},{9,15},{10,... | collective-permute-start | bytes 503816 | tf_op jit(solution)/shard_map/ppermute | solution.py:354
  4.3 0.5 %collective-permute-start.1 = (f32[328,128]{1,0:T(8,128)S(1)}, f32[328,128]{1,0:T(8,128)S(1)}, u32[]{:S(2)}, u32[]{:S(2)}) collective-permute-start(f32[328,128]{1,0:T(8,128)S(1)} %get-tuple-element.26.refs_0_.refs_4_.own_tile), channel_id=1, source_target_pairs={{0,2},{1,3},{2,0},{3,1},{4,6},{5,7},{6,4},{7,5},{8,10},{9,11},{10,... | collective-permute-start | bytes 503816 | tf_op jit(solution)/shard_map/ppermute | solution.py:354
  4.9 0.0 collective-permute-start.4
  4.9 5.0 %collective-permute-start.5 = (f32[72,128]{1,0:T(8,128)S(1)}, f32[72,128]{1,0:T(8,128)S(1)}, u32[]{:S(2)}, u32[]{:S(2)}) collective-permute-start(f32[72,128]{1,0:T(8,128)S(1)} %get-tuple-element.29), channel_id=1, source_target_pairs={{8,16},{16,8},{9,17},{17,9},{10,18},{18,10},{11,19},{19,11},{12,20... | collective-permute-start | bytes 110600 | tf_op jit(solution)/shard_map/ppermute | solution.py:360
  9.9 0.0 collective-permute-done.4.e1
  9.9 0.1 collective-permute-start
  10.0 1.8 %collective-permute-done.5.e2 = f32[72,128]{1,0:T(8,128)S(1)} collective-permute-done((f32[72,128]{1,0:T(8,128)S(1)}, f32[72,128]{1,0:T(8,128)S(1)}, u32[]{:S(2)}, u32[]{:S(2)}) %collective-permute-start.5) | collective-permute-done | bytes 36896 | tf_op jit(solution)/shard_map/ppermute | solution.py:360
  11.8 0.0 collective-permute-done.3.refs_2_.refs_6_
  11.8 0.0 collective-permute-start.6
  11.9 0.0 collective-permute-done.7.refs_3_.refs_7_
  11.9 0.5 %collective-permute-start.8 = (f32[328,128]{1,0:T(8,128)S(1)}, f32[328,128]{1,0:T(8,128)S(1)}, u32[]{:S(2)}, u32[]{:S(2)}) collective-permute-start(f32[328,128]{1,0:T(8,128)S(1)} %collective-permute-done.7.refs_3_.refs_7_), channel_id=1, source_target_pairs={{0,1},{1,0},{2,3},{3,2},{4,5},{5,4},{6,7},{7,6},{8,9},{9,8},{10,11... | collective-permute-start | bytes 503816 | tf_op jit(solution)/shard_map/ppermute | solution.py:354
  12.4 0.0 collective-permute-done.1.refs_1_.refs_5_
  12.4 0.1 collective-permute-start.2
  12.4 1.6 %shard_map.65.refs_8_ = f32[30,32,128]{2,1,0:T(8,128)S(1)} custom-call(f32[328,128]{1,0:T(8,128)S(1)} %get-tuple-element.26.refs_0_.refs_4_.own_tile, f32[328,128]{1,0:T(8,128)S(1)} %collective-permute-done.1.refs_1_.refs_5_, f32[328,128]{1,0:T(8,128)S(1)} %collective-permute-done.3.refs_2_.refs_6_, f32[328,128]{1,0:T(8,128)S(1)} %collective-permute-done.7.refs_3_.refs_7_, ...), custom_call_target="tpu_custom_call" | custom-call | flops 524288 | bytes 524288 | tf_op jit(solution)/shard_map/pallas_call | solution.py:113
  14.0 0.0 collective-permute-done.refs_0_.refs_4_
  14.0 0.0 collective-permute-done.8.refs_3_.refs_7_
  14.0 0.0 collective-permute-done.6.refs_2_.refs_6_
  14.0 0.0 collective-permute-done.2.refs_1_.refs_5_
  14.1 1.6 %shard_map.66 = (f32[30,32,128]{2,1,0:T(8,128)S(1)}, f32[512,128]{1,0:T(8,128)S(1)}, f32[512,128]{1,0:T(8,128)S(1)}) custom-call(f32[328,128]{1,0:T(8,128)S(1)} %collective-permute-done.refs_0_.refs_4_, f32[328,128]{1,0:T(8,128)S(1)} %collective-permute-done.2.refs_1_.refs_5_, f32[328,128]{1,0:T(8,128)S(1)} %collective-permute-done.6.refs_2_.refs_6_, ...), custom_call_target="tpu_custom_call" | custom-call | flops 524288 | bytes 524288 | tf_op jit(solution)/shard_map/pallas_call | solution.py:113
  15.7 0.2 collective-permute-start.11
  15.8 4.8 %collective-permute-start.9 = (f32[512,128]{1,0:T(8,128)S(1)}, f32[512,128]{1,0:T(8,128)S(1)}, u32[]{:S(2)}, u32[]{:S(2)}) collective-permute-start(f32[512,128]{1,0:T(8,128)S(1)} %get-tuple-element.32), channel_id=1, source_target_pairs={{8,16},{16,8},{9,17},{17,9},{10,18},{18,10},{11,19},{19,11},{12,20... | collective-permute-start | bytes 786440 | tf_op jit(solution)/shard_map/ppermute | solution.py:360
  20.6 0.0 copy-done
  20.6 0.0 copy-done.2
  20.6 0.0 copy-done.1
  20.6 0.9 %shard_map.67 = (f32[128,128]{1,0:T(8,128)S(1)}, bf16[512,128]{1,0:T(8,128)(2,1)S(1)}, bf16[256,128]{1,0:T(8,128)(2,1)S(1)}) custom-call(f32[328,128]{1,0:T(8,128)S(1)} %get-tuple-element.26.refs_0_.refs_4_.own_tile, f32[64,128]{1,0:T(8,128)S(1)} %bitcast.7, f32[64,128]{1,0:T(8,128)S(1)} %bitcast.9, f32[72,128]{1,0:T(8,128)S(1)} %collective-permute-done.4.e1, ...), custom_call_target="tpu_custom_call" | custom-call | flops 65536 | bytes 65536 | tf_op jit(solution)/shard_map/pallas_call | solution.py:113
  21.6 1.6 %collective-permute-start.10 = (f32[128,128]{1,0:T(8,128)S(1)}, f32[128,128]{1,0:T(8,128)S(1)}, u32[]{:S(2)}, u32[]{:S(2)}) collective-permute-start(f32[128,128]{1,0:T(8,128)S(1)} %get-tuple-element.35.refs_2_.refs_5_), channel_id=1, source_target_pairs={{0,4},{1,5},{2,6},{3,7},{4,0},{5,1},{6,2},{7,3},{8,12},{9,13},{10,... | collective-permute-start | bytes 196616 | tf_op jit(solution)/shard_map/ppermute | solution.py:354
  23.1 2.7 %collective-permute-done.10.refs_3_.refs_6_ = f32[128,128]{1,0:T(8,128)S(1)} collective-permute-done((f32[128,128]{1,0:T(8,128)S(1)}, f32[128,128]{1,0:T(8,128)S(1)}, u32[]{:S(2)}, u32[]{:S(2)}) %collective-permute-start.10) | collective-permute-done | bytes 65568 | tf_op jit(solution)/shard_map/ppermute | solution.py:354
  25.9 0.0 collective-permute-done.11.refs_1_
  25.9 1.5 %shard_map.68.refs_7_ = f32[176,32,128]{2,1,0:T(8,128)S(1)} custom-call(f32[30,32,128]{2,1,0:T(8,128)S(1)} %get-tuple-element.31.after_this.refs_0_, f32[512,128]{1,0:T(8,128)S(1)} %collective-permute-done.11.refs_1_, f32[128,128]{1,0:T(8,128)S(1)} %get-tuple-element.35.refs_2_.refs_5_, f32[128,128]{1,0:T(8,128)S(1)} %collective-permute-done.10.refs_3_.refs_6_, ...), custom_call_target="tpu_custom_call" | custom-call | flops 524288 | bytes 524288 | tf_op jit(solution)/shard_map/pallas_call | solution.py:113
  27.4 0.0 collective-permute-done.9.refs_1_
  27.4 1.7 %shard_map.69 = (f32[256,128]{1,0:T(8,128)S(1)}, f32[256,128]{1,0:T(8,128)S(1)}, f32[256,128]{1,0:T(8,128)S(1)}, f32[256,128]{1,0:T(8,128)S(1)}, f32[256,128]{1,...) custom-call(f32[30,32,128]{2,1,0:T(8,128)S(1)} %get-tuple-element.31.after_this.refs_0_, ...), custom_call_target="tpu_custom_call" | custom-call | flops 524288 | bytes 524288 | tf_op jit(solution)/shard_map/pallas_call | solution.py:113
  29.1 0.1 collective-permute-start.13
  29.2 0.5 %collective-permute-start.15 = (f32[256,128]{1,0:T(8,128)S(1)}, f32[256,128]{1,0:T(8,128)S(1)}, u32[]{:S(2)}, u32[]{:S(2)}) collective-permute-start(f32[256,128]{1,0:T(8,128)S(1)} %get-tuple-element.43), channel_id=1, source_target_pairs={{0,1},{1,0},{2,3},{3,2},{4,5},{5,4},{6,7},{7,6},{8,9},{9,8},{10,11... | collective-permute-start | bytes 393224 | tf_op jit(solution)/shard_map/ppermute | solution.py:354
  29.7 0.1 collective-permute-start.17
  29.7 0.4 %collective-permute-start.12 = (f32[256,128]{1,0:T(8,128)S(1)}, f32[256,128]{1,0:T(8,128)S(1)}, u32[]{:S(2)}, u32[]{:S(2)}) collective-permute-start(f32[256,128]{1,0:T(8,128)S(1)} %get-tuple-element.39), channel_id=1, source_target_pairs={{0,1},{1,0},{2,3},{3,2},{4,5},{5,4},{6,7},{7,6},{8,9},{9,8},{10,11... | collective-permute-start | bytes 393224 | tf_op jit(solution)/shard_map/ppermute | solution.py:354
  30.2 0.3 collective-permute-done.13
  30.5 1.6 %collective-permute-start.14 = (f32[256,128]{1,0:T(8,128)S(1)}, f32[256,128]{1,0:T(8,128)S(1)}, u32[]{:S(2)}, u32[]{:S(2)}) collective-permute-start(f32[256,128]{1,0:T(8,128)S(1)} %add.9), channel_id=1, source_target_pairs={{0,2},{1,3},{2,0},{3,1},{4,6},{5,7},{6,4},{7,5},{8,10},{9,11},{10,... | collective-permute-start | bytes 393224 | tf_op jit(solution)/shard_map/ppermute | solution.py:354
  32.1 0.0 collective-permute-done.15
  32.1 1.6 %collective-permute-start.16 = (f32[256,128]{1,0:T(8,128)S(1)}, f32[256,128]{1,0:T(8,128)S(1)}, u32[]{:S(2)}, u32[]{:S(2)}) collective-permute-start(f32[256,128]{1,0:T(8,128)S(1)} %add.10), channel_id=1, source_target_pairs={{0,4},{1,5},{2,6},{3,7},{4,0},{5,1},{6,2},{7,3},{8,12},{9,13},{10,... | collective-permute-start | bytes 393224 | tf_op jit(solution)/shard_map/ppermute | solution.py:354
  33.7 0.0 collective-permute-done.17
  33.7 0.6 %collective-permute-start.18 = (f32[256,128]{1,0:T(8,128)S(1)}, f32[256,128]{1,0:T(8,128)S(1)}, u32[]{:S(2)}, u32[]{:S(2)}) collective-permute-start(f32[256,128]{1,0:T(8,128)S(1)} %add.11), channel_id=1, source_target_pairs={{0,6},{1,7},{2,4},{3,5},{4,2},{5,3},{6,0},{7,1},{8,14},{9,15},{10,... | collective-permute-start | bytes 393224 | tf_op jit(solution)/shard_map/ppermute | solution.py:354
  34.3 0.0 collective-permute-done.12.pair
  34.3 2.1 %collective-permute-done.14.across = f32[256,128]{1,0:T(8,128)S(1)} collective-permute-done((f32[256,128]{1,0:T(8,128)S(1)}, f32[256,128]{1,0:T(8,128)S(1)}, u32[]{:S(2)}, u32[]{:S(2)}) %collective-permute-start.14) | collective-permute-done | bytes 131104 | tf_op jit(solution)/shard_map/ppermute | solution.py:354
  36.3 3.9 %collective-permute-done.16.up = f32[256,128]{1,0:T(8,128)S(1)} collective-permute-done((f32[256,128]{1,0:T(8,128)S(1)}, f32[256,128]{1,0:T(8,128)S(1)}, u32[]{:S(2)}, u32[]{:S(2)}) %collective-permute-start.16) | collective-permute-done | bytes 131104 | tf_op jit(solution)/shard_map/ppermute | solution.py:354
  40.2 0.0 collective-permute-done.18.diagonal
  40.2 0.9 %shard_map.70 = f32[512,128]{1,0:T(8,128)} custom-call(f32[256,128]{1,0:T(8,128)S(1)} %get-tuple-element.38.own, f32[256,128]{1,0:T(8,128)S(1)} %collective-permute-done.12.pair, f32[256,128]{1,0:T(8,128)S(1)} %collective-permute-done.14.across, f32[256,128]{1,0:T(8,128)S(1)} %collective-permute-done.16.up, f32[256,128]{1,0:T(8,128)S(1)} %collective-permute-done.18.diagonal, ...), custom_call_target="tpu_custom_call" | custom-call | flops 65536 | bytes 65536 | tf_op jit(solution)/shard_map/pallas_call | solution.py:113
  (3 shorter events, 0.0 us)
Async XLA Ops:
  0.0 20.6 %copy-start = (f32[2,8,32,32]{3,2,1,0:T(8,128)S(1)}, f32[2,8,32,32]{3,2,1,0:T(8,128)}, u32[]{:S(2)}) copy-start(f32[2,8,32,32]{3,2,1,0:T(8,128)} %v.3) | copy-start | bytes 196612
  0.0 20.6 %copy-start.2 = (f32[2,4,8,128]{3,2,1,0:T(8,128)S(1)}, f32[2,4,8,128]{3,2,1,0:T(8,128)}, u32[]{:S(2)}) copy-start(f32[2,4,8,128]{3,2,1,0:T(8,128)} %param.8) | copy-start | bytes 98308
  0.0 20.6 %copy-start.1 = (f32[2,4,8,128]{3,2,1,0:T(8,128)S(1)}, f32[2,4,8,128]{3,2,1,0:T(8,128)}, u32[]{:S(2)}) copy-start(f32[2,4,8,128]{3,2,1,0:T(8,128)} %param.7) | copy-start | bytes 98308
  1.3 10.5 %collective-permute-start.3 = (f32[328,128]{1,0:T(8,128)S(1)}, f32[328,128]{1,0:T(8,128)S(1)}, u32[]{:S(2)}, u32[]{:S(2)}) collective-permute-start(f32[328,128]{1,0:T(8,128)S(1)} %get-tuple-element.27), channel_id=1, source_target_pairs={{0,4},{1,5},{2,6},{3,7},{4,0},{5,1},{6,2},{7,3},{8,12},{9,13},{10,... | collective-permute-start | bytes 503816 | tf_op jit(solution)/shard_map/ppermute | solution.py:354
  2.9 9.0 %collective-permute-start.7 = (f32[328,128]{1,0:T(8,128)S(1)}, f32[328,128]{1,0:T(8,128)S(1)}, u32[]{:S(2)}, u32[]{:S(2)}) collective-permute-start(f32[328,128]{1,0:T(8,128)S(1)} %get-tuple-element.27), channel_id=1, source_target_pairs={{0,6},{1,7},{2,4},{3,5},{4,2},{5,3},{6,0},{7,1},{8,14},{9,15},{10,... | collective-permute-start | bytes 503816 | tf_op jit(solution)/shard_map/ppermute | solution.py:354
  4.3 8.0 %collective-permute-start.1 = (f32[328,128]{1,0:T(8,128)S(1)}, f32[328,128]{1,0:T(8,128)S(1)}, u32[]{:S(2)}, u32[]{:S(2)}) collective-permute-start(f32[328,128]{1,0:T(8,128)S(1)} %get-tuple-element.26.refs_0_.refs_4_.own_tile), channel_id=1, source_target_pairs={{0,2},{1,3},{2,0},{3,1},{4,6},{5,7},{6,4},{7,5},{8,10},{9,11},{10,... | collective-permute-start | bytes 503816 | tf_op jit(solution)/shard_map/ppermute | solution.py:354
  4.9 5.1 %collective-permute-start.4 = (f32[72,128]{1,0:T(8,128)S(1)}, f32[72,128]{1,0:T(8,128)S(1)}, u32[]{:S(2)}, u32[]{:S(2)}) collective-permute-start(f32[72,128]{1,0:T(8,128)S(1)} %get-tuple-element.28), channel_id=1, source_target_pairs={{0,8},{16,24},{8,0},{24,16},{1,9},{17,25},{9,1},{25,17},{2,10},{18... | collective-permute-start | bytes 110600 | tf_op jit(solution)/shard_map/ppermute | solution.py:360
  4.9 7.0 %collective-permute-start.5 = (f32[72,128]{1,0:T(8,128)S(1)}, f32[72,128]{1,0:T(8,128)S(1)}, u32[]{:S(2)}, u32[]{:S(2)}) collective-permute-start(f32[72,128]{1,0:T(8,128)S(1)} %get-tuple-element.29), channel_id=1, source_target_pairs={{8,16},{16,8},{9,17},{17,9},{10,18},{18,10},{11,19},{19,11},{12,20... | collective-permute-start | bytes 110600 | tf_op jit(solution)/shard_map/ppermute | solution.py:360
  9.9 4.1 %collective-permute-start = (f32[328,128]{1,0:T(8,128)S(1)}, f32[328,128]{1,0:T(8,128)S(1)}, u32[]{:S(2)}, u32[]{:S(2)}) collective-permute-start(f32[328,128]{1,0:T(8,128)S(1)} %get-tuple-element.26.refs_0_.refs_4_.own_tile), channel_id=1, source_target_pairs={{0,1},{1,0},{2,3},{3,2},{4,5},{5,4},{6,7},{7,6},{8,9},{9,8},{10,11... | collective-permute-start | bytes 503816 | tf_op jit(solution)/shard_map/ppermute | solution.py:354
  11.8 2.2 %collective-permute-start.6 = (f32[328,128]{1,0:T(8,128)S(1)}, f32[328,128]{1,0:T(8,128)S(1)}, u32[]{:S(2)}, u32[]{:S(2)}) collective-permute-start(f32[328,128]{1,0:T(8,128)S(1)} %collective-permute-done.3.refs_2_.refs_6_), channel_id=1, source_target_pairs={{0,1},{1,0},{2,3},{3,2},{4,5},{5,4},{6,7},{7,6},{8,9},{9,8},{10,11... | collective-permute-start | bytes 503816 | tf_op jit(solution)/shard_map/ppermute | solution.py:354
  11.9 2.2 %collective-permute-start.8 = (f32[328,128]{1,0:T(8,128)S(1)}, f32[328,128]{1,0:T(8,128)S(1)}, u32[]{:S(2)}, u32[]{:S(2)}) collective-permute-start(f32[328,128]{1,0:T(8,128)S(1)} %collective-permute-done.7.refs_3_.refs_7_), channel_id=1, source_target_pairs={{0,1},{1,0},{2,3},{3,2},{4,5},{5,4},{6,7},{7,6},{8,9},{9,8},{10,11... | collective-permute-start | bytes 503816 | tf_op jit(solution)/shard_map/ppermute | solution.py:354
  12.4 1.7 %collective-permute-start.2 = (f32[328,128]{1,0:T(8,128)S(1)}, f32[328,128]{1,0:T(8,128)S(1)}, u32[]{:S(2)}, u32[]{:S(2)}) collective-permute-start(f32[328,128]{1,0:T(8,128)S(1)} %collective-permute-done.1.refs_1_.refs_5_), channel_id=1, source_target_pairs={{0,1},{1,0},{2,3},{3,2},{4,5},{5,4},{6,7},{7,6},{8,9},{9,8},{10,11... | collective-permute-start | bytes 503816 | tf_op jit(solution)/shard_map/ppermute | solution.py:354
  15.7 10.2 %collective-permute-start.11 = (f32[512,128]{1,0:T(8,128)S(1)}, f32[512,128]{1,0:T(8,128)S(1)}, u32[]{:S(2)}, u32[]{:S(2)}) collective-permute-start(f32[512,128]{1,0:T(8,128)S(1)} %get-tuple-element.37), channel_id=1, source_target_pairs={{0,8},{16,24},{8,0},{24,16},{1,9},{17,25},{9,1},{25,17},{2,10},{18... | collective-permute-start | bytes 786440 | tf_op jit(solution)/shard_map/ppermute | solution.py:360
  15.8 11.6 %collective-permute-start.9 = (f32[512,128]{1,0:T(8,128)S(1)}, f32[512,128]{1,0:T(8,128)S(1)}, u32[]{:S(2)}, u32[]{:S(2)}) collective-permute-start(f32[512,128]{1,0:T(8,128)S(1)} %get-tuple-element.32), channel_id=1, source_target_pairs={{8,16},{16,8},{9,17},{17,9},{10,18},{18,10},{11,19},{19,11},{12,20... | collective-permute-start | bytes 786440 | tf_op jit(solution)/shard_map/ppermute | solution.py:360
  21.6 4.3 %collective-permute-start.10 = (f32[128,128]{1,0:T(8,128)S(1)}, f32[128,128]{1,0:T(8,128)S(1)}, u32[]{:S(2)}, u32[]{:S(2)}) collective-permute-start(f32[128,128]{1,0:T(8,128)S(1)} %get-tuple-element.35.refs_2_.refs_5_), channel_id=1, source_target_pairs={{0,4},{1,5},{2,6},{3,7},{4,0},{5,1},{6,2},{7,3},{8,12},{9,13},{10,... | collective-permute-start | bytes 196616 | tf_op jit(solution)/shard_map/ppermute | solution.py:354
  29.1 1.4 %collective-permute-start.13 = (f32[256,128]{1,0:T(8,128)S(1)}, f32[256,128]{1,0:T(8,128)S(1)}, u32[]{:S(2)}, u32[]{:S(2)}) collective-permute-start(f32[256,128]{1,0:T(8,128)S(1)} %get-tuple-element.41), channel_id=1, source_target_pairs={{0,1},{1,0},{2,3},{3,2},{4,5},{5,4},{6,7},{7,6},{8,9},{9,8},{10,11... | collective-permute-start | bytes 393224 | tf_op jit(solution)/shard_map/ppermute | solution.py:354
  29.2 2.9 %collective-permute-start.15 = (f32[256,128]{1,0:T(8,128)S(1)}, f32[256,128]{1,0:T(8,128)S(1)}, u32[]{:S(2)}, u32[]{:S(2)}) collective-permute-start(f32[256,128]{1,0:T(8,128)S(1)} %get-tuple-element.43), channel_id=1, source_target_pairs={{0,1},{1,0},{2,3},{3,2},{4,5},{5,4},{6,7},{7,6},{8,9},{9,8},{10,11... | collective-permute-start | bytes 393224 | tf_op jit(solution)/shard_map/ppermute | solution.py:354
  29.7 4.0 %collective-permute-start.17 = (f32[256,128]{1,0:T(8,128)S(1)}, f32[256,128]{1,0:T(8,128)S(1)}, u32[]{:S(2)}, u32[]{:S(2)}) collective-permute-start(f32[256,128]{1,0:T(8,128)S(1)} %get-tuple-element.45), channel_id=1, source_target_pairs={{0,1},{1,0},{2,3},{3,2},{4,5},{5,4},{6,7},{7,6},{8,9},{9,8},{10,11... | collective-permute-start | bytes 393224 | tf_op jit(solution)/shard_map/ppermute | solution.py:354
  29.7 4.5 %collective-permute-start.12 = (f32[256,128]{1,0:T(8,128)S(1)}, f32[256,128]{1,0:T(8,128)S(1)}, u32[]{:S(2)}, u32[]{:S(2)}) collective-permute-start(f32[256,128]{1,0:T(8,128)S(1)} %get-tuple-element.39), channel_id=1, source_target_pairs={{0,1},{1,0},{2,3},{3,2},{4,5},{5,4},{6,7},{7,6},{8,9},{9,8},{10,11... | collective-permute-start | bytes 393224 | tf_op jit(solution)/shard_map/ppermute | solution.py:354
  30.5 5.8 %collective-permute-start.14 = (f32[256,128]{1,0:T(8,128)S(1)}, f32[256,128]{1,0:T(8,128)S(1)}, u32[]{:S(2)}, u32[]{:S(2)}) collective-permute-start(f32[256,128]{1,0:T(8,128)S(1)} %add.9), channel_id=1, source_target_pairs={{0,2},{1,3},{2,0},{3,1},{4,6},{5,7},{6,4},{7,5},{8,10},{9,11},{10,... | collective-permute-start | bytes 393224 | tf_op jit(solution)/shard_map/ppermute | solution.py:354
  32.1 8.1 %collective-permute-start.16 = (f32[256,128]{1,0:T(8,128)S(1)}, f32[256,128]{1,0:T(8,128)S(1)}, u32[]{:S(2)}, u32[]{:S(2)}) collective-permute-start(f32[256,128]{1,0:T(8,128)S(1)} %add.10), channel_id=1, source_target_pairs={{0,4},{1,5},{2,6},{3,7},{4,0},{5,1},{6,2},{7,3},{8,12},{9,13},{10,... | collective-permute-start | bytes 393224 | tf_op jit(solution)/shard_map/ppermute | solution.py:354
  33.7 6.5 %collective-permute-start.18 = (f32[256,128]{1,0:T(8,128)S(1)}, f32[256,128]{1,0:T(8,128)S(1)}, u32[]{:S(2)}, u32[]{:S(2)}) collective-permute-start(f32[256,128]{1,0:T(8,128)S(1)} %add.11), channel_id=1, source_target_pairs={{0,6},{1,7},{2,4},{3,5},{4,2},{5,3},{6,0},{7,1},{8,14},{9,15},{10,... | collective-permute-start | bytes 393224 | tf_op jit(solution)/shard_map/ppermute | solution.py:354

commit v6 on v5

--- a/solution.py
+++ b/solution.py
@@ -104,10 +104,6 @@
     return pl.BlockSpec(shape, lambda i: (0,) * rank, memory_space=pltpu.VMEM)
 
 
-def smem_tile(tile):
-    return pl.BlockSpec((8, 128), lambda i: (tile, 0), memory_space=pltpu.SMEM)
-
-
 def call(kernel, outs, in_specs, scratch, cost, *args):
     outs = [((n, 128), jnp.float32) if isinstance(n, int) else n for n in outs]
     return pl.pallas_call(
@@ -158,26 +154,27 @@
 
 
 def assemble(levels, rows, blocks, adj, lat_w, lon_w, v, own, other, e1, e2, *scratch):
-    tables, lat0, lon0, v1, sems = scratch
+    tables, lat_all, lon_all, v1, sems = scratch
     field, even = lax.axis_index("lon") // 4, even_band()
     per_field = 8 * levels
-    sem = iter(range(16))
+    sem = iter(range(7))
 
     def copy(source, target):
         return pltpu.make_async_copy(source, target, sems.at[next(sem)])
 
     small = [copy(rows, tables.at[0]), copy(blocks, tables.at[1])]
-    small += [copy(lat_w.at[pl.ds(0, 32)], lat0), copy(lon_w.at[pl.ds(0, 32)], lon0), copy(v.at[1], v1)]
+    small += [copy(lat_w, lat_all), copy(lon_w, lon_all), copy(v.at[1], v1)]
     large = []
     for out, which in ((own, field), (other, 1 - field)):
         large.append(copy(adj.at[pl.ds(pl.multiple_of(which * per_field, per_field), per_field)], out.at[pl.ds(0, per_field)]))
-        large.append(copy(lat_w.at[pl.ds(32, 32)], out.at[pl.ds(per_field, 32)]))
-        large.append(copy(lon_w.at[pl.ds(32, 32)], out.at[pl.ds(per_field + 32, 32)]))
     for each in small + large:
         each.start()
     for each in small:
         each.wait()
     table = jnp.concatenate([tables[0], tables[1], tables[0], tables[1]], axis=0).astype(jnp.float32)
+    for out in (own, other):
+        out[per_field : per_field + 32, :] = lat_all[32:64, :]
+        out[per_field + 32 : per_field + 64, :] = lon_all[32:64, :]
     for out, first in ((own, per_field + 64), (other, per_field + 64), (e1, 32 + levels), (e2, 32 + levels)):
         out[first : first + 8, 0:8] = table
     low = jnp.concatenate([v1[j] for j in range(4)], axis=1)
@@ -185,8 +182,8 @@
     for out, takes_high in ((e1, even == 1), (e2, even == 0)):
         first = jnp.where(takes_high, 4, 0)
         for i in range(4):
-            out[8 * i : 8 * i + 4, :] = lat0[pl.ds(first + i, 4, stride=8), :]
-            out[8 * i + 4 : 8 * i + 8, :] = lon0[pl.ds(first + i, 4, stride=8), :]
+            out[8 * i : 8 * i + 4, :] = lat_all[pl.ds(first + i, 4, stride=8), :]
+            out[8 * i + 4 : 8 * i + 8, :] = lon_all[pl.ds(first + i, 4, stride=8), :]
         out[32 : 32 + levels, :] = jnp.where(takes_high, high, low)
     for each in large:
         each.wait()
@@ -223,55 +220,58 @@
     matrices0[4 * levels : 8 * levels, :] = turned(four(0, 4))
 
 
-def spread_messages(levels, messages, tables, acc, masks):
+def to_scalars(sources, target, sems):
+    copies = [pltpu.make_async_copy(source, target.at[n], sems.at[n]) for n, source in enumerate(sources)]
+    for copy in copies:
+        copy.start()
+    return copies
+
+
+def first_spread(levels, count, *refs):
+    messages, refs = refs[:count], refs[count:]
+    (*refs, masks, tables, sems) = refs
     per_field = 8 * levels
     me, lat_start = lax.axis_index("lon"), 8 * lax.axis_index("lat")
+    copies = to_scalars([message.at[pl.ds(per_field + 64, 8)] for message in messages], tables, sems)
+    if len(refs) == 1:
+        (acc,) = refs
+        acc[...] = jnp.zeros_like(acc)
+    else:
+        before, acc, *out = refs
+        acc[...] = before[...]
     stay, back, on = lane_masks()
     for n, mask in enumerate((stay, back, jnp.zeros_like(stay), on)):
         masks[n] = mask
-    for message, table in zip(messages, tables):
-
-        def row(i, _, message=message, table=table):
-            first = table[1, i].astype(jnp.int32) - lat_start + LOW
-            tau = table[3, i].astype(jnp.int32)
+    for copy in copies:
+        copy.wait()
+    for at, message in enumerate(messages):
+        for i in range(8):
+            first = tables[at, 1, i].astype(jnp.int32) - lat_start + LOW
+            tau = tables[at, 3, i].astype(jnp.int32)
             delta = (tau - me) & 3
             block = (tau + jnp.where(delta == 1, 7, jnp.where(delta == 3, 1, 0))) & 7
             weights = message[pl.ds(per_field + i, 8, stride=8), :]
             terms = masked(products(weights), masks[delta], range(NODES))
             sources = [rolled(message[pl.ds(8 * kk + i, 8, stride=8), :]) for kk in range(0, levels, 8)]
             add_terms(sources, terms, acc, (block // 4) * 15 + first)
-            return 0
-
-        lax.fori_loop(0, 8, row, 0, unroll=True)
-
-
-def first_spread_own(levels, *refs):
-    messages, tables, (acc, masks) = refs[0:4], refs[4:8], refs[8:]
-    acc[...] = jnp.zeros_like(acc)
-    spread_messages(levels, messages, tables, acc, masks)
-
-
-def first_spread_other(levels, *refs):
-    messages, tables, (before, acc, m1, m2, masks) = refs[0:4], refs[4:8], refs[8:]
-    acc[...] = before[...]
-    spread_messages(levels, messages, tables, acc, masks)
+    if len(refs) < 4:
+        return
     even = even_band()
 
-    def write(out, part_row, count):
+    def write(to, part_row, rows):
         for h in range(2):
-            out[h * 8 * levels : (h * 8 + count) * levels, :] = acc[
-                h * 15 + part_row : h * 15 + part_row + count
-            ].reshape(count * levels, 128)
-
-    @pl.when(even == 1)
-    def _():
-        write(m1, 7, 8)
-        write(m2, 0, 6)
-
-    @pl.when(even == 0)
-    def _():
-        write(m2, 7, 8)
-        write(m1, 0, 6)
+            value = acc[h * 15 + part_row : h * 15 + part_row + rows]
+            to[h * 8 * levels : (h * 8 + rows) * levels, :] = value.reshape(rows * levels, 128)
+
+    for to, is_upper in zip(out, (even == 1, even == 0)):
+
+        @pl.when(is_upper)
+        def _(to=to):
+            write(to, 7, 8)
+
+        @pl.when(~is_upper)
+        def _(to=to):
+            write(to, 0, 6)
 
 
 def vertical(matrix, column):
@@ -280,11 +280,12 @@
     return jnp.dot(matrix, jnp.concatenate([high, high, low, low], axis=0), preferred_element_type=jnp.float32)
 
 
-def spread_half(levels, upper, part, received, own_pack, y_pack, matrices, own_tab, y_tab, state, acc):
+def spread_half(levels, upper, part, received, own_pack, y_pack, matrices, state, tables, sems, acc):
     me, band = lax.axis_index("lon"), lax.axis_index("lat")
     lat_start, at_start, at_end = 8 * band, band == 0, band == lax.axis_size("lat") - 1
     slot = me // 4
     base = 8 * upper
+    copies = to_scalars([pack.at[pl.ds(120, 8)] for pack in (own_pack, y_pack)], tables, sems)
 
     def exists(j):
         n = base + j
@@ -309,14 +310,16 @@
     for q in range(8):
         acc[q * 22 + 7 : q * 22 + 15] = jnp.zeros((8, levels, 128), jnp.float32)
     stay, back, on = lane_masks()
+    for copy in copies:
+        copy.wait()
     for j in range(8):
         n = base + j
         there = exists(j)
         at = pl.ds(pl.multiple_of(8 * n, 8), 8)
         for h in range(2):
             mine = slot == h
-            tau = jnp.where(there, jnp.where(mine, own_tab[2, n], y_tab[2, n]).astype(jnp.int32), 0)
-            first = jnp.where(mine, own_tab[0, n], y_tab[0, n]).astype(jnp.int32) - lat_start + 7
+            tau = jnp.where(there, jnp.where(mine, tables[0, 2, n], tables[1, 2, n]).astype(jnp.int32), 0)
+            first = jnp.where(mine, tables[0, 0, n], tables[1, 0, n]).astype(jnp.int32) - lat_start + 7
             first = jnp.where(there, first, 7)
             prods = products(jnp.where(there, jnp.where(mine, own_pack[at, :], y_pack[at, :]), 0.0))
             sources = [rolled(state[h * 8 + j, kk : kk + 8, :]) for kk in range(0, levels, 8)]
@@ -326,19 +329,19 @@
 
 
 def second_spread_early(levels, *refs):
-    (acc, state), refs = refs[-2:], refs[:-2]
-    spread_half(levels, even_band(), *refs, state, acc)
+    (*refs, acc, state, tables, sems) = refs
+    spread_half(levels, even_band(), *refs, state, tables, sems, acc)
 
 
 def second_spread_late(levels, *refs):
-    (before, *outs, state, acc), refs = refs[7:], refs[:7]
-    spread_half(levels, 1 - even_band(), *refs, state, acc)
+    refs, before, outs, (state, tables, sems, acc) = refs[:5], refs[5], refs[6:14], refs[14:]
+    spread_half(levels, 1 - even_band(), *refs, state, tables, sems, acc)
     for q, out in enumerate(outs):
         rows = slice(q * 22 + 7, q * 22 + 15)
         out[...] = (acc[rows] + before[rows]).reshape(8 * levels, 128)
 
 
-def finish(levels, own, pair, across, up, diagonal, matrices, out):
+def finish(levels, own, diagonal, across, up, pair, matrices, out):
     field = lax.axis_index("lon") // 4
     for i in range(8):
         rows = slice(i * levels, (i + 1) * levels)
@@ -377,41 +380,37 @@
         out_specs=[pl.BlockSpec(memory_space=pltpu.VMEM)] * 4,
         scratch_shapes=[
             pltpu.VMEM((2, 2, 8), jnp.int32),
-            pltpu.VMEM((32, points), jnp.float32),
-            pltpu.VMEM((32, points), jnp.float32),
+            pltpu.VMEM((64, points), jnp.float32),
+            pltpu.VMEM((64, points), jnp.float32),
             pltpu.VMEM((8, levels, levels), jnp.float32),
-            pltpu.SemaphoreType.DMA((16,)),
+            pltpu.SemaphoreType.DMA((7,)),
         ],
         compiler_params=pltpu.CompilerParams(vmem_limit_bytes=VMEM_LIMIT),
     )(*(pltpu.with_memory_space_constraint(value, pltpu.HBM) for value in arguments))
     far = {2: swap_lon(own, 2), 4: swap_lon(other, 4), 6: swap_lon(other, 6)}
     tile = pl.BlockSpec((8, 128), lambda i: (message // 8 - 1, 0), memory_space=pltpu.VMEM)
     e1, e2 = swap_lat(e1, 0), swap_lat(e2, 1)
-    far[4], e1, e2 = lax.optimization_barrier((far[4], e1, e2))
-    messages = [own, far[2], far[4], far[6]]
-    messages = messages + [swap_lon(value, 1) for value in messages]
-    table = smem_tile(message // 8 - 1)
-    masks = pltpu.VMEM((4, 8, 128), jnp.float32)
     partial = ((30, levels, 128), jnp.float32)
-    (part,) = call(
-        functools.partial(first_spread_own, levels),
-        [partial],
-        [vmem((message, 128))] * 4 + [table] * 4,
-        [masks],
-        8 * size,
-        *messages[:4],
-        *messages[:4],
-    )
-    part, m1, m2 = call(
-        functools.partial(first_spread_other, levels),
-        [partial, 16 * levels, 16 * levels],
-        [vmem((message, 128))] * 4 + [table] * 4 + [vmem(partial[0], 3)],
-        [masks],
-        8 * size,
-        *messages[4:],
-        *messages[4:],
-        part,
-    )
+
+    def spread(those, *before, outs=()):
+        count = len(those)
+        scratch = [pltpu.VMEM((4, 8, 128), jnp.float32), pltpu.SMEM((count, 8, 128), jnp.float32)]
+        return call(
+            functools.partial(first_spread, levels, count),
+            [partial, *outs],
+            [vmem((message, 128))] * count + [vmem(partial[0], 3)] * len(before),
+            scratch + [pltpu.SemaphoreType.DMA((count,))],
+            4 * size,
+            *those,
+            *before,
+        )
+
+    (part,) = spread([own])
+    far[4], part, e1 = lax.optimization_barrier((far[4], part, e1))
+    far[6], e2 = lax.optimization_barrier((far[6], e2))
+    (part,) = spread([far[4], far[6], far[2]], part)
+    others = [swap_lon(value, 1) for value in (own, far[4], far[6], far[2])]
+    part, m1, m2 = spread(others, part, outs=(16 * levels, 16 * levels))
     r1, r2 = swap_lat(m1, 0), swap_lat(m2, 1)
     pack, matrices1, matrices0 = call(
         functools.partial(rim_data, levels),
@@ -430,24 +429,24 @@
     )
     y_pack = swap_lon(pack, 4)
     half_specs = [vmem(partial[0], 3), vmem((16 * levels, 128)), vmem((128, 128)), vmem((128, 128))]
-    half_specs += [vmem((16 * levels, 128)), smem_tile(15), smem_tile(15)]
+    half_specs += [vmem((16 * levels, 128))]
     spread_shape = ((8 * 22, levels, 128), jnp.float32)
-    state = pltpu.VMEM((16, levels, 128), jnp.float32)
+    scratch = [pltpu.VMEM((16, levels, 128), jnp.float32), pltpu.SMEM((2, 8, 128), jnp.float32), pltpu.SemaphoreType.DMA((2,))]
     (early,) = call(
         functools.partial(second_spread_early, levels),
         [spread_shape],
         half_specs,
-        [state],
+        scratch,
         8 * size,
-        *(part, r1, pack, y_pack, matrices1, pack, y_pack),
+        *(part, r1, pack, y_pack, matrices1),
     )
     pieces = call(
         functools.partial(second_spread_late, levels),
         [8 * levels] * 8,
         half_specs + [vmem(spread_shape[0], 3)],
-        [state, pltpu.VMEM(*spread_shape)],
+        scratch + [pltpu.VMEM(*spread_shape)],
         8 * size,
-        *(part, r2, pack, y_pack, matrices1, pack, y_pack, early),
+        *(part, r2, pack, y_pack, matrices1, early),
     )
     received = {}
     for bits in (6, 4, 2):
@@ -460,10 +459,10 @@
         [],
         size,
         pieces[0],
-        pair,
+        received[6],
         received[2],
         received[4],
-        received[6],
+        pair,
         matrices0,
     )
     return out.reshape(adjoint_in.shape)

time: 41.3 us -> 40.9 us (level)
  starting transfers between devices: 20.5 us -> 19.1 us
  waiting for transfers between devices: 10.9 us -> 11.4 us
    ppermute x4, starting transfers between devices: 9.96 us -> 8.28 us  [swap_lat(): return lax.ppermute(value, 'lat', pairs + [(b, a) for a, b in pairs])]
    ppermute x4, waiting for transfers between devices: 1.84 us -> 2.58 us  [swap_lat(): return lax.ppermute(value, 'lat', pairs + [(b, a) for a, b in pairs])]
    pallas_call x6 -> x7, Pallas kernels: 8.19 us -> 8.64 us  [call(): pl.pallas_call(kernel, grid=(1,), out_shape=[jax.ShapeDtypeStruct(*out) f...]
  transfers between devices with their start and end apart: 19 -> 19, of which waited for: 5 -> 6; matrix products, arithmetic and copies ran while one was open for 0% -> 0% of each run, Pallas kernels for 10% -> 11%
where the time goes in v6:
time: 40.9 us; the launch traced here: 40.6 us
  starting transfers between devices  19.1 us (47%)
  waiting for transfers between devices  11.4 us (28%)
  Pallas kernels  9.85 us (24%)
    ppermute x15, starting transfers between devices, swap_lon(): return lax.ppermute(value, 'lon', [(i, i ^ bits) for i in range(RING)])  10.8 us
    ppermute x15, waiting for transfers between devices, swap_lon(): return lax.ppermute(value, 'lon', [(i, i ^ bits) for i in range(RING)])  8.78 us
    pallas_call x7, Pallas kernels, call(): pl.pallas_call(kernel, grid=(1,), out_shape=[jax.ShapeDtypeStruct(*out) f...  8.64 us
    ppermute x4, starting transfers between devices, swap_lat(): return lax.ppermute(value, 'lat', pairs + [(b, a) for a, b in pairs])  8.28 us
    ppermute x4, waiting for transfers between devices, swap_lat(): return lax.ppermute(value, 'lat', pairs + [(b, a) for a, b in pairs])  2.58 us
    pallas_call x1, Pallas kernels, ring_body(): pl.pallas_call(functools.partial(assemble, levels), out_shape=[pltpu.VMEM...  1.21 us
  transfers between devices with their start and end apart: 19, of which 6 were waited for; matrix products, arithmetic and copies ran while one was open for 0% of the time, Pallas kernels for 11%

profile of v6, /device:TPU:8, one launch (start us, length us, event | category | flops | bytes accessed | tf_op | source)
XLA Modules:
  0.0 40.6 jit_solution(2074976378517995489)
XLA Ops:
  0.0 0.0 copy-start
  0.0 0.0 copy-start.2
  0.0 0.0 copy-start.1
  0.0 1.2 %shard_map.64 = (f32[328,128]{1,0:T(8,128)S(1)}, f32[328,128]{1,0:T(8,128)S(1)}, f32[72,128]{1,0:T(8,128)S(1)}, f32[72,128]{1,0:T(8,128)S(1)}) custom-call(s32[2,8]{1,0:T(2,128)} %bitcast.11, s32[2,8]{1,0:T(2,128)} %bitcast.12, f32[512,128]{1,0:T(8,128)} %bitcast.10, f32[64,128]{1,0:T(8,128)} %bitcast.6, f32[64,128]{1,0:T(8,128)} %bitcast.8, f32[2,8,32,32]{3,2,1,0:T(8,128)} %v.3), custom_call_target="tpu_custom_call" | custom-call | tf_op jit(solution)/shard_map/pallas_call | solution.py:376
  1.2 2.5 %collective-permute-start.4 = (f32[328,128]{1,0:T(8,128)S(1)}, f32[328,128]{1,0:T(8,128)S(1)}, u32[]{:S(2)}, u32[]{:S(2)}) collective-permute-start(f32[328,128]{1,0:T(8,128)S(1)} %get-tuple-element.29), channel_id=1, source_target_pairs={{0,6},{1,7},{2,4},{3,5},{4,2},{5,3},{6,0},{7,1},{8,14},{9,15},{10,... | collective-permute-start | bytes 503816 | tf_op jit(solution)/shard_map/ppermute | solution.py:357
  3.7 0.5 %collective-permute-start.1 = (f32[328,128]{1,0:T(8,128)S(1)}, f32[328,128]{1,0:T(8,128)S(1)}, u32[]{:S(2)}, u32[]{:S(2)}) collective-permute-start(f32[328,128]{1,0:T(8,128)S(1)} %get-tuple-element.29), channel_id=1, source_target_pairs={{0,4},{1,5},{2,6},{3,7},{4,0},{5,1},{6,2},{7,3},{8,12},{9,13},{10,... | collective-permute-start | bytes 503816 | tf_op jit(solution)/shard_map/ppermute | solution.py:357
  4.2 0.5 %collective-permute-start.7 = (f32[328,128]{1,0:T(8,128)S(1)}, f32[328,128]{1,0:T(8,128)S(1)}, u32[]{:S(2)}, u32[]{:S(2)}) collective-permute-start(f32[328,128]{1,0:T(8,128)S(1)} %get-tuple-element.28.refs_0_.own_tile), channel_id=1, source_target_pairs={{0,2},{1,3},{2,0},{3,1},{4,6},{5,7},{6,4},{7,5},{8,10},{9,11},{10,... | collective-permute-start | bytes 503816 | tf_op jit(solution)/shard_map/ppermute | solution.py:357
  4.8 3.5 %collective-permute-start.5 = (f32[72,128]{1,0:T(8,128)S(1)}, f32[72,128]{1,0:T(8,128)S(1)}, u32[]{:S(2)}, u32[]{:S(2)}) collective-permute-start(f32[72,128]{1,0:T(8,128)S(1)} %get-tuple-element.32), channel_id=1, source_target_pairs={{8,16},{16,8},{9,17},{17,9},{10,18},{18,10},{11,19},{19,11},{12,20... | collective-permute-start | bytes 110600 | tf_op jit(solution)/shard_map/ppermute | solution.py:363
  8.3 0.1 collective-permute-start.2
  8.3 0.8 %shard_map.65.refs_3_ = f32[30,32,128]{2,1,0:T(8,128)S(1)} custom-call(f32[328,128]{1,0:T(8,128)S(1)} %get-tuple-element.28.refs_0_.own_tile), custom_call_target="tpu_custom_call" | custom-call | flops 262144 | bytes 262144 | tf_op jit(solution)/shard_map/pallas_call | solution.py:109
  9.2 1.4 %collective-permute-done.5.e2 = f32[72,128]{1,0:T(8,128)S(1)} collective-permute-done((f32[72,128]{1,0:T(8,128)S(1)}, f32[72,128]{1,0:T(8,128)S(1)}, u32[]{:S(2)}, u32[]{:S(2)}) %collective-permute-start.5) | collective-permute-done | bytes 36896 | tf_op jit(solution)/shard_map/ppermute | solution.py:363
  10.6 0.0 collective-permute-start
  10.6 0.0 collective-permute-done.4.refs_1_
  10.6 0.5 %collective-permute-start.6 = (f32[328,128]{1,0:T(8,128)S(1)}, f32[328,128]{1,0:T(8,128)S(1)}, u32[]{:S(2)}, u32[]{:S(2)}) collective-permute-start(f32[328,128]{1,0:T(8,128)S(1)} %collective-permute-done.4.refs_1_), channel_id=1, source_target_pairs={{0,1},{1,0},{2,3},{3,2},{4,5},{5,4},{6,7},{7,6},{8,9},{9,8},{10,11... | collective-permute-start | bytes 503816 | tf_op jit(solution)/shard_map/ppermute | solution.py:357
  11.1 1.1 %collective-permute-done.2.e1 = f32[72,128]{1,0:T(8,128)S(1)} collective-permute-done((f32[72,128]{1,0:T(8,128)S(1)}, f32[72,128]{1,0:T(8,128)S(1)}, u32[]{:S(2)}, u32[]{:S(2)}) %collective-permute-start.2) | collective-permute-done | bytes 36896 | tf_op jit(solution)/shard_map/ppermute | solution.py:363
  12.3 0.0 collective-permute-done.1.refs_0_
  12.3 0.0 collective-permute-done.7.refs_2_
  12.3 0.0 collective-permute-start.8
  12.3 0.5 %collective-permute-start.3 = (f32[328,128]{1,0:T(8,128)S(1)}, f32[328,128]{1,0:T(8,128)S(1)}, u32[]{:S(2)}, u32[]{:S(2)}) collective-permute-start(f32[328,128]{1,0:T(8,128)S(1)} %collective-permute-done.1.refs_0_), channel_id=1, source_target_pairs={{0,1},{1,0},{2,3},{3,2},{4,5},{5,4},{6,7},{7,6},{8,9},{9,8},{10,11... | collective-permute-start | bytes 503816 | tf_op jit(solution)/shard_map/ppermute | solution.py:357
  12.8 1.3 %shard_map.66.refs_4_ = f32[30,32,128]{2,1,0:T(8,128)S(1)} custom-call(f32[328,128]{1,0:T(8,128)S(1)} %collective-permute-done.1.refs_0_, f32[328,128]{1,0:T(8,128)S(1)} %collective-permute-done.4.refs_1_, f32[328,128]{1,0:T(8,128)S(1)} %collective-permute-done.7.refs_2_, f32[30,32,128]{2,1,0:T(8,128)S(1)} %shard_map.65.refs_3_), custom_call_target="tpu_custom_call" | custom-call | flops 262144 | bytes 262144 | tf_op jit(solution)/shard_map/pallas_call | solution.py:109
  14.2 0.0 collective-permute-done.refs_0_
  14.2 0.0 collective-permute-done.6.refs_2_
  14.2 0.0 collective-permute-done.8.refs_3_
  14.2 0.0 collective-permute-done.3.refs_1_
  14.2 1.6 %shard_map.67 = (f32[30,32,128]{2,1,0:T(8,128)S(1)}, f32[512,128]{1,0:T(8,128)S(1)}, f32[512,128]{1,0:T(8,128)S(1)}) custom-call(f32[328,128]{1,0:T(8,128)S(1)} %collective-permute-done.refs_0_, f32[328,128]{1,0:T(8,128)S(1)} %collective-permute-done.3.refs_1_, f32[328,128]{1,0:T(8,128)S(1)} %collective-permute-done.6.refs_2_, ...), custom_call_target="tpu_custom_call" | custom-call | flops 262144 | bytes 262144 | tf_op jit(solution)/shard_map/pallas_call | solution.py:109
  15.8 0.1 collective-permute-start.11
  16.0 4.6 %collective-permute-start.9 = (f32[512,128]{1,0:T(8,128)S(1)}, f32[512,128]{1,0:T(8,128)S(1)}, u32[]{:S(2)}, u32[]{:S(2)}) collective-permute-start(f32[512,128]{1,0:T(8,128)S(1)} %get-tuple-element.36), channel_id=1, source_target_pairs={{8,16},{16,8},{9,17},{17,9},{10,18},{18,10},{11,19},{19,11},{12,20... | collective-permute-start | bytes 786440 | tf_op jit(solution)/shard_map/ppermute | solution.py:363
  20.6 0.0 copy-done
  20.6 0.0 copy-done.2
  20.6 0.0 copy-done.1
  20.6 0.9 %shard_map.68 = (f32[128,128]{1,0:T(8,128)S(1)}, bf16[512,128]{1,0:T(8,128)(2,1)S(1)}, bf16[256,128]{1,0:T(8,128)(2,1)S(1)}) custom-call(f32[328,128]{1,0:T(8,128)S(1)} %get-tuple-element.28.refs_0_.own_tile, f32[64,128]{1,0:T(8,128)S(1)} %bitcast.7, f32[64,128]{1,0:T(8,128)S(1)} %bitcast.9, f32[72,128]{1,0:T(8,128)S(1)} %collective-permute-done.2.e1, ...), custom_call_target="tpu_custom_call" | custom-call | flops 65536 | bytes 65536 | tf_op jit(solution)/shard_map/pallas_call | solution.py:109
  21.6 1.5 %collective-permute-start.10 = (f32[128,128]{1,0:T(8,128)S(1)}, f32[128,128]{1,0:T(8,128)S(1)}, u32[]{:S(2)}, u32[]{:S(2)}) collective-permute-start(f32[128,128]{1,0:T(8,128)S(1)} %get-tuple-element.39.refs_2_), channel_id=1, source_target_pairs={{0,4},{1,5},{2,6},{3,7},{4,0},{5,1},{6,2},{7,3},{8,12},{9,13},{10,... | collective-permute-start | bytes 196616 | tf_op jit(solution)/shard_map/ppermute | solution.py:357
  23.1 2.8 %collective-permute-done.10.refs_3_ = f32[128,128]{1,0:T(8,128)S(1)} collective-permute-done((f32[128,128]{1,0:T(8,128)S(1)}, f32[128,128]{1,0:T(8,128)S(1)}, u32[]{:S(2)}, u32[]{:S(2)}) %collective-permute-start.10) | collective-permute-done | bytes 65568 | tf_op jit(solution)/shard_map/ppermute | solution.py:357
  25.9 0.0 collective-permute-done.11.refs_1_
  25.9 1.4 %shard_map.69.refs_5_ = f32[176,32,128]{2,1,0:T(8,128)S(1)} custom-call(f32[30,32,128]{2,1,0:T(8,128)S(1)} %get-tuple-element.35.after_this.refs_0_, f32[512,128]{1,0:T(8,128)S(1)} %collective-permute-done.11.refs_1_, f32[128,128]{1,0:T(8,128)S(1)} %get-tuple-element.39.refs_2_, f32[128,128]{1,0:T(8,128)S(1)} %collective-permute-done.10.refs_3_, ...), custom_call_target="tpu_custom_call" | custom-call | flops 524288 | bytes 524288 | tf_op jit(solution)/shard_map/pallas_call | solution.py:109
  27.3 0.0 collective-permute-done.9.refs_1_
  27.3 1.5 %shard_map.70 = (f32[256,128]{1,0:T(8,128)S(1)}, f32[256,128]{1,0:T(8,128)S(1)}, f32[256,128]{1,0:T(8,128)S(1)}, f32[256,128]{1,0:T(8,128)S(1)}, f32[256,128]{1,...) custom-call(f32[30,32,128]{2,1,0:T(8,128)S(1)} %get-tuple-element.35.after_this.refs_0_, ...), custom_call_target="tpu_custom_call" | custom-call | flops 524288 | bytes 524288 | tf_op jit(solution)/shard_map/pallas_call | solution.py:109
  28.9 0.1 collective-permute-start.12
  29.0 0.5 %collective-permute-start.14 = (f32[256,128]{1,0:T(8,128)S(1)}, f32[256,128]{1,0:T(8,128)S(1)}, u32[]{:S(2)}, u32[]{:S(2)}) collective-permute-start(f32[256,128]{1,0:T(8,128)S(1)} %get-tuple-element.46), channel_id=1, source_target_pairs={{0,1},{1,0},{2,3},{3,2},{4,5},{5,4},{6,7},{7,6},{8,9},{9,8},{10,11... | collective-permute-start | bytes 393224 | tf_op jit(solution)/shard_map/ppermute | solution.py:357
  29.5 0.1 collective-permute-start.16
  29.5 0.4 %collective-permute-start.18 = (f32[256,128]{1,0:T(8,128)S(1)}, f32[256,128]{1,0:T(8,128)S(1)}, u32[]{:S(2)}, u32[]{:S(2)}) collective-permute-start(f32[256,128]{1,0:T(8,128)S(1)} %get-tuple-element.49), channel_id=1, source_target_pairs={{0,1},{1,0},{2,3},{3,2},{4,5},{5,4},{6,7},{7,6},{8,9},{9,8},{10,11... | collective-permute-start | bytes 393224 | tf_op jit(solution)/shard_map/ppermute | solution.py:357
  30.0 0.3 collective-permute-done.12
  30.3 1.7 %collective-permute-start.13 = (f32[256,128]{1,0:T(8,128)S(1)}, f32[256,128]{1,0:T(8,128)S(1)}, u32[]{:S(2)}, u32[]{:S(2)}) collective-permute-start(f32[256,128]{1,0:T(8,128)S(1)} %add.9), channel_id=1, source_target_pairs={{0,6},{1,7},{2,4},{3,5},{4,2},{5,3},{6,0},{7,1},{8,14},{9,15},{10,... | collective-permute-start | bytes 393224 | tf_op jit(solution)/shard_map/ppermute | solution.py:357
  32.0 0.0 collective-permute-done.14
  32.1 1.3 %collective-permute-start.15 = (f32[256,128]{1,0:T(8,128)S(1)}, f32[256,128]{1,0:T(8,128)S(1)}, u32[]{:S(2)}, u32[]{:S(2)}) collective-permute-start(f32[256,128]{1,0:T(8,128)S(1)} %add.10), channel_id=1, source_target_pairs={{0,2},{1,3},{2,0},{3,1},{4,6},{5,7},{6,4},{7,5},{8,10},{9,11},{10,... | collective-permute-start | bytes 393224 | tf_op jit(solution)/shard_map/ppermute | solution.py:357
  33.4 0.0 collective-permute-done.16
  33.4 0.7 %collective-permute-start.17 = (f32[256,128]{1,0:T(8,128)S(1)}, f32[256,128]{1,0:T(8,128)S(1)}, u32[]{:S(2)}, u32[]{:S(2)}) collective-permute-start(f32[256,128]{1,0:T(8,128)S(1)} %add.11), channel_id=1, source_target_pairs={{0,4},{1,5},{2,6},{3,7},{4,0},{5,1},{6,2},{7,3},{8,12},{9,13},{10,... | collective-permute-start | bytes 393224 | tf_op jit(solution)/shard_map/ppermute | solution.py:357
  34.1 0.0 collective-permute-done.18.pair
  34.1 3.6 %collective-permute-done.13.diagonal = f32[256,128]{1,0:T(8,128)S(1)} collective-permute-done((f32[256,128]{1,0:T(8,128)S(1)}, f32[256,128]{1,0:T(8,128)S(1)}, u32[]{:S(2)}, u32[]{:S(2)}) %collective-permute-start.13) | collective-permute-done | bytes 131104 | tf_op jit(solution)/shard_map/ppermute | solution.py:357
  37.6 2.0 %collective-permute-done.15.across = f32[256,128]{1,0:T(8,128)S(1)} collective-permute-done((f32[256,128]{1,0:T(8,128)S(1)}, f32[256,128]{1,0:T(8,128)S(1)}, u32[]{:S(2)}, u32[]{:S(2)}) %collective-permute-start.15) | collective-permute-done | bytes 131104 | tf_op jit(solution)/shard_map/ppermute | solution.py:357
  39.6 0.0 collective-permute-done.17.up
  39.6 0.9 %shard_map.71 = f32[512,128]{1,0:T(8,128)} custom-call(f32[256,128]{1,0:T(8,128)S(1)} %get-tuple-element.42.own, f32[256,128]{1,0:T(8,128)S(1)} %collective-permute-done.13.diagonal, f32[256,128]{1,0:T(8,128)S(1)} %collective-permute-done.15.across, f32[256,128]{1,0:T(8,128)S(1)} %collective-permute-done.17.up, f32[256,128]{1,0:T(8,128)S(1)} %collective-permute-done.18.pair, ...), custom_call_target="tpu_custom_call" | custom-call | flops 65536 | bytes 65536 | tf_op jit(solution)/shard_map/pallas_call | solution.py:109
  (3 shorter events, 0.0 us)
Async XLA Ops:
  0.0 20.6 %copy-start = (f32[2,8,32,32]{3,2,1,0:T(8,128)S(1)}, f32[2,8,32,32]{3,2,1,0:T(8,128)}, u32[]{:S(2)}) copy-start(f32[2,8,32,32]{3,2,1,0:T(8,128)} %v.3) | copy-start | bytes 196612
  0.0 20.6 %copy-start.2 = (f32[2,4,8,128]{3,2,1,0:T(8,128)S(1)}, f32[2,4,8,128]{3,2,1,0:T(8,128)}, u32[]{:S(2)}) copy-start(f32[2,4,8,128]{3,2,1,0:T(8,128)} %param.8) | copy-start | bytes 98308
  0.0 20.6 %copy-start.1 = (f32[2,4,8,128]{3,2,1,0:T(8,128)S(1)}, f32[2,4,8,128]{3,2,1,0:T(8,128)}, u32[]{:S(2)}) copy-start(f32[2,4,8,128]{3,2,1,0:T(8,128)} %param.7) | copy-start | bytes 98308
  1.2 9.4 %collective-permute-start.4 = (f32[328,128]{1,0:T(8,128)S(1)}, f32[328,128]{1,0:T(8,128)S(1)}, u32[]{:S(2)}, u32[]{:S(2)}) collective-permute-start(f32[328,128]{1,0:T(8,128)S(1)} %get-tuple-element.29), channel_id=1, source_target_pairs={{0,6},{1,7},{2,4},{3,5},{4,2},{5,3},{6,0},{7,1},{8,14},{9,15},{10,... | collective-permute-start | bytes 503816 | tf_op jit(solution)/shard_map/ppermute | solution.py:357
  3.7 8.6 %collective-permute-start.1 = (f32[328,128]{1,0:T(8,128)S(1)}, f32[328,128]{1,0:T(8,128)S(1)}, u32[]{:S(2)}, u32[]{:S(2)}) collective-permute-start(f32[328,128]{1,0:T(8,128)S(1)} %get-tuple-element.29), channel_id=1, source_target_pairs={{0,4},{1,5},{2,6},{3,7},{4,0},{5,1},{6,2},{7,3},{8,12},{9,13},{10,... | collective-permute-start | bytes 503816 | tf_op jit(solution)/shard_map/ppermute | solution.py:357
  4.2 8.0 %collective-permute-start.7 = (f32[328,128]{1,0:T(8,128)S(1)}, f32[328,128]{1,0:T(8,128)S(1)}, u32[]{:S(2)}, u32[]{:S(2)}) collective-permute-start(f32[328,128]{1,0:T(8,128)S(1)} %get-tuple-element.28.refs_0_.own_tile), channel_id=1, source_target_pairs={{0,2},{1,3},{2,0},{3,1},{4,6},{5,7},{6,4},{7,5},{8,10},{9,11},{10,... | collective-permute-start | bytes 503816 | tf_op jit(solution)/shard_map/ppermute | solution.py:357
  4.8 5.8 %collective-permute-start.5 = (f32[72,128]{1,0:T(8,128)S(1)}, f32[72,128]{1,0:T(8,128)S(1)}, u32[]{:S(2)}, u32[]{:S(2)}) collective-permute-start(f32[72,128]{1,0:T(8,128)S(1)} %get-tuple-element.32), channel_id=1, source_target_pairs={{8,16},{16,8},{9,17},{17,9},{10,18},{18,10},{11,19},{19,11},{12,20... | collective-permute-start | bytes 110600 | tf_op jit(solution)/shard_map/ppermute | solution.py:363
  8.3 4.0 %collective-permute-start.2 = (f32[72,128]{1,0:T(8,128)S(1)}, f32[72,128]{1,0:T(8,128)S(1)}, u32[]{:S(2)}, u32[]{:S(2)}) collective-permute-start(f32[72,128]{1,0:T(8,128)S(1)} %get-tuple-element.30), channel_id=1, source_target_pairs={{0,8},{16,24},{8,0},{24,16},{1,9},{17,25},{9,1},{25,17},{2,10},{18... | collective-permute-start | bytes 110600 | tf_op jit(solution)/shard_map/ppermute | solution.py:363
  10.6 3.5 %collective-permute-start = (f32[328,128]{1,0:T(8,128)S(1)}, f32[328,128]{1,0:T(8,128)S(1)}, u32[]{:S(2)}, u32[]{:S(2)}) collective-permute-start(f32[328,128]{1,0:T(8,128)S(1)} %get-tuple-element.28.refs_0_.own_tile), channel_id=1, source_target_pairs={{0,1},{1,0},{2,3},{3,2},{4,5},{5,4},{6,7},{7,6},{8,9},{9,8},{10,11... | collective-permute-start | bytes 503816 | tf_op jit(solution)/shard_map/ppermute | solution.py:357
  10.6 3.5 %collective-permute-start.6 = (f32[328,128]{1,0:T(8,128)S(1)}, f32[328,128]{1,0:T(8,128)S(1)}, u32[]{:S(2)}, u32[]{:S(2)}) collective-permute-start(f32[328,128]{1,0:T(8,128)S(1)} %collective-permute-done.4.refs_1_), channel_id=1, source_target_pairs={{0,1},{1,0},{2,3},{3,2},{4,5},{5,4},{6,7},{7,6},{8,9},{9,8},{10,11... | collective-permute-start | bytes 503816 | tf_op jit(solution)/shard_map/ppermute | solution.py:357
  12.3 1.9 %collective-permute-start.8 = (f32[328,128]{1,0:T(8,128)S(1)}, f32[328,128]{1,0:T(8,128)S(1)}, u32[]{:S(2)}, u32[]{:S(2)}) collective-permute-start(f32[328,128]{1,0:T(8,128)S(1)} %collective-permute-done.7.refs_2_), channel_id=1, source_target_pairs={{0,1},{1,0},{2,3},{3,2},{4,5},{5,4},{6,7},{7,6},{8,9},{9,8},{10,11... | collective-permute-start | bytes 503816 | tf_op jit(solution)/shard_map/ppermute | solution.py:357
  12.3 1.9 %collective-permute-start.3 = (f32[328,128]{1,0:T(8,128)S(1)}, f32[328,128]{1,0:T(8,128)S(1)}, u32[]{:S(2)}, u32[]{:S(2)}) collective-permute-start(f32[328,128]{1,0:T(8,128)S(1)} %collective-permute-done.1.refs_0_), channel_id=1, source_target_pairs={{0,1},{1,0},{2,3},{3,2},{4,5},{5,4},{6,7},{7,6},{8,9},{9,8},{10,11... | collective-permute-start | bytes 503816 | tf_op jit(solution)/shard_map/ppermute | solution.py:357
  15.8 10.1 %collective-permute-start.11 = (f32[512,128]{1,0:T(8,128)S(1)}, f32[512,128]{1,0:T(8,128)S(1)}, u32[]{:S(2)}, u32[]{:S(2)}) collective-permute-start(f32[512,128]{1,0:T(8,128)S(1)} %get-tuple-element.41), channel_id=1, source_target_pairs={{0,8},{16,24},{8,0},{24,16},{1,9},{17,25},{9,1},{25,17},{2,10},{18... | collective-permute-start | bytes 786440 | tf_op jit(solution)/shard_map/ppermute | solution.py:363
  16.0 11.3 %collective-permute-start.9 = (f32[512,128]{1,0:T(8,128)S(1)}, f32[512,128]{1,0:T(8,128)S(1)}, u32[]{:S(2)}, u32[]{:S(2)}) collective-permute-start(f32[512,128]{1,0:T(8,128)S(1)} %get-tuple-element.36), channel_id=1, source_target_pairs={{8,16},{16,8},{9,17},{17,9},{10,18},{18,10},{11,19},{19,11},{12,20... | collective-permute-start | bytes 786440 | tf_op jit(solution)/shard_map/ppermute | solution.py:363
  21.6 4.3 %collective-permute-start.10 = (f32[128,128]{1,0:T(8,128)S(1)}, f32[128,128]{1,0:T(8,128)S(1)}, u32[]{:S(2)}, u32[]{:S(2)}) collective-permute-start(f32[128,128]{1,0:T(8,128)S(1)} %get-tuple-element.39.refs_2_), channel_id=1, source_target_pairs={{0,4},{1,5},{2,6},{3,7},{4,0},{5,1},{6,2},{7,3},{8,12},{9,13},{10,... | collective-permute-start | bytes 196616 | tf_op jit(solution)/shard_map/ppermute | solution.py:357
  28.9 1.4 %collective-permute-start.12 = (f32[256,128]{1,0:T(8,128)S(1)}, f32[256,128]{1,0:T(8,128)S(1)}, u32[]{:S(2)}, u32[]{:S(2)}) collective-permute-start(f32[256,128]{1,0:T(8,128)S(1)} %get-tuple-element.44), channel_id=1, source_target_pairs={{0,1},{1,0},{2,3},{3,2},{4,5},{5,4},{6,7},{7,6},{8,9},{9,8},{10,11... | collective-permute-start | bytes 393224 | tf_op jit(solution)/shard_map/ppermute | solution.py:357
  29.0 3.1 %collective-permute-start.14 = (f32[256,128]{1,0:T(8,128)S(1)}, f32[256,128]{1,0:T(8,128)S(1)}, u32[]{:S(2)}, u32[]{:S(2)}) collective-permute-start(f32[256,128]{1,0:T(8,128)S(1)} %get-tuple-element.46), channel_id=1, source_target_pairs={{0,1},{1,0},{2,3},{3,2},{4,5},{5,4},{6,7},{7,6},{8,9},{9,8},{10,11... | collective-permute-start | bytes 393224 | tf_op jit(solution)/shard_map/ppermute | solution.py:357
  29.5 3.9 %collective-permute-start.16 = (f32[256,128]{1,0:T(8,128)S(1)}, f32[256,128]{1,0:T(8,128)S(1)}, u32[]{:S(2)}, u32[]{:S(2)}) collective-permute-start(f32[256,128]{1,0:T(8,128)S(1)} %get-tuple-element.48), channel_id=1, source_target_pairs={{0,1},{1,0},{2,3},{3,2},{4,5},{5,4},{6,7},{7,6},{8,9},{9,8},{10,11... | collective-permute-start | bytes 393224 | tf_op jit(solution)/shard_map/ppermute | solution.py:357
  29.5 4.5 %collective-permute-start.18 = (f32[256,128]{1,0:T(8,128)S(1)}, f32[256,128]{1,0:T(8,128)S(1)}, u32[]{:S(2)}, u32[]{:S(2)}) collective-permute-start(f32[256,128]{1,0:T(8,128)S(1)} %get-tuple-element.49), channel_id=1, source_target_pairs={{0,1},{1,0},{2,3},{3,2},{4,5},{5,4},{6,7},{7,6},{8,9},{9,8},{10,11... | collective-permute-start | bytes 393224 | tf_op jit(solution)/shard_map/ppermute | solution.py:357
  30.3 7.3 %collective-permute-start.13 = (f32[256,128]{1,0:T(8,128)S(1)}, f32[256,128]{1,0:T(8,128)S(1)}, u32[]{:S(2)}, u32[]{:S(2)}) collective-permute-start(f32[256,128]{1,0:T(8,128)S(1)} %add.9), channel_id=1, source_target_pairs={{0,6},{1,7},{2,4},{3,5},{4,2},{5,3},{6,0},{7,1},{8,14},{9,15},{10,... | collective-permute-start | bytes 393224 | tf_op jit(solution)/shard_map/ppermute | solution.py:357
  32.1 7.6 %collective-permute-start.15 = (f32[256,128]{1,0:T(8,128)S(1)}, f32[256,128]{1,0:T(8,128)S(1)}, u32[]{:S(2)}, u32[]{:S(2)}) collective-permute-start(f32[256,128]{1,0:T(8,128)S(1)} %add.10), channel_id=1, source_target_pairs={{0,2},{1,3},{2,0},{3,1},{4,6},{5,7},{6,4},{7,5},{8,10},{9,11},{10,... | collective-permute-start | bytes 393224 | tf_op jit(solution)/shard_map/ppermute | solution.py:357
  33.4 6.3 %collective-permute-start.17 = (f32[256,128]{1,0:T(8,128)S(1)}, f32[256,128]{1,0:T(8,128)S(1)}, u32[]{:S(2)}, u32[]{:S(2)}) collective-permute-start(f32[256,128]{1,0:T(8,128)S(1)} %add.11), channel_id=1, source_target_pairs={{0,4},{1,5},{2,6},{3,7},{4,0},{5,1},{6,2},{7,3},{8,12},{9,13},{10,... | collective-permute-start | bytes 393224 | tf_op jit(solution)/shard_map/ppermute | solution.py:357

commit v7 on v6

--- a/solution.py
+++ b/solution.py
@@ -153,8 +153,7 @@
             target[first + m, 8 * kk : 8 * kk + 8, :] += total
 
 
-def assemble(levels, rows, blocks, adj, lat_w, lon_w, v, own, other, e1, e2, *scratch):
-    tables, lat_all, lon_all, v1, sems = scratch
+def assemble(levels, rows, blocks, adj, lat_w, lon_w, v, own, other, e1, e2, lat_all, lon_all, v_all, tables, sems):
     field, even = lax.axis_index("lon") // 4, even_band()
     per_field = 8 * levels
     sem = iter(range(7))
@@ -163,7 +162,7 @@
         return pltpu.make_async_copy(source, target, sems.at[next(sem)])
 
     small = [copy(rows, tables.at[0]), copy(blocks, tables.at[1])]
-    small += [copy(lat_w, lat_all), copy(lon_w, lon_all), copy(v.at[1], v1)]
+    small += [copy(lat_w, lat_all), copy(lon_w, lon_all), copy(v, v_all)]
     large = []
     for out, which in ((own, field), (other, 1 - field)):
         large.append(copy(adj.at[pl.ds(pl.multiple_of(which * per_field, per_field), per_field)], out.at[pl.ds(0, per_field)]))
@@ -177,8 +176,8 @@
         out[per_field + 32 : per_field + 64, :] = lon_all[32:64, :]
     for out, first in ((own, per_field + 64), (other, per_field + 64), (e1, 32 + levels), (e2, 32 + levels)):
         out[first : first + 8, 0:8] = table
-    low = jnp.concatenate([v1[j] for j in range(4)], axis=1)
-    high = jnp.concatenate([v1[j + 4] for j in range(4)], axis=1)
+    low = jnp.concatenate([v_all[1, j] for j in range(4)], axis=1)
+    high = jnp.concatenate([v_all[1, j + 4] for j in range(4)], axis=1)
     for out, takes_high in ((e1, even == 1), (e2, even == 0)):
         first = jnp.where(takes_high, 4, 0)
         for i in range(4):
@@ -292,10 +291,12 @@
         there = (n < 15) & (~at_start | (n >= 4)) if j < 4 else n < 15
         return there & (~at_end | (n < 12)) if j >= 4 else there
 
+    sender = jnp.where(upper == 1, ~at_end, ~at_start)
     for j in range(8):
         halves = []
         for h in range(2):
             sent = received[pl.ds(pl.multiple_of((h * 8 + j - upper) * levels, levels) if j else h * 8 * levels, levels), :]
+            sent = jnp.where(sender, sent, 0.0)
             if j == 0:
                 value = jnp.where(upper == 1, part[h * 15 + 7], sent)
             else:
@@ -360,7 +361,9 @@
 def swap_lat(value, odd):
     count = lax.axis_size("lat")
     pairs = [(i, i + 1) for i in range(odd, count - 1, 2)]
-    return lax.ppermute(value, "lat", pairs + [(b, a) for a, b in pairs])
+    partner = {a: b for pair in pairs for a, b in (pair, pair[::-1])}
+    moves = [(i * RING + j, partner[i] * RING + j if i in partner else i * RING + (j ^ 1)) for i in range(count) for j in range(RING)]
+    return lax.ppermute(value, ("lat", "lon"), moves)
 
 
 def ring_body(adjoint_in, lat_weights, lon_weights, depart_rows, depart_blocks, vertical_inverse):
@@ -371,20 +374,14 @@
     side = 32 + levels + 8
     adjoint = adjoint_in.reshape(-1, points)
     lat_w, lon_w = lat_weights.reshape(-1, points), lon_weights.reshape(-1, points)
-    sizes = [message, message, side, side]
+    shapes = [(n, points) for n in (message, message, side, side, 64, 64)] + [vertical_inverse.shape]
     arguments = depart_rows[:, :, 0], depart_blocks[:, :, 0], adjoint, lat_w, lon_w, vertical_inverse
-    own, other, e1, e2 = pl.pallas_call(
+    own, other, e1, e2, lat_w, lon_w, matrices = pl.pallas_call(
         functools.partial(assemble, levels),
-        out_shape=[pltpu.VMEM((n, points), jnp.float32) for n in sizes],
+        out_shape=[pltpu.VMEM(shape, jnp.float32) for shape in shapes],
         in_specs=[pl.BlockSpec(memory_space=pltpu.HBM)] * 6,
-        out_specs=[pl.BlockSpec(memory_space=pltpu.VMEM)] * 4,
-        scratch_shapes=[
-            pltpu.VMEM((2, 2, 8), jnp.int32),
-            pltpu.VMEM((64, points), jnp.float32),
-            pltpu.VMEM((64, points), jnp.float32),
-            pltpu.VMEM((8, levels, levels), jnp.float32),
-            pltpu.SemaphoreType.DMA((7,)),
-        ],
+        out_specs=[pl.BlockSpec(memory_space=pltpu.VMEM)] * 7,
+        scratch_shapes=[pltpu.VMEM((2, 2, 8), jnp.int32), pltpu.SemaphoreType.DMA((7,))],
         compiler_params=pltpu.CompilerParams(vmem_limit_bytes=VMEM_LIMIT),
     )(*(pltpu.with_memory_space_constraint(value, pltpu.HBM) for value in arguments))
     far = {2: swap_lon(own, 2), 4: swap_lon(other, 4), 6: swap_lon(other, 6)}
@@ -424,7 +421,7 @@
         lon_w,
         e1,
         e2,
-        vertical_inverse,
+        matrices,
         part,
     )
     y_pack = swap_lon(pack, 4)

time: 40.9 us -> 40 us (0.978)
  the two profiles are of different devices: /device:TPU:8 before, /device:TPU:0 now
where the time goes in v7:
time: 40 us; the launch traced here: 39.8 us
  starting transfers between devices  17.1 us (43%)
  waiting for transfers between devices  12.7 us (32%)
  Pallas kernels  9.84 us (25%)
    ppermute x15, starting transfers between devices, swap_lon(): return lax.ppermute(value, 'lon', [(i, i ^ bits) for i in range(RING)])  11.9 us
    ppermute x15, waiting for transfers between devices, swap_lon(): return lax.ppermute(value, 'lon', [(i, i ^ bits) for i in range(RING)])  11.1 us
    pallas_call x7, Pallas kernels, call(): pl.pallas_call(kernel, grid=(1,), out_shape=[jax.ShapeDtypeStruct(*out) f...  8.66 us
    ppermute x4, starting transfers between devices, swap_lat(): return lax.ppermute(value, ('lat', 'lon'), moves)  5.2 us
    ppermute x4, waiting for transfers between devices, swap_lat(): return lax.ppermute(value, ('lat', 'lon'), moves)  1.62 us
    pallas_call x1, Pallas kernels, ring_body(): pl.pallas_call(functools.partial(assemble, levels), out_shape=[pltpu.VMEM...  1.18 us
  transfers between devices with their start and end apart: 19, of which 8 were waited for; matrix products, arithmetic and copies ran while one was open for 0% of the time, Pallas kernels for 11%

profile of v7, /device:TPU:0, one launch (start us, length us, event | category | flops | bytes accessed | tf_op | source)
XLA Modules:
  0.0 39.8 jit_solution(9834038678083665521)
XLA Ops:
  0.0 1.2 %shard_map.64 = (f32[328,128]{1,0:T(8,128)S(1)}, f32[328,128]{1,0:T(8,128)S(1)}, f32[72,128]{1,0:T(8,128)S(1)}, f32[72,128]{1,0:T(8,128)S(1)}, f32[64,128]{1,0:T...) custom-call(s32[2,8]{1,0:T(2,128)} %bitcast.9, s32[2,8]{1,0:T(2,128)} %bitcast.10, f32[512,128]{1,0:T(8,128)} %bitcast.6, ...), custom_call_target="tpu_custom_call" | custom-call | tf_op jit(solution)/shard_map/pallas_call | solution.py:379
  1.2 4.0 %collective-permute-start.4 = (f32[328,128]{1,0:T(8,128)S(1)}, f32[328,128]{1,0:T(8,128)S(1)}, u32[]{:S(2)}, u32[]{:S(2)}) collective-permute-start(f32[328,128]{1,0:T(8,128)S(1)} %get-tuple-element.32), channel_id=1, source_target_pairs={{0,6},{1,7},{2,4},{3,5},{4,2},{5,3},{6,0},{7,1},{8,14},{9,15},{10,... | collective-permute-start | bytes 503816 | tf_op jit(solution)/shard_map/ppermute | solution.py:358
  5.1 0.5 %collective-permute-start.1 = (f32[328,128]{1,0:T(8,128)S(1)}, f32[328,128]{1,0:T(8,128)S(1)}, u32[]{:S(2)}, u32[]{:S(2)}) collective-permute-start(f32[328,128]{1,0:T(8,128)S(1)} %get-tuple-element.32), channel_id=1, source_target_pairs={{0,4},{1,5},{2,6},{3,7},{4,0},{5,1},{6,2},{7,3},{8,12},{9,13},{10,... | collective-permute-start | bytes 503816 | tf_op jit(solution)/shard_map/ppermute | solution.py:358
  5.7 0.1 collective-permute-start.7
  5.8 0.0 collective-permute-start.5
  5.8 3.5 %collective-permute-start.2 = (f32[72,128]{1,0:T(8,128)S(1)}, f32[72,128]{1,0:T(8,128)S(1)}, u32[]{:S(2)}, u32[]{:S(2)}) collective-permute-start(f32[72,128]{1,0:T(8,128)S(1)} %get-tuple-element.33), channel_id=1, source_target_pairs={{0,8},{1,9},{2,10},{3,11},{4,12},{5,13},{6,14},{7,15},{8,0},{9,1},... | collective-permute-start | bytes 110600 | tf_op jit(solution)/shard_map/ppermute | solution.py:366
  9.3 0.8 %shard_map.65.refs_3_ = f32[30,32,128]{2,1,0:T(8,128)S(1)} custom-call(f32[328,128]{1,0:T(8,128)S(1)} %get-tuple-element.31.refs_0_.own_tile), custom_call_target="tpu_custom_call" | custom-call | flops 262144 | bytes 262144 | tf_op jit(solution)/shard_map/pallas_call | solution.py:109
  10.2 0.0 collective-permute-done.5.e2
  10.2 0.1 collective-permute-start
  10.3 0.0 collective-permute-done.4.refs_1_
  10.3 0.5 %collective-permute-start.6 = (f32[328,128]{1,0:T(8,128)S(1)}, f32[328,128]{1,0:T(8,128)S(1)}, u32[]{:S(2)}, u32[]{:S(2)}) collective-permute-start(f32[328,128]{1,0:T(8,128)S(1)} %collective-permute-done.4.refs_1_), channel_id=1, source_target_pairs={{0,1},{1,0},{2,3},{3,2},{4,5},{5,4},{6,7},{7,6},{8,9},{9,8},{10,11... | collective-permute-start | bytes 503816 | tf_op jit(solution)/shard_map/ppermute | solution.py:358
  10.8 0.5 %collective-permute-done.2.e1 = f32[72,128]{1,0:T(8,128)S(1)} collective-permute-done((f32[72,128]{1,0:T(8,128)S(1)}, f32[72,128]{1,0:T(8,128)S(1)}, u32[]{:S(2)}, u32[]{:S(2)}) %collective-permute-start.2) | collective-permute-done | bytes 36896 | tf_op jit(solution)/shard_map/ppermute | solution.py:366
  11.3 1.8 %collective-permute-done.1.refs_0_ = f32[328,128]{1,0:T(8,128)S(1)} collective-permute-done((f32[328,128]{1,0:T(8,128)S(1)}, f32[328,128]{1,0:T(8,128)S(1)}, u32[]{:S(2)}, u32[]{:S(2)}) %collective-permute-start.1) | collective-permute-done | bytes 167968 | tf_op jit(solution)/shard_map/ppermute | solution.py:358
  13.0 0.3 collective-permute-done.7.refs_2_
  13.3 0.0 collective-permute-start.8
  13.3 0.5 %collective-permute-start.3 = (f32[328,128]{1,0:T(8,128)S(1)}, f32[328,128]{1,0:T(8,128)S(1)}, u32[]{:S(2)}, u32[]{:S(2)}) collective-permute-start(f32[328,128]{1,0:T(8,128)S(1)} %collective-permute-done.1.refs_0_), channel_id=1, source_target_pairs={{0,1},{1,0},{2,3},{3,2},{4,5},{5,4},{6,7},{7,6},{8,9},{9,8},{10,11... | collective-permute-start | bytes 503816 | tf_op jit(solution)/shard_map/ppermute | solution.py:358
  13.8 1.3 %shard_map.66.refs_4_ = f32[30,32,128]{2,1,0:T(8,128)S(1)} custom-call(f32[328,128]{1,0:T(8,128)S(1)} %collective-permute-done.1.refs_0_, f32[328,128]{1,0:T(8,128)S(1)} %collective-permute-done.4.refs_1_, f32[328,128]{1,0:T(8,128)S(1)} %collective-permute-done.7.refs_2_, f32[30,32,128]{2,1,0:T(8,128)S(1)} %shard_map.65.refs_3_), custom_call_target="tpu_custom_call" | custom-call | flops 262144 | bytes 262144 | tf_op jit(solution)/shard_map/pallas_call | solution.py:109
  15.2 0.0 collective-permute-done.refs_0_
  15.2 0.0 collective-permute-done.6.refs_2_
  15.2 0.0 collective-permute-done.8.refs_3_
  15.2 0.0 collective-permute-done.3.refs_1_
  15.2 1.6 %shard_map.67 = (f32[30,32,128]{2,1,0:T(8,128)S(1)}, f32[512,128]{1,0:T(8,128)S(1)}, f32[512,128]{1,0:T(8,128)S(1)}) custom-call(f32[328,128]{1,0:T(8,128)S(1)} %collective-permute-done.refs_0_, f32[328,128]{1,0:T(8,128)S(1)} %collective-permute-done.3.refs_1_, f32[328,128]{1,0:T(8,128)S(1)} %collective-permute-done.6.refs_2_, ...), custom_call_target="tpu_custom_call" | custom-call | flops 262144 | bytes 262144 | tf_op jit(solution)/shard_map/pallas_call | solution.py:109
  16.9 1.6 %collective-permute-start.11 = (f32[512,128]{1,0:T(8,128)S(1)}, f32[512,128]{1,0:T(8,128)S(1)}, u32[]{:S(2)}, u32[]{:S(2)}) collective-permute-start(f32[512,128]{1,0:T(8,128)S(1)} %get-tuple-element.47), channel_id=1, source_target_pairs={{0,8},{1,9},{2,10},{3,11},{4,12},{5,13},{6,14},{7,15},{8,0},{9,1},... | collective-permute-start | bytes 786440 | tf_op jit(solution)/shard_map/ppermute | solution.py:366
  18.5 0.0 collective-permute-start.9
  18.5 0.9 %shard_map.68 = (f32[128,128]{1,0:T(8,128)S(1)}, bf16[512,128]{1,0:T(8,128)(2,1)S(1)}, bf16[256,128]{1,0:T(8,128)(2,1)S(1)}) custom-call(f32[328,128]{1,0:T(8,128)S(1)} %get-tuple-element.31.refs_0_.own_tile, f32[64,128]{1,0:T(8,128)S(1)} %get-tuple-element.40.lat_w, f32[64,128]{1,0:T(8,128)S(1)} %get-tuple-element.41.lon_w, ...), custom_call_target="tpu_custom_call" | custom-call | flops 65536 | bytes 65536 | tf_op jit(solution)/shard_map/pallas_call | solution.py:109
  19.5 1.5 %collective-permute-start.10 = (f32[128,128]{1,0:T(8,128)S(1)}, f32[128,128]{1,0:T(8,128)S(1)}, u32[]{:S(2)}, u32[]{:S(2)}) collective-permute-start(f32[128,128]{1,0:T(8,128)S(1)} %get-tuple-element.45.refs_2_), channel_id=1, source_target_pairs={{0,4},{1,5},{2,6},{3,7},{4,0},{5,1},{6,2},{7,3},{8,12},{9,13},{10,... | collective-permute-start | bytes 196616 | tf_op jit(solution)/shard_map/ppermute | solution.py:358
  21.0 3.1 %collective-permute-done.10.refs_3_ = f32[128,128]{1,0:T(8,128)S(1)} collective-permute-done((f32[128,128]{1,0:T(8,128)S(1)}, f32[128,128]{1,0:T(8,128)S(1)}, u32[]{:S(2)}, u32[]{:S(2)}) %collective-permute-start.10) | collective-permute-done | bytes 65568 | tf_op jit(solution)/shard_map/ppermute | solution.py:358
  24.0 1.1 %collective-permute-done.11.refs_1_ = f32[512,128]{1,0:T(8,128)S(1)} collective-permute-done((f32[512,128]{1,0:T(8,128)S(1)}, f32[512,128]{1,0:T(8,128)S(1)}, u32[]{:S(2)}, u32[]{:S(2)}) %collective-permute-start.11) | collective-permute-done | bytes 262176 | tf_op jit(solution)/shard_map/ppermute | solution.py:366
  25.2 1.4 %shard_map.69.refs_5_ = f32[176,32,128]{2,1,0:T(8,128)S(1)} custom-call(f32[30,32,128]{2,1,0:T(8,128)S(1)} %get-tuple-element.38.after_this.refs_0_, f32[512,128]{1,0:T(8,128)S(1)} %collective-permute-done.11.refs_1_, f32[128,128]{1,0:T(8,128)S(1)} %get-tuple-element.45.refs_2_, f32[128,128]{1,0:T(8,128)S(1)} %collective-permute-done.10.refs_3_, ...), custom_call_target="tpu_custom_call" | custom-call | flops 524288 | bytes 524288 | tf_op jit(solution)/shard_map/pallas_call | solution.py:109
  26.6 0.0 collective-permute-done.9.refs_1_
  26.6 1.6 %shard_map.70 = (f32[256,128]{1,0:T(8,128)S(1)}, f32[256,128]{1,0:T(8,128)S(1)}, f32[256,128]{1,0:T(8,128)S(1)}, f32[256,128]{1,0:T(8,128)S(1)}, f32[256,128]{1,...) custom-call(f32[30,32,128]{2,1,0:T(8,128)S(1)} %get-tuple-element.38.after_this.refs_0_, ...), custom_call_target="tpu_custom_call" | custom-call | flops 524288 | bytes 524288 | tf_op jit(solution)/shard_map/pallas_call | solution.py:109
  28.2 0.1 collective-permute-start.12
  28.3 0.5 %collective-permute-start.14 = (f32[256,128]{1,0:T(8,128)S(1)}, f32[256,128]{1,0:T(8,128)S(1)}, u32[]{:S(2)}, u32[]{:S(2)}) collective-permute-start(f32[256,128]{1,0:T(8,128)S(1)} %get-tuple-element.52), channel_id=1, source_target_pairs={{0,1},{1,0},{2,3},{3,2},{4,5},{5,4},{6,7},{7,6},{8,9},{9,8},{10,11... | collective-permute-start | bytes 393224 | tf_op jit(solution)/shard_map/ppermute | solution.py:358
  28.8 0.1 collective-permute-start.16
  28.8 0.4 %collective-permute-start.18 = (f32[256,128]{1,0:T(8,128)S(1)}, f32[256,128]{1,0:T(8,128)S(1)}, u32[]{:S(2)}, u32[]{:S(2)}) collective-permute-start(f32[256,128]{1,0:T(8,128)S(1)} %get-tuple-element.55), channel_id=1, source_target_pairs={{0,1},{1,0},{2,3},{3,2},{4,5},{5,4},{6,7},{7,6},{8,9},{9,8},{10,11... | collective-permute-start | bytes 393224 | tf_op jit(solution)/shard_map/ppermute | solution.py:358
  29.3 0.3 collective-permute-done.12
  29.6 1.6 %collective-permute-start.13 = (f32[256,128]{1,0:T(8,128)S(1)}, f32[256,128]{1,0:T(8,128)S(1)}, u32[]{:S(2)}, u32[]{:S(2)}) collective-permute-start(f32[256,128]{1,0:T(8,128)S(1)} %add.9), channel_id=1, source_target_pairs={{0,6},{1,7},{2,4},{3,5},{4,2},{5,3},{6,0},{7,1},{8,14},{9,15},{10,... | collective-permute-start | bytes 393224 | tf_op jit(solution)/shard_map/ppermute | solution.py:358
  31.2 0.0 collective-permute-done.14
  31.2 1.4 %collective-permute-start.15 = (f32[256,128]{1,0:T(8,128)S(1)}, f32[256,128]{1,0:T(8,128)S(1)}, u32[]{:S(2)}, u32[]{:S(2)}) collective-permute-start(f32[256,128]{1,0:T(8,128)S(1)} %add.10), channel_id=1, source_target_pairs={{0,2},{1,3},{2,0},{3,1},{4,6},{5,7},{6,4},{7,5},{8,10},{9,11},{10,... | collective-permute-start | bytes 393224 | tf_op jit(solution)/shard_map/ppermute | solution.py:358
  32.7 0.0 collective-permute-done.16
  32.7 0.7 %collective-permute-start.17 = (f32[256,128]{1,0:T(8,128)S(1)}, f32[256,128]{1,0:T(8,128)S(1)}, u32[]{:S(2)}, u32[]{:S(2)}) collective-permute-start(f32[256,128]{1,0:T(8,128)S(1)} %add.11), channel_id=1, source_target_pairs={{0,4},{1,5},{2,6},{3,7},{4,0},{5,1},{6,2},{7,3},{8,12},{9,13},{10,... | collective-permute-start | bytes 393224 | tf_op jit(solution)/shard_map/ppermute | solution.py:358
  33.3 0.0 collective-permute-done.18.pair
  33.3 3.6 %collective-permute-done.13.diagonal = f32[256,128]{1,0:T(8,128)S(1)} collective-permute-done((f32[256,128]{1,0:T(8,128)S(1)}, f32[256,128]{1,0:T(8,128)S(1)}, u32[]{:S(2)}, u32[]{:S(2)}) %collective-permute-start.13) | collective-permute-done | bytes 131104 | tf_op jit(solution)/shard_map/ppermute | solution.py:358
  36.9 2.0 %collective-permute-done.15.across = f32[256,128]{1,0:T(8,128)S(1)} collective-permute-done((f32[256,128]{1,0:T(8,128)S(1)}, f32[256,128]{1,0:T(8,128)S(1)}, u32[]{:S(2)}, u32[]{:S(2)}) %collective-permute-start.15) | collective-permute-done | bytes 131104 | tf_op jit(solution)/shard_map/ppermute | solution.py:358
  38.9 0.0 collective-permute-done.17.up
  38.9 0.9 %shard_map.71 = f32[512,128]{1,0:T(8,128)} custom-call(f32[256,128]{1,0:T(8,128)S(1)} %get-tuple-element.48.own, f32[256,128]{1,0:T(8,128)S(1)} %collective-permute-done.13.diagonal, f32[256,128]{1,0:T(8,128)S(1)} %collective-permute-done.15.across, f32[256,128]{1,0:T(8,128)S(1)} %collective-permute-done.17.up, f32[256,128]{1,0:T(8,128)S(1)} %collective-permute-done.18.pair, ...), custom_call_target="tpu_custom_call" | custom-call | flops 65536 | bytes 65536 | tf_op jit(solution)/shard_map/pallas_call | solution.py:109
  (3 shorter events, 0.0 us)
Async XLA Ops:
  1.2 9.1 %collective-permute-start.4 = (f32[328,128]{1,0:T(8,128)S(1)}, f32[328,128]{1,0:T(8,128)S(1)}, u32[]{:S(2)}, u32[]{:S(2)}) collective-permute-start(f32[328,128]{1,0:T(8,128)S(1)} %get-tuple-element.32), channel_id=1, source_target_pairs={{0,6},{1,7},{2,4},{3,5},{4,2},{5,3},{6,0},{7,1},{8,14},{9,15},{10,... | collective-permute-start | bytes 503816 | tf_op jit(solution)/shard_map/ppermute | solution.py:358
  5.1 7.9 %collective-permute-start.1 = (f32[328,128]{1,0:T(8,128)S(1)}, f32[328,128]{1,0:T(8,128)S(1)}, u32[]{:S(2)}, u32[]{:S(2)}) collective-permute-start(f32[328,128]{1,0:T(8,128)S(1)} %get-tuple-element.32), channel_id=1, source_target_pairs={{0,4},{1,5},{2,6},{3,7},{4,0},{5,1},{6,2},{7,3},{8,12},{9,13},{10,... | collective-permute-start | bytes 503816 | tf_op jit(solution)/shard_map/ppermute | solution.py:358
  5.7 7.7 %collective-permute-start.7 = (f32[328,128]{1,0:T(8,128)S(1)}, f32[328,128]{1,0:T(8,128)S(1)}, u32[]{:S(2)}, u32[]{:S(2)}) collective-permute-start(f32[328,128]{1,0:T(8,128)S(1)} %get-tuple-element.31.refs_0_.own_tile), channel_id=1, source_target_pairs={{0,2},{1,3},{2,0},{3,1},{4,6},{5,7},{6,4},{7,5},{8,10},{9,11},{10,... | collective-permute-start | bytes 503816 | tf_op jit(solution)/shard_map/ppermute | solution.py:358
  5.8 4.4 %collective-permute-start.5 = (f32[72,128]{1,0:T(8,128)S(1)}, f32[72,128]{1,0:T(8,128)S(1)}, u32[]{:S(2)}, u32[]{:S(2)}) collective-permute-start(f32[72,128]{1,0:T(8,128)S(1)} %get-tuple-element.35), channel_id=1, source_target_pairs={{0,1},{1,0},{2,3},{3,2},{4,5},{5,4},{6,7},{7,6},{8,16},{9,17},{10,... | collective-permute-start | bytes 110600 | tf_op jit(solution)/shard_map/ppermute | solution.py:366
  5.8 5.5 %collective-permute-start.2 = (f32[72,128]{1,0:T(8,128)S(1)}, f32[72,128]{1,0:T(8,128)S(1)}, u32[]{:S(2)}, u32[]{:S(2)}) collective-permute-start(f32[72,128]{1,0:T(8,128)S(1)} %get-tuple-element.33), channel_id=1, source_target_pairs={{0,8},{1,9},{2,10},{3,11},{4,12},{5,13},{6,14},{7,15},{8,0},{9,1},... | collective-permute-start | bytes 110600 | tf_op jit(solution)/shard_map/ppermute | solution.py:366
  10.2 5.0 %collective-permute-start = (f32[328,128]{1,0:T(8,128)S(1)}, f32[328,128]{1,0:T(8,128)S(1)}, u32[]{:S(2)}, u32[]{:S(2)}) collective-permute-start(f32[328,128]{1,0:T(8,128)S(1)} %get-tuple-element.31.refs_0_.own_tile), channel_id=1, source_target_pairs={{0,1},{1,0},{2,3},{3,2},{4,5},{5,4},{6,7},{7,6},{8,9},{9,8},{10,11... | collective-permute-start | bytes 503816 | tf_op jit(solution)/shard_map/ppermute | solution.py:358
  10.3 4.9 %collective-permute-start.6 = (f32[328,128]{1,0:T(8,128)S(1)}, f32[328,128]{1,0:T(8,128)S(1)}, u32[]{:S(2)}, u32[]{:S(2)}) collective-permute-start(f32[328,128]{1,0:T(8,128)S(1)} %collective-permute-done.4.refs_1_), channel_id=1, source_target_pairs={{0,1},{1,0},{2,3},{3,2},{4,5},{5,4},{6,7},{7,6},{8,9},{9,8},{10,11... | collective-permute-start | bytes 503816 | tf_op jit(solution)/shard_map/ppermute | solution.py:358
  13.3 1.9 %collective-permute-start.8 = (f32[328,128]{1,0:T(8,128)S(1)}, f32[328,128]{1,0:T(8,128)S(1)}, u32[]{:S(2)}, u32[]{:S(2)}) collective-permute-start(f32[328,128]{1,0:T(8,128)S(1)} %collective-permute-done.7.refs_2_), channel_id=1, source_target_pairs={{0,1},{1,0},{2,3},{3,2},{4,5},{5,4},{6,7},{7,6},{8,9},{9,8},{10,11... | collective-permute-start | bytes 503816 | tf_op jit(solution)/shard_map/ppermute | solution.py:358
  13.3 1.9 %collective-permute-start.3 = (f32[328,128]{1,0:T(8,128)S(1)}, f32[328,128]{1,0:T(8,128)S(1)}, u32[]{:S(2)}, u32[]{:S(2)}) collective-permute-start(f32[328,128]{1,0:T(8,128)S(1)} %collective-permute-done.1.refs_0_), channel_id=1, source_target_pairs={{0,1},{1,0},{2,3},{3,2},{4,5},{5,4},{6,7},{7,6},{8,9},{9,8},{10,11... | collective-permute-start | bytes 503816 | tf_op jit(solution)/shard_map/ppermute | solution.py:358
  16.9 8.3 %collective-permute-start.11 = (f32[512,128]{1,0:T(8,128)S(1)}, f32[512,128]{1,0:T(8,128)S(1)}, u32[]{:S(2)}, u32[]{:S(2)}) collective-permute-start(f32[512,128]{1,0:T(8,128)S(1)} %get-tuple-element.47), channel_id=1, source_target_pairs={{0,8},{1,9},{2,10},{3,11},{4,12},{5,13},{6,14},{7,15},{8,0},{9,1},... | collective-permute-start | bytes 786440 | tf_op jit(solution)/shard_map/ppermute | solution.py:366
  18.5 8.1 %collective-permute-start.9 = (f32[512,128]{1,0:T(8,128)S(1)}, f32[512,128]{1,0:T(8,128)S(1)}, u32[]{:S(2)}, u32[]{:S(2)}) collective-permute-start(f32[512,128]{1,0:T(8,128)S(1)} %get-tuple-element.39), channel_id=1, source_target_pairs={{0,1},{1,0},{2,3},{3,2},{4,5},{5,4},{6,7},{7,6},{8,16},{9,17},{10,... | collective-permute-start | bytes 786440 | tf_op jit(solution)/shard_map/ppermute | solution.py:366
  19.5 4.6 %collective-permute-start.10 = (f32[128,128]{1,0:T(8,128)S(1)}, f32[128,128]{1,0:T(8,128)S(1)}, u32[]{:S(2)}, u32[]{:S(2)}) collective-permute-start(f32[128,128]{1,0:T(8,128)S(1)} %get-tuple-element.45.refs_2_), channel_id=1, source_target_pairs={{0,4},{1,5},{2,6},{3,7},{4,0},{5,1},{6,2},{7,3},{8,12},{9,13},{10,... | collective-permute-start | bytes 196616 | tf_op jit(solution)/shard_map/ppermute | solution.py:358
  28.2 1.4 %collective-permute-start.12 = (f32[256,128]{1,0:T(8,128)S(1)}, f32[256,128]{1,0:T(8,128)S(1)}, u32[]{:S(2)}, u32[]{:S(2)}) collective-permute-start(f32[256,128]{1,0:T(8,128)S(1)} %get-tuple-element.50), channel_id=1, source_target_pairs={{0,1},{1,0},{2,3},{3,2},{4,5},{5,4},{6,7},{7,6},{8,9},{9,8},{10,11... | collective-permute-start | bytes 393224 | tf_op jit(solution)/shard_map/ppermute | solution.py:358
  28.3 3.0 %collective-permute-start.14 = (f32[256,128]{1,0:T(8,128)S(1)}, f32[256,128]{1,0:T(8,128)S(1)}, u32[]{:S(2)}, u32[]{:S(2)}) collective-permute-start(f32[256,128]{1,0:T(8,128)S(1)} %get-tuple-element.52), channel_id=1, source_target_pairs={{0,1},{1,0},{2,3},{3,2},{4,5},{5,4},{6,7},{7,6},{8,9},{9,8},{10,11... | collective-permute-start | bytes 393224 | tf_op jit(solution)/shard_map/ppermute | solution.py:358
  28.8 3.9 %collective-permute-start.16 = (f32[256,128]{1,0:T(8,128)S(1)}, f32[256,128]{1,0:T(8,128)S(1)}, u32[]{:S(2)}, u32[]{:S(2)}) collective-permute-start(f32[256,128]{1,0:T(8,128)S(1)} %get-tuple-element.54), channel_id=1, source_target_pairs={{0,1},{1,0},{2,3},{3,2},{4,5},{5,4},{6,7},{7,6},{8,9},{9,8},{10,11... | collective-permute-start | bytes 393224 | tf_op jit(solution)/shard_map/ppermute | solution.py:358
  28.8 4.5 %collective-permute-start.18 = (f32[256,128]{1,0:T(8,128)S(1)}, f32[256,128]{1,0:T(8,128)S(1)}, u32[]{:S(2)}, u32[]{:S(2)}) collective-permute-start(f32[256,128]{1,0:T(8,128)S(1)} %get-tuple-element.55), channel_id=1, source_target_pairs={{0,1},{1,0},{2,3},{3,2},{4,5},{5,4},{6,7},{7,6},{8,9},{9,8},{10,11... | collective-permute-start | bytes 393224 | tf_op jit(solution)/shard_map/ppermute | solution.py:358
  29.6 7.3 %collective-permute-start.13 = (f32[256,128]{1,0:T(8,128)S(1)}, f32[256,128]{1,0:T(8,128)S(1)}, u32[]{:S(2)}, u32[]{:S(2)}) collective-permute-start(f32[256,128]{1,0:T(8,128)S(1)} %add.9), channel_id=1, source_target_pairs={{0,6},{1,7},{2,4},{3,5},{4,2},{5,3},{6,0},{7,1},{8,14},{9,15},{10,... | collective-permute-start | bytes 393224 | tf_op jit(solution)/shard_map/ppermute | solution.py:358
  31.2 7.7 %collective-permute-start.15 = (f32[256,128]{1,0:T(8,128)S(1)}, f32[256,128]{1,0:T(8,128)S(1)}, u32[]{:S(2)}, u32[]{:S(2)}) collective-permute-start(f32[256,128]{1,0:T(8,128)S(1)} %add.10), channel_id=1, source_target_pairs={{0,2},{1,3},{2,0},{3,1},{4,6},{5,7},{6,4},{7,5},{8,10},{9,11},{10,... | collective-permute-start | bytes 393224 | tf_op jit(solution)/shard_map/ppermute | solution.py:358
  32.7 6.2 %collective-permute-start.17 = (f32[256,128]{1,0:T(8,128)S(1)}, f32[256,128]{1,0:T(8,128)S(1)}, u32[]{:S(2)}, u32[]{:S(2)}) collective-permute-start(f32[256,128]{1,0:T(8,128)S(1)} %add.11), channel_id=1, source_target_pairs={{0,4},{1,5},{2,6},{3,7},{4,0},{5,1},{6,2},{7,3},{8,12},{9,13},{10,... | collective-permute-start | bytes 393224 | tf_op jit(solution)/shard_map/ppermute | solution.py:358

commit v8 on v7

--- a/solution.py
+++ b/solution.py
@@ -279,19 +279,10 @@
     return jnp.dot(matrix, jnp.concatenate([high, high, low, low], axis=0), preferred_element_type=jnp.float32)
 
 
-def spread_half(levels, upper, part, received, own_pack, y_pack, matrices, state, tables, sems, acc):
-    me, band = lax.axis_index("lon"), lax.axis_index("lat")
-    lat_start, at_start, at_end = 8 * band, band == 0, band == lax.axis_size("lat") - 1
-    slot = me // 4
+def finish_rows(levels, upper, part, received, matrices, state, at):
+    band = lax.axis_index("lat")
     base = 8 * upper
-    copies = to_scalars([pack.at[pl.ds(120, 8)] for pack in (own_pack, y_pack)], tables, sems)
-
-    def exists(j):
-        n = base + j
-        there = (n < 15) & (~at_start | (n >= 4)) if j < 4 else n < 15
-        return there & (~at_end | (n < 12)) if j >= 4 else there
-
-    sender = jnp.where(upper == 1, ~at_end, ~at_start)
+    sender = jnp.where(upper == 1, band < lax.axis_size("lat") - 1, band > 0)
     for j in range(8):
         halves = []
         for h in range(2):
@@ -306,40 +297,45 @@
             halves.append(value)
         matrix = matrices[pl.ds(pl.multiple_of((base + j) * levels, levels), levels), :]
         result = vertical(matrix, jnp.concatenate(halves, axis=1))
-        state[j] = result[:, :128]
-        state[8 + j] = result[:, 128:]
-    for q in range(8):
-        acc[q * 22 + 7 : q * 22 + 15] = jnp.zeros((8, levels, 128), jnp.float32)
+        state[at + j] = result[:, :128]
+        state[at + 8 + j] = result[:, 128:]
+
+
+def spread_rows(levels, upper, own_pack, y_pack, state, at, tables, acc):
+    me, band = lax.axis_index("lon"), lax.axis_index("lat")
+    lat_start, at_start, at_end = 8 * band, band == 0, band == lax.axis_size("lat") - 1
+    slot = me // 4
     stay, back, on = lane_masks()
-    for copy in copies:
-        copy.wait()
     for j in range(8):
-        n = base + j
-        there = exists(j)
-        at = pl.ds(pl.multiple_of(8 * n, 8), 8)
+        n = 8 * upper + j
+        there = (n < 15) & (~at_start | (n >= 4) if j < 4 else ~at_end | (n < 12))
+        rows = pl.ds(pl.multiple_of(8 * n, 8), 8)
         for h in range(2):
             mine = slot == h
             tau = jnp.where(there, jnp.where(mine, tables[0, 2, n], tables[1, 2, n]).astype(jnp.int32), 0)
             first = jnp.where(mine, tables[0, 0, n], tables[1, 0, n]).astype(jnp.int32) - lat_start + 7
             first = jnp.where(there, first, 7)
-            prods = products(jnp.where(there, jnp.where(mine, own_pack[at, :], y_pack[at, :]), 0.0))
-            sources = [rolled(state[h * 8 + j, kk : kk + 8, :]) for kk in range(0, levels, 8)]
+            prods = products(jnp.where(there, jnp.where(mine, own_pack[rows, :], y_pack[rows, :]), 0.0))
+            sources = [rolled(state[at + h * 8 + j, kk : kk + 8, :]) for kk in range(0, levels, 8)]
             add_terms(sources, masked(prods, stay, range(NODES)), acc, (tau ^ me) * 22 + first)
             add_terms(sources, masked(prods, back, (0,)), acc, (((tau + 7) & 7) ^ me) * 22 + first)
             add_terms(sources, masked(prods, on, (2, 3)), acc, (((tau + 1) & 7) ^ me) * 22 + first)
 
 
-def second_spread_early(levels, *refs):
-    (*refs, acc, state, tables, sems) = refs
-    spread_half(levels, even_band(), *refs, state, tables, sems, acc)
-
-
-def second_spread_late(levels, *refs):
-    refs, before, outs, (state, tables, sems, acc) = refs[:5], refs[5], refs[6:14], refs[14:]
-    spread_half(levels, 1 - even_band(), *refs, state, tables, sems, acc)
+def second_spread(levels, part, r1, r2, own_pack, y_pack, matrices, *refs):
+    outs, (state, tables, sems, acc) = refs[:8], refs[8:]
+    copies = to_scalars([pack.at[pl.ds(120, 8)] for pack in (own_pack, y_pack)], tables, sems)
+    even = even_band()
+    finish_rows(levels, even, part, r1, matrices, state, 0)
+    finish_rows(levels, 1 - even, part, r2, matrices, state, 16)
+    for q in range(8):
+        acc[q * 22 + 7 : q * 22 + 15] = jnp.zeros((8, levels, 128), jnp.float32)
+    for copy in copies:
+        copy.wait()
+    spread_rows(levels, even, own_pack, y_pack, state, 0, tables, acc)
+    spread_rows(levels, 1 - even, own_pack, y_pack, state, 16, tables, acc)
     for q, out in enumerate(outs):
-        rows = slice(q * 22 + 7, q * 22 + 15)
-        out[...] = (acc[rows] + before[rows]).reshape(8 * levels, 128)
+        out[...] = acc[q * 22 + 7 : q * 22 + 15].reshape(8 * levels, 128)
 
 
 def finish(levels, own, diagonal, across, up, pair, matrices, out):
@@ -425,25 +421,18 @@
         part,
     )
     y_pack = swap_lon(pack, 4)
-    half_specs = [vmem(partial[0], 3), vmem((16 * levels, 128)), vmem((128, 128)), vmem((128, 128))]
-    half_specs += [vmem((16 * levels, 128))]
-    spread_shape = ((8 * 22, levels, 128), jnp.float32)
-    scratch = [pltpu.VMEM((16, levels, 128), jnp.float32), pltpu.SMEM((2, 8, 128), jnp.float32), pltpu.SemaphoreType.DMA((2,))]
-    (early,) = call(
-        functools.partial(second_spread_early, levels),
-        [spread_shape],
-        half_specs,
-        scratch,
-        8 * size,
-        *(part, r1, pack, y_pack, matrices1),
-    )
     pieces = call(
-        functools.partial(second_spread_late, levels),
+        functools.partial(second_spread, levels),
         [8 * levels] * 8,
-        half_specs + [vmem(spread_shape[0], 3)],
-        scratch + [pltpu.VMEM(*spread_shape)],
-        8 * size,
-        *(part, r2, pack, y_pack, matrices1, early),
+        [vmem(partial[0], 3)] + [vmem((16 * levels, 128))] * 2 + [vmem((128, 128))] * 2 + [vmem((16 * levels, 128))],
+        [
+            pltpu.VMEM((32, levels, 128), jnp.float32),
+            pltpu.SMEM((2, 8, 128), jnp.float32),
+            pltpu.SemaphoreType.DMA((2,)),
+            pltpu.VMEM((8 * 22, levels, 128), jnp.float32),
+        ],
+        16 * size,
+        *(part, r1, r2, pack, y_pack, matrices1),
     )
     received = {}
     for bits in (6, 4, 2):

time: 40 us -> 39.2 us (0.980)
  the two profiles are of different devices: /device:TPU:0 before, /device:TPU:8 now
where the time goes in v8:
time: 39.2 us; the launch traced here: 38.7 us
  starting transfers between devices  15.1 us (39%)
  waiting for transfers between devices  14.4 us (37%)
  Pallas kernels  9.04 us (23%)
    ppermute x15, waiting for transfers between devices, swap_lon(): return lax.ppermute(value, 'lon', [(i, i ^ bits) for i in range(RING)])  11 us
    ppermute x15, starting transfers between devices, swap_lon(): return lax.ppermute(value, 'lon', [(i, i ^ bits) for i in range(RING)])  10.3 us
    pallas_call x6, Pallas kernels, call(): pl.pallas_call(kernel, grid=(1,), out_shape=[jax.ShapeDtypeStruct(*out) f...  7.86 us
    ppermute x4, starting transfers between devices, swap_lat(): return lax.ppermute(value, ('lat', 'lon'), moves)  4.79 us
    ppermute x4, waiting for transfers between devices, swap_lat(): return lax.ppermute(value, ('lat', 'lon'), moves)  3.44 us
    pallas_call x1, Pallas kernels, ring_body(): pl.pallas_call(functools.partial(assemble, levels), out_shape=[pltpu.VMEM...  1.18 us
  transfers between devices with their start and end apart: 19, of which 10 were waited for; matrix products, arithmetic and copies ran while one was open for 0% of the time, Pallas kernels for 8%

profile of v8, /device:TPU:8, one launch (start us, length us, event | category | flops | bytes accessed | tf_op | source)
XLA Modules:
  0.0 38.7 jit_solution(13480922743231846998)
XLA Ops:
  0.0 1.2 %shard_map.64 = (f32[328,128]{1,0:T(8,128)S(1)}, f32[328,128]{1,0:T(8,128)S(1)}, f32[72,128]{1,0:T(8,128)S(1)}, f32[72,128]{1,0:T(8,128)S(1)}, f32[64,128]{1,0:T...) custom-call(s32[2,8]{1,0:T(2,128)} %bitcast.9, s32[2,8]{1,0:T(2,128)} %bitcast.10, f32[512,128]{1,0:T(8,128)} %bitcast.6, ...), custom_call_target="tpu_custom_call" | custom-call | tf_op jit(solution)/shard_map/pallas_call | solution.py:375
  1.2 2.5 %collective-permute-start.4 = (f32[328,128]{1,0:T(8,128)S(1)}, f32[328,128]{1,0:T(8,128)S(1)}, u32[]{:S(2)}, u32[]{:S(2)}) collective-permute-start(f32[328,128]{1,0:T(8,128)S(1)} %get-tuple-element.32), channel_id=1, source_target_pairs={{0,6},{1,7},{2,4},{3,5},{4,2},{5,3},{6,0},{7,1},{8,14},{9,15},{10,... | collective-permute-start | bytes 503816 | tf_op jit(solution)/shard_map/ppermute | solution.py:354
  3.7 0.5 %collective-permute-start.1 = (f32[328,128]{1,0:T(8,128)S(1)}, f32[328,128]{1,0:T(8,128)S(1)}, u32[]{:S(2)}, u32[]{:S(2)}) collective-permute-start(f32[328,128]{1,0:T(8,128)S(1)} %get-tuple-element.32), channel_id=1, source_target_pairs={{0,4},{1,5},{2,6},{3,7},{4,0},{5,1},{6,2},{7,3},{8,12},{9,13},{10,... | collective-permute-start | bytes 503816 | tf_op jit(solution)/shard_map/ppermute | solution.py:354
  4.2 0.5 %collective-permute-start.7 = (f32[328,128]{1,0:T(8,128)S(1)}, f32[328,128]{1,0:T(8,128)S(1)}, u32[]{:S(2)}, u32[]{:S(2)}) collective-permute-start(f32[328,128]{1,0:T(8,128)S(1)} %get-tuple-element.31.refs_0_.own_tile), channel_id=1, source_target_pairs={{0,2},{1,3},{2,0},{3,1},{4,6},{5,7},{6,4},{7,5},{8,10},{9,11},{10,... | collective-permute-start | bytes 503816 | tf_op jit(solution)/shard_map/ppermute | solution.py:354
  4.7 1.6 %collective-permute-start.5 = (f32[72,128]{1,0:T(8,128)S(1)}, f32[72,128]{1,0:T(8,128)S(1)}, u32[]{:S(2)}, u32[]{:S(2)}) collective-permute-start(f32[72,128]{1,0:T(8,128)S(1)} %get-tuple-element.35), channel_id=1, source_target_pairs={{0,1},{1,0},{2,3},{3,2},{4,5},{5,4},{6,7},{7,6},{8,16},{9,17},{10,... | collective-permute-start | bytes 110600 | tf_op jit(solution)/shard_map/ppermute | solution.py:362
  6.3 0.0 collective-permute-start.2
  6.3 0.8 %shard_map.65.refs_3_ = f32[30,32,128]{2,1,0:T(8,128)S(1)} custom-call(f32[328,128]{1,0:T(8,128)S(1)} %get-tuple-element.31.refs_0_.own_tile), custom_call_target="tpu_custom_call" | custom-call | flops 262144 | bytes 262144 | tf_op jit(solution)/shard_map/pallas_call | solution.py:109
  7.2 1.5 %collective-permute-done.5.e2 = f32[72,128]{1,0:T(8,128)S(1)} collective-permute-done((f32[72,128]{1,0:T(8,128)S(1)}, f32[72,128]{1,0:T(8,128)S(1)}, u32[]{:S(2)}, u32[]{:S(2)}) %collective-permute-start.5) | collective-permute-done | bytes 36896 | tf_op jit(solution)/shard_map/ppermute | solution.py:362
  8.7 0.0 collective-permute-start
  8.7 0.6 %collective-permute-done.4.refs_1_ = f32[328,128]{1,0:T(8,128)S(1)} collective-permute-done((f32[328,128]{1,0:T(8,128)S(1)}, f32[328,128]{1,0:T(8,128)S(1)}, u32[]{:S(2)}, u32[]{:S(2)}) %collective-permute-start.4) | collective-permute-done | bytes 167968 | tf_op jit(solution)/shard_map/ppermute | solution.py:354
  9.3 0.0 collective-permute-start.6
  9.3 1.0 %collective-permute-done.2.e1 = f32[72,128]{1,0:T(8,128)S(1)} collective-permute-done((f32[72,128]{1,0:T(8,128)S(1)}, f32[72,128]{1,0:T(8,128)S(1)}, u32[]{:S(2)}, u32[]{:S(2)}) %collective-permute-start.2) | collective-permute-done | bytes 36896 | tf_op jit(solution)/shard_map/ppermute | solution.py:362
  10.3 1.5 %collective-permute-done.1.refs_0_ = f32[328,128]{1,0:T(8,128)S(1)} collective-permute-done((f32[328,128]{1,0:T(8,128)S(1)}, f32[328,128]{1,0:T(8,128)S(1)}, u32[]{:S(2)}, u32[]{:S(2)}) %collective-permute-start.1) | collective-permute-done | bytes 167968 | tf_op jit(solution)/shard_map/ppermute | solution.py:354
  11.8 0.1 collective-permute-done.7.refs_2_
  11.9 0.0 collective-permute-start.8
  11.9 0.5 %collective-permute-start.3 = (f32[328,128]{1,0:T(8,128)S(1)}, f32[328,128]{1,0:T(8,128)S(1)}, u32[]{:S(2)}, u32[]{:S(2)}) collective-permute-start(f32[328,128]{1,0:T(8,128)S(1)} %collective-permute-done.1.refs_0_), channel_id=1, source_target_pairs={{0,1},{1,0},{2,3},{3,2},{4,5},{5,4},{6,7},{7,6},{8,9},{9,8},{10,11... | collective-permute-start | bytes 503816 | tf_op jit(solution)/shard_map/ppermute | solution.py:354
  12.4 1.3 %shard_map.66.refs_4_ = f32[30,32,128]{2,1,0:T(8,128)S(1)} custom-call(f32[328,128]{1,0:T(8,128)S(1)} %collective-permute-done.1.refs_0_, f32[328,128]{1,0:T(8,128)S(1)} %collective-permute-done.4.refs_1_, f32[328,128]{1,0:T(8,128)S(1)} %collective-permute-done.7.refs_2_, f32[30,32,128]{2,1,0:T(8,128)S(1)} %shard_map.65.refs_3_), custom_call_target="tpu_custom_call" | custom-call | flops 262144 | bytes 262144 | tf_op jit(solution)/shard_map/pallas_call | solution.py:109
  13.7 0.0 collective-permute-done.refs_0_
  13.8 0.0 collective-permute-done.6.refs_2_
  13.8 0.0 collective-permute-done.8.refs_3_
  13.8 0.0 collective-permute-done.3.refs_1_
  13.8 1.6 %shard_map.67 = (f32[30,32,128]{2,1,0:T(8,128)S(1)}, f32[512,128]{1,0:T(8,128)S(1)}, f32[512,128]{1,0:T(8,128)S(1)}) custom-call(f32[328,128]{1,0:T(8,128)S(1)} %collective-permute-done.refs_0_, f32[328,128]{1,0:T(8,128)S(1)} %collective-permute-done.3.refs_1_, f32[328,128]{1,0:T(8,128)S(1)} %collective-permute-done.6.refs_2_, ...), custom_call_target="tpu_custom_call" | custom-call | flops 262144 | bytes 262144 | tf_op jit(solution)/shard_map/pallas_call | solution.py:109
  15.4 0.5 %collective-permute-start.9 = (f32[512,128]{1,0:T(8,128)S(1)}, f32[512,128]{1,0:T(8,128)S(1)}, u32[]{:S(2)}, u32[]{:S(2)}) collective-permute-start(f32[512,128]{1,0:T(8,128)S(1)} %get-tuple-element.39), channel_id=1, source_target_pairs={{0,8},{1,9},{2,10},{3,11},{4,12},{5,13},{6,14},{7,15},{8,0},{9,1},... | collective-permute-start | bytes 786440 | tf_op jit(solution)/shard_map/ppermute | solution.py:362
  16.0 2.7 %collective-permute-start.10 = (f32[512,128]{1,0:T(8,128)S(1)}, f32[512,128]{1,0:T(8,128)S(1)}, u32[]{:S(2)}, u32[]{:S(2)}) collective-permute-start(f32[512,128]{1,0:T(8,128)S(1)} %get-tuple-element.40), channel_id=1, source_target_pairs={{0,1},{1,0},{2,3},{3,2},{4,5},{5,4},{6,7},{7,6},{8,16},{9,17},{10,... | collective-permute-start | bytes 786440 | tf_op jit(solution)/shard_map/ppermute | solution.py:362
  18.7 0.9 %shard_map.68 = (f32[128,128]{1,0:T(8,128)S(1)}, bf16[512,128]{1,0:T(8,128)(2,1)S(1)}, bf16[256,128]{1,0:T(8,128)(2,1)S(1)}) custom-call(f32[328,128]{1,0:T(8,128)S(1)} %get-tuple-element.31.refs_0_.own_tile, f32[64,128]{1,0:T(8,128)S(1)} %get-tuple-element.41.lat_w, f32[64,128]{1,0:T(8,128)S(1)} %get-tuple-element.42.lon_w, ...), custom_call_target="tpu_custom_call" | custom-call | flops 65536 | bytes 65536 | tf_op jit(solution)/shard_map/pallas_call | solution.py:109
  19.6 1.5 %collective-permute-start.11 = (f32[128,128]{1,0:T(8,128)S(1)}, f32[128,128]{1,0:T(8,128)S(1)}, u32[]{:S(2)}, u32[]{:S(2)}) collective-permute-start(f32[128,128]{1,0:T(8,128)S(1)} %get-tuple-element.46.own_pack), channel_id=1, source_target_pairs={{0,4},{1,5},{2,6},{3,7},{4,0},{5,1},{6,2},{7,3},{8,12},{9,13},{10,... | collective-permute-start | bytes 196616 | tf_op jit(solution)/shard_map/ppermute | solution.py:354
  21.1 2.8 %collective-permute-done.11.y_pack = f32[128,128]{1,0:T(8,128)S(1)} collective-permute-done((f32[128,128]{1,0:T(8,128)S(1)}, f32[128,128]{1,0:T(8,128)S(1)}, u32[]{:S(2)}, u32[]{:S(2)}) %collective-permute-start.11) | collective-permute-done | bytes 65568 | tf_op jit(solution)/shard_map/ppermute | solution.py:354
  23.9 0.0 collective-permute-done.9.r1
  23.9 0.9 %collective-permute-done.10.r2 = f32[512,128]{1,0:T(8,128)S(1)} collective-permute-done((f32[512,128]{1,0:T(8,128)S(1)}, f32[512,128]{1,0:T(8,128)S(1)}, u32[]{:S(2)}, u32[]{:S(2)}) %collective-permute-start.10) | collective-permute-done | bytes 262176 | tf_op jit(solution)/shard_map/ppermute | solution.py:362
  24.8 2.2 %shard_map.69 = (f32[256,128]{1,0:T(8,128)S(1)}, f32[256,128]{1,0:T(8,128)S(1)}, f32[256,128]{1,0:T(8,128)S(1)}, f32[256,128]{1,0:T(8,128)S(1)}, f32[256,128]{1,...) custom-call(f32[30,32,128]{2,1,0:T(8,128)S(1)} %get-tuple-element.38.after_this.part, ...), custom_call_target="tpu_custom_call" | custom-call | flops 1048576 | bytes 1048576 | tf_op jit(solution)/shard_map/pallas_call | solution.py:109
  27.0 0.1 collective-permute-start.12
  27.1 0.5 %collective-permute-start.14 = (f32[256,128]{1,0:T(8,128)S(1)}, f32[256,128]{1,0:T(8,128)S(1)}, u32[]{:S(2)}, u32[]{:S(2)}) collective-permute-start(f32[256,128]{1,0:T(8,128)S(1)} %get-tuple-element.52), channel_id=1, source_target_pairs={{0,1},{1,0},{2,3},{3,2},{4,5},{5,4},{6,7},{7,6},{8,9},{9,8},{10,11... | collective-permute-start | bytes 393224 | tf_op jit(solution)/shard_map/ppermute | solution.py:354
  27.6 0.1 collective-permute-start.16
  27.7 0.4 %collective-permute-start.18 = (f32[256,128]{1,0:T(8,128)S(1)}, f32[256,128]{1,0:T(8,128)S(1)}, u32[]{:S(2)}, u32[]{:S(2)}) collective-permute-start(f32[256,128]{1,0:T(8,128)S(1)} %get-tuple-element.55), channel_id=1, source_target_pairs={{0,1},{1,0},{2,3},{3,2},{4,5},{5,4},{6,7},{7,6},{8,9},{9,8},{10,11... | collective-permute-start | bytes 393224 | tf_op jit(solution)/shard_map/ppermute | solution.py:354
  28.1 0.3 collective-permute-done.12
  28.5 1.7 %collective-permute-start.13 = (f32[256,128]{1,0:T(8,128)S(1)}, f32[256,128]{1,0:T(8,128)S(1)}, u32[]{:S(2)}, u32[]{:S(2)}) collective-permute-start(f32[256,128]{1,0:T(8,128)S(1)} %add.9), channel_id=1, source_target_pairs={{0,6},{1,7},{2,4},{3,5},{4,2},{5,3},{6,0},{7,1},{8,14},{9,15},{10,... | collective-permute-start | bytes 393224 | tf_op jit(solution)/shard_map/ppermute | solution.py:354
  30.2 0.0 collective-permute-done.14
  30.2 1.3 %collective-permute-start.15 = (f32[256,128]{1,0:T(8,128)S(1)}, f32[256,128]{1,0:T(8,128)S(1)}, u32[]{:S(2)}, u32[]{:S(2)}) collective-permute-start(f32[256,128]{1,0:T(8,128)S(1)} %add.10), channel_id=1, source_target_pairs={{0,2},{1,3},{2,0},{3,1},{4,6},{5,7},{6,4},{7,5},{8,10},{9,11},{10,... | collective-permute-start | bytes 393224 | tf_op jit(solution)/shard_map/ppermute | solution.py:354
  31.5 0.0 collective-permute-done.16
  31.5 0.7 %collective-permute-start.17 = (f32[256,128]{1,0:T(8,128)S(1)}, f32[256,128]{1,0:T(8,128)S(1)}, u32[]{:S(2)}, u32[]{:S(2)}) collective-permute-start(f32[256,128]{1,0:T(8,128)S(1)} %add.11), channel_id=1, source_target_pairs={{0,4},{1,5},{2,6},{3,7},{4,0},{5,1},{6,2},{7,3},{8,12},{9,13},{10,... | collective-permute-start | bytes 393224 | tf_op jit(solution)/shard_map/ppermute | solution.py:354
  32.2 0.0 collective-permute-done.18.pair
  32.2 3.6 %collective-permute-done.13.diagonal = f32[256,128]{1,0:T(8,128)S(1)} collective-permute-done((f32[256,128]{1,0:T(8,128)S(1)}, f32[256,128]{1,0:T(8,128)S(1)}, u32[]{:S(2)}, u32[]{:S(2)}) %collective-permute-start.13) | collective-permute-done | bytes 131104 | tf_op jit(solution)/shard_map/ppermute | solution.py:354
  35.8 2.0 %collective-permute-done.15.across = f32[256,128]{1,0:T(8,128)S(1)} collective-permute-done((f32[256,128]{1,0:T(8,128)S(1)}, f32[256,128]{1,0:T(8,128)S(1)}, u32[]{:S(2)}, u32[]{:S(2)}) %collective-permute-start.15) | collective-permute-done | bytes 131104 | tf_op jit(solution)/shard_map/ppermute | solution.py:354
  37.8 0.0 collective-permute-done.17.up
  37.8 0.9 %shard_map.70 = f32[512,128]{1,0:T(8,128)} custom-call(f32[256,128]{1,0:T(8,128)S(1)} %get-tuple-element.48.own, f32[256,128]{1,0:T(8,128)S(1)} %collective-permute-done.13.diagonal, f32[256,128]{1,0:T(8,128)S(1)} %collective-permute-done.15.across, f32[256,128]{1,0:T(8,128)S(1)} %collective-permute-done.17.up, f32[256,128]{1,0:T(8,128)S(1)} %collective-permute-done.18.pair, ...), custom_call_target="tpu_custom_call" | custom-call | flops 65536 | bytes 65536 | tf_op jit(solution)/shard_map/pallas_call | solution.py:109
  (3 shorter events, 0.0 us)
Async XLA Ops:
  1.2 8.1 %collective-permute-start.4 = (f32[328,128]{1,0:T(8,128)S(1)}, f32[328,128]{1,0:T(8,128)S(1)}, u32[]{:S(2)}, u32[]{:S(2)}) collective-permute-start(f32[328,128]{1,0:T(8,128)S(1)} %get-tuple-element.32), channel_id=1, source_target_pairs={{0,6},{1,7},{2,4},{3,5},{4,2},{5,3},{6,0},{7,1},{8,14},{9,15},{10,... | collective-permute-start | bytes 503816 | tf_op jit(solution)/shard_map/ppermute | solution.py:354
  3.7 8.1 %collective-permute-start.1 = (f32[328,128]{1,0:T(8,128)S(1)}, f32[328,128]{1,0:T(8,128)S(1)}, u32[]{:S(2)}, u32[]{:S(2)}) collective-permute-start(f32[328,128]{1,0:T(8,128)S(1)} %get-tuple-element.32), channel_id=1, source_target_pairs={{0,4},{1,5},{2,6},{3,7},{4,0},{5,1},{6,2},{7,3},{8,12},{9,13},{10,... | collective-permute-start | bytes 503816 | tf_op jit(solution)/shard_map/ppermute | solution.py:354
  4.2 7.7 %collective-permute-start.7 = (f32[328,128]{1,0:T(8,128)S(1)}, f32[328,128]{1,0:T(8,128)S(1)}, u32[]{:S(2)}, u32[]{:S(2)}) collective-permute-start(f32[328,128]{1,0:T(8,128)S(1)} %get-tuple-element.31.refs_0_.own_tile), channel_id=1, source_target_pairs={{0,2},{1,3},{2,0},{3,1},{4,6},{5,7},{6,4},{7,5},{8,10},{9,11},{10,... | collective-permute-start | bytes 503816 | tf_op jit(solution)/shard_map/ppermute | solution.py:354
  4.7 4.0 %collective-permute-start.5 = (f32[72,128]{1,0:T(8,128)S(1)}, f32[72,128]{1,0:T(8,128)S(1)}, u32[]{:S(2)}, u32[]{:S(2)}) collective-permute-start(f32[72,128]{1,0:T(8,128)S(1)} %get-tuple-element.35), channel_id=1, source_target_pairs={{0,1},{1,0},{2,3},{3,2},{4,5},{5,4},{6,7},{7,6},{8,16},{9,17},{10,... | collective-permute-start | bytes 110600 | tf_op jit(solution)/shard_map/ppermute | solution.py:362
  6.3 4.0 %collective-permute-start.2 = (f32[72,128]{1,0:T(8,128)S(1)}, f32[72,128]{1,0:T(8,128)S(1)}, u32[]{:S(2)}, u32[]{:S(2)}) collective-permute-start(f32[72,128]{1,0:T(8,128)S(1)} %get-tuple-element.33), channel_id=1, source_target_pairs={{0,8},{1,9},{2,10},{3,11},{4,12},{5,13},{6,14},{7,15},{8,0},{9,1},... | collective-permute-start | bytes 110600 | tf_op jit(solution)/shard_map/ppermute | solution.py:362
  8.7 5.0 %collective-permute-start = (f32[328,128]{1,0:T(8,128)S(1)}, f32[328,128]{1,0:T(8,128)S(1)}, u32[]{:S(2)}, u32[]{:S(2)}) collective-permute-start(f32[328,128]{1,0:T(8,128)S(1)} %get-tuple-element.31.refs_0_.own_tile), channel_id=1, source_target_pairs={{0,1},{1,0},{2,3},{3,2},{4,5},{5,4},{6,7},{7,6},{8,9},{9,8},{10,11... | collective-permute-start | bytes 503816 | tf_op jit(solution)/shard_map/ppermute | solution.py:354
  9.3 4.5 %collective-permute-start.6 = (f32[328,128]{1,0:T(8,128)S(1)}, f32[328,128]{1,0:T(8,128)S(1)}, u32[]{:S(2)}, u32[]{:S(2)}) collective-permute-start(f32[328,128]{1,0:T(8,128)S(1)} %collective-permute-done.4.refs_1_), channel_id=1, source_target_pairs={{0,1},{1,0},{2,3},{3,2},{4,5},{5,4},{6,7},{7,6},{8,9},{9,8},{10,11... | collective-permute-start | bytes 503816 | tf_op jit(solution)/shard_map/ppermute | solution.py:354
  11.9 1.9 %collective-permute-start.8 = (f32[328,128]{1,0:T(8,128)S(1)}, f32[328,128]{1,0:T(8,128)S(1)}, u32[]{:S(2)}, u32[]{:S(2)}) collective-permute-start(f32[328,128]{1,0:T(8,128)S(1)} %collective-permute-done.7.refs_2_), channel_id=1, source_target_pairs={{0,1},{1,0},{2,3},{3,2},{4,5},{5,4},{6,7},{7,6},{8,9},{9,8},{10,11... | collective-permute-start | bytes 503816 | tf_op jit(solution)/shard_map/ppermute | solution.py:354
  11.9 1.9 %collective-permute-start.3 = (f32[328,128]{1,0:T(8,128)S(1)}, f32[328,128]{1,0:T(8,128)S(1)}, u32[]{:S(2)}, u32[]{:S(2)}) collective-permute-start(f32[328,128]{1,0:T(8,128)S(1)} %collective-permute-done.1.refs_0_), channel_id=1, source_target_pairs={{0,1},{1,0},{2,3},{3,2},{4,5},{5,4},{6,7},{7,6},{8,9},{9,8},{10,11... | collective-permute-start | bytes 503816 | tf_op jit(solution)/shard_map/ppermute | solution.py:354
  15.4 8.5 %collective-permute-start.9 = (f32[512,128]{1,0:T(8,128)S(1)}, f32[512,128]{1,0:T(8,128)S(1)}, u32[]{:S(2)}, u32[]{:S(2)}) collective-permute-start(f32[512,128]{1,0:T(8,128)S(1)} %get-tuple-element.39), channel_id=1, source_target_pairs={{0,8},{1,9},{2,10},{3,11},{4,12},{5,13},{6,14},{7,15},{8,0},{9,1},... | collective-permute-start | bytes 786440 | tf_op jit(solution)/shard_map/ppermute | solution.py:362
  16.0 8.9 %collective-permute-start.10 = (f32[512,128]{1,0:T(8,128)S(1)}, f32[512,128]{1,0:T(8,128)S(1)}, u32[]{:S(2)}, u32[]{:S(2)}) collective-permute-start(f32[512,128]{1,0:T(8,128)S(1)} %get-tuple-element.40), channel_id=1, source_target_pairs={{0,1},{1,0},{2,3},{3,2},{4,5},{5,4},{6,7},{7,6},{8,16},{9,17},{10,... | collective-permute-start | bytes 786440 | tf_op jit(solution)/shard_map/ppermute | solution.py:362
  19.6 4.3 %collective-permute-start.11 = (f32[128,128]{1,0:T(8,128)S(1)}, f32[128,128]{1,0:T(8,128)S(1)}, u32[]{:S(2)}, u32[]{:S(2)}) collective-permute-start(f32[128,128]{1,0:T(8,128)S(1)} %get-tuple-element.46.own_pack), channel_id=1, source_target_pairs={{0,4},{1,5},{2,6},{3,7},{4,0},{5,1},{6,2},{7,3},{8,12},{9,13},{10,... | collective-permute-start | bytes 196616 | tf_op jit(solution)/shard_map/ppermute | solution.py:354
  27.0 1.4 %collective-permute-start.12 = (f32[256,128]{1,0:T(8,128)S(1)}, f32[256,128]{1,0:T(8,128)S(1)}, u32[]{:S(2)}, u32[]{:S(2)}) collective-permute-start(f32[256,128]{1,0:T(8,128)S(1)} %get-tuple-element.50), channel_id=1, source_target_pairs={{0,1},{1,0},{2,3},{3,2},{4,5},{5,4},{6,7},{7,6},{8,9},{9,8},{10,11... | collective-permute-start | bytes 393224 | tf_op jit(solution)/shard_map/ppermute | solution.py:354
  27.1 3.1 %collective-permute-start.14 = (f32[256,128]{1,0:T(8,128)S(1)}, f32[256,128]{1,0:T(8,128)S(1)}, u32[]{:S(2)}, u32[]{:S(2)}) collective-permute-start(f32[256,128]{1,0:T(8,128)S(1)} %get-tuple-element.52), channel_id=1, source_target_pairs={{0,1},{1,0},{2,3},{3,2},{4,5},{5,4},{6,7},{7,6},{8,9},{9,8},{10,11... | collective-permute-start | bytes 393224 | tf_op jit(solution)/shard_map/ppermute | solution.py:354
  27.6 3.9 %collective-permute-start.16 = (f32[256,128]{1,0:T(8,128)S(1)}, f32[256,128]{1,0:T(8,128)S(1)}, u32[]{:S(2)}, u32[]{:S(2)}) collective-permute-start(f32[256,128]{1,0:T(8,128)S(1)} %get-tuple-element.54), channel_id=1, source_target_pairs={{0,1},{1,0},{2,3},{3,2},{4,5},{5,4},{6,7},{7,6},{8,9},{9,8},{10,11... | collective-permute-start | bytes 393224 | tf_op jit(solution)/shard_map/ppermute | solution.py:354
  27.7 4.5 %collective-permute-start.18 = (f32[256,128]{1,0:T(8,128)S(1)}, f32[256,128]{1,0:T(8,128)S(1)}, u32[]{:S(2)}, u32[]{:S(2)}) collective-permute-start(f32[256,128]{1,0:T(8,128)S(1)} %get-tuple-element.55), channel_id=1, source_target_pairs={{0,1},{1,0},{2,3},{3,2},{4,5},{5,4},{6,7},{7,6},{8,9},{9,8},{10,11... | collective-permute-start | bytes 393224 | tf_op jit(solution)/shard_map/ppermute | solution.py:354
  28.5 7.3 %collective-permute-start.13 = (f32[256,128]{1,0:T(8,128)S(1)}, f32[256,128]{1,0:T(8,128)S(1)}, u32[]{:S(2)}, u32[]{:S(2)}) collective-permute-start(f32[256,128]{1,0:T(8,128)S(1)} %add.9), channel_id=1, source_target_pairs={{0,6},{1,7},{2,4},{3,5},{4,2},{5,3},{6,0},{7,1},{8,14},{9,15},{10,... | collective-permute-start | bytes 393224 | tf_op jit(solution)/shard_map/ppermute | solution.py:354
  30.2 7.6 %collective-permute-start.15 = (f32[256,128]{1,0:T(8,128)S(1)}, f32[256,128]{1,0:T(8,128)S(1)}, u32[]{:S(2)}, u32[]{:S(2)}) collective-permute-start(f32[256,128]{1,0:T(8,128)S(1)} %add.10), channel_id=1, source_target_pairs={{0,2},{1,3},{2,0},{3,1},{4,6},{5,7},{6,4},{7,5},{8,10},{9,11},{10,... | collective-permute-start | bytes 393224 | tf_op jit(solution)/shard_map/ppermute | solution.py:354
  31.5 6.2 %collective-permute-start.17 = (f32[256,128]{1,0:T(8,128)S(1)}, f32[256,128]{1,0:T(8,128)S(1)}, u32[]{:S(2)}, u32[]{:S(2)}) collective-permute-start(f32[256,128]{1,0:T(8,128)S(1)} %add.11), channel_id=1, source_target_pairs={{0,4},{1,5},{2,6},{3,7},{4,0},{5,1},{6,2},{7,3},{8,12},{9,13},{10,... | collective-permute-start | bytes 393224 | tf_op jit(solution)/shard_map/ppermute | solution.py:354
